TPU v7x, 32 devices: a whole 2x2x4 slice. The times are simulated.
32 devices in a mesh: ctx: 8 (over z, core), fsdp: 4 (over y, x).
Axes of the slice: x: 2, y: 2, z: 4, core: 2. Of those that a mesh axis runs over, the one named last changes fastest.
Arguments:
- tokens: bfloat16 [4, 2048, 2048], P('fsdp', 'ctx'), may hold values from -6 to 6
- cotangent: bfloat16 [4, 2048, 2048], P('fsdp', 'ctx'), may hold values from -6 to 6
- lengths: int32 [4, 4], P('fsdp'), may hold values from 1 to 1793, 2048 in all within a row
- attn_gain: bfloat16 [2048], P(('ctx', 'fsdp')), may hold values from 0.099609375 to 1.8984375
- query_weight: bfloat16 [2048, 2048], P(('ctx', 'fsdp')), may hold values from -0.1875 to 0.1875
- key_weight: bfloat16 [2048, 512], P(('ctx', 'fsdp')), may hold values from -0.1875 to 0.1875
- value_weight: bfloat16 [2048, 512], P(('ctx', 'fsdp')), may hold values from -0.125 to 0.125
- out_weight: bfloat16 [2048, 2048], P(('ctx', 'fsdp')), may hold values from -1 to 1
- mlp_gain: bfloat16 [2048], P(('ctx', 'fsdp')), may hold values from 0.099609375 to 1.8984375
- gate_weight: bfloat16 [2048, 8192], P(('ctx', 'fsdp')), may hold values from -0.125 to 0.125
- up_weight: bfloat16 [2048, 8192], P(('ctx', 'fsdp')), may hold values from -0.125 to 0.125
- down_weight: bfloat16 [8192, 2048], P(('ctx', 'fsdp')), may hold values from -0.09375 to 0.09375
Outputs:
- mixed: bfloat16 [4, 2048, 2048], P('fsdp', 'ctx')
- grad_tokens: bfloat16 [4, 2048, 2048], P('fsdp', 'ctx')
- grad_attn_gain: float32 [2048], P(('ctx', 'fsdp'))
- grad_query: float32 [2048, 2048], P(('ctx', 'fsdp'))
- grad_key: float32 [2048, 512], P(('ctx', 'fsdp'))
- grad_value: float32 [2048, 512], P(('ctx', 'fsdp'))
- grad_out: float32 [2048, 2048], P(('ctx', 'fsdp'))
- grad_mlp_gain: float32 [2048], P(('ctx', 'fsdp'))
- grad_gate: float32 [2048, 8192], P(('ctx', 'fsdp'))
- grad_up: float32 [2048, 8192], P(('ctx', 'fsdp'))
- grad_down: float32 [8192, 2048], P(('ctx', 'fsdp'))
Inputs may be any that keep to these rules, and one draw needn't show every extreme that they name: Row s holds the lengths of the 4 documents that fill sequence s in order; one of them is 1793 tokens long.
All inputs are finite; a program needn't handle non-finite values.
Results may differ from a plain program's by a relative error of at most 0.015.
The roundings to bfloat16 on the way count: a program that leaves them out, or rounds other values in their place, can miss the bound.
Values may be sent and summed in bfloat16 or wider, within the bound.
A program may use at most 640 MiB of HBM per device.

v0:
```python
import jax
import jax.numpy as jnp
from jax import lax
from jax.sharding import PartitionSpec as P

D = 2048
FF = 8192
HEADS = 32
KV_HEADS = 8
HEAD_DIM = 64
WINDOW = 1024
STRETCH = 256


EPS = 1e-05
THETA = 500000.0


def passed_along(x, axis, by):
    size = lax.axis_size(axis)
    pairs = [(i, i + by) for i in range(size) if 0 <= i + by < size]
    return lax.ppermute(x, axis, pairs)


def product(left, right):
    return jnp.dot(left, right, preferred_element_type=jnp.float32)


def against(left, right):
    return lax.dot_general(
        left, right, (((1,), (1,)), ((), ())), preferred_element_type=jnp.float32
    )


def across(left, right):
    return lax.dot_general(
        left, right, (((0,), (0,)), ((), ())), preferred_element_type=jnp.float32
    )


def doc_segment(doc_lengths, index):
    doc_ends = jnp.cumsum(doc_lengths)
    return jnp.sum((index[:, None] >= doc_ends[None, :]).astype(jnp.int32), axis=1)


def doc_position(doc_lengths, index, segment):
    doc_ends = jnp.cumsum(doc_lengths)
    doc_starts = doc_ends - doc_lengths
    member = segment[:, None] == jnp.arange(doc_lengths.shape[0], dtype=jnp.int32)[None, :]
    return index - jnp.sum(jnp.where(member, doc_starts[None, :], 0), axis=1)


def rotate(heads, position, direction):
    half_dim = heads.shape[-1] // 2
    frequency = THETA ** (-2.0 * jnp.arange(half_dim, dtype=jnp.float32) / heads.shape[-1])
    angles = position.astype(jnp.float32)[:, None] * frequency[None, :]
    cosine = jnp.cos(angles)[:, None, :]
    sine_part = direction * jnp.sin(angles)[:, None, :]
    first_half = heads[..., :half_dim]
    second_half = heads[..., half_dim:]
    return jnp.concatenate(
        [
            first_half * cosine - second_half * sine_part,
            second_half * cosine + first_half * sine_part,
        ],
        axis=-1,
    )


def to_groups(matrix, tok_rows):
    shaped = matrix.reshape(tok_rows, KV_HEADS, HEADS // KV_HEADS, HEAD_DIM).transpose(1, 2, 0, 3)
    return shaped.reshape(KV_HEADS, -1, HEAD_DIM)


def from_groups(stacked, tok_rows):
    shaped = stacked.reshape(KV_HEADS, HEADS // KV_HEADS, tok_rows, HEAD_DIM).transpose(2, 0, 1, 3)
    return shaped.reshape(tok_rows, HEADS * HEAD_DIM)


def to_kv_heads(matrix):
    return matrix.reshape(matrix.shape[0], KV_HEADS, HEAD_DIM).transpose(1, 0, 2)


def from_kv_heads(stacked):
    return stacked.transpose(1, 0, 2).reshape(stacked.shape[1], KV_HEADS * HEAD_DIM)


def attend_forward(query_heads, key_heads, value_heads, visible):
    score_scale = HEAD_DIM ** (-0.5)

    def one_head(inputs):
        query_block, key_block, value_block = inputs
        scores = jnp.where(visible, against(query_block, key_block) * score_scale, -1e30)
        row_max = jnp.max(scores, axis=1, keepdims=True)
        raised = jnp.exp(scores - row_max)
        row_total = jnp.sum(raised, axis=1, keepdims=True)
        probability = (raised / row_total).astype(jnp.bfloat16)
        return (product(probability, value_block), row_max, row_total)

    return lax.map(one_head, (query_heads, key_heads, value_heads))


def attend_backward(query_heads, key_heads, value_heads, grad_heads, row_max, row_total, visible):
    score_scale = HEAD_DIM ** (-0.5)

    def one_head(inputs):
        query_block, key_block, value_block, grad_block, block_max, block_total = inputs
        scores = jnp.where(visible, against(query_block, key_block) * score_scale, -1e30)
        probability = jnp.exp(scores - block_max) / block_total
        grad_prob = against(grad_block, value_block)
        delta = jnp.sum(probability * grad_prob, axis=1, keepdims=True)
        grad_scores = (probability * (grad_prob - delta)).astype(jnp.bfloat16)
        grad_query = product(grad_scores, key_block) * score_scale
        grad_key = across(grad_scores, query_block) * score_scale
        grad_value = across(probability.astype(jnp.bfloat16), grad_block)
        return (grad_query, grad_key, grad_value)

    return lax.map(one_head, (query_heads, key_heads, value_heads, grad_heads, row_max, row_total))


def norm_back(grad_normal, normal, inverse):
    return inverse * (grad_normal - normal * jnp.mean(grad_normal * normal, axis=1, keepdims=True))


def local(
    tokens,
    cotangent,
    lengths,
    attn_gain,
    query_weight,
    key_weight,
    value_weight,
    out_weight,
    mlp_gain,
    gate_weight,
    up_weight,
    down_weight,
):
    stream = tokens[0].astype(jnp.float32)
    tok_rows = stream.shape[0]
    group_size = HEADS // KV_HEADS
    kv_width = KV_HEADS * HEAD_DIM
    reach_blocks = WINDOW // STRETCH
    ctx_place = lax.axis_index("ctx")
    doc_lengths = lengths[0]
    query_index = ctx_place * tok_rows + jnp.arange(tok_rows, dtype=jnp.int32)
    key_index = (ctx_place - reach_blocks) * tok_rows + jnp.arange(
        (reach_blocks + 1) * tok_rows, dtype=jnp.int32
    )
    query_doc = doc_segment(doc_lengths, query_index)
    key_doc = doc_segment(doc_lengths, key_index)
    position = doc_position(doc_lengths, query_index, query_doc)
    visible = (key_index[None, :] >= 0) & (key_index[None, :] <= query_index[:, None])
    visible = (
        visible
        & (query_index[:, None] - key_index[None, :] < WINDOW)
        & (query_doc[:, None] == key_doc[None, :])
    )
    visible = jnp.tile(visible, (group_size, 1))
    inv_one = lax.rsqrt(jnp.mean(stream * stream, axis=1, keepdims=True) + EPS)
    normal_one = stream * inv_one
    pieces = (
        lax.all_gather(attn_gain, ("ctx", "fsdp"), axis=0, tiled=True),
        lax.all_gather(query_weight, ("ctx", "fsdp"), axis=0, tiled=True),
        lax.all_gather(key_weight, ("ctx", "fsdp"), axis=0, tiled=True),
        lax.all_gather(value_weight, ("ctx", "fsdp"), axis=0, tiled=True),
    )
    gain_piece = pieces[0].astype(jnp.float32)
    normed = (normal_one * gain_piece).astype(jnp.bfloat16)
    gain_full = gain_piece
    front = (
        product(normed, pieces[1]),
        product(normed, pieces[2]),
        product(normed, pieces[3]),
        gain_full,
    )
    kept = tuple((pieces[1 + slot] for slot in range(3)))
    attn_sums = front + kept
    gain_one = attn_sums[3]
    normed_one = (normal_one * gain_one).astype(jnp.bfloat16)
    query_rot = (
        rotate(attn_sums[0].reshape(tok_rows, HEADS, HEAD_DIM), position, 1.0)
        .astype(jnp.bfloat16)
        .reshape(tok_rows, D)
    )
    key_rot = (
        rotate(attn_sums[1].reshape(tok_rows, KV_HEADS, HEAD_DIM), position, 1.0)
        .astype(jnp.bfloat16)
        .reshape(tok_rows, kv_width)
    )
    value_low = attn_sums[2].astype(jnp.bfloat16)
    key_list = [key_rot]
    value_list = [value_low]
    own_pair = jnp.stack([key_rot, value_low])
    for step in range(1, reach_blocks + 1):
        earlier = passed_along(own_pair, "ctx", step)
        key_list.insert(0, earlier[0])
        value_list.insert(0, earlier[1])
    key_heads = to_kv_heads(jnp.concatenate(key_list, axis=0))
    value_heads = to_kv_heads(jnp.concatenate(value_list, axis=0))
    query_heads = to_groups(query_rot, tok_rows)
    head_out, row_max, row_total = attend_forward(query_heads, key_heads, value_heads, visible)
    attn_mix = from_groups(head_out, tok_rows).astype(jnp.bfloat16)
    pieces = (
        lax.all_gather(out_weight, ("ctx", "fsdp"), axis=0, tiled=True),
        lax.all_gather(mlp_gain, ("ctx", "fsdp"), axis=0, tiled=True),
    )
    mixed_part = attn_mix
    gain_full = pieces[1].astype(jnp.float32)
    kept = pieces[0]
    resid = stream + product(mixed_part, pieces[0])
    inv_two = lax.rsqrt(jnp.mean(resid * resid, axis=1, keepdims=True) + EPS)
    normal_two = resid * inv_two
    normed_two = (normal_two * gain_full).astype(jnp.bfloat16)
    pieces = (
        lax.all_gather(gate_weight, ("ctx", "fsdp"), axis=0, tiled=True),
        lax.all_gather(up_weight, ("ctx", "fsdp"), axis=0, tiled=True),
    )
    part = normed_two
    gate_sum = product(part, pieces[0])
    up_sum = product(part, pieces[1])
    sigmoid_gate = jax.nn.sigmoid(gate_sum)
    silu_gate = gate_sum * sigmoid_gate
    hidden = (silu_gate * up_sum).astype(jnp.bfloat16)
    down_sum = product(hidden, lax.all_gather(down_weight, ("ctx", "fsdp"), axis=0, tiled=True))
    mixed = (resid + down_sum).astype(jnp.bfloat16)
    grad_low = cotangent[0]
    grad_stream = grad_low.astype(jnp.float32)
    grad_hidden = against(
        grad_low, lax.all_gather(down_weight, ("ctx", "fsdp"), axis=0, tiled=True)
    )
    grad_down = lax.psum_scatter(
        across(hidden, grad_low), ("ctx", "fsdp"), scatter_dimension=0, tiled=True
    )
    grad_gate_low = (
        grad_hidden * up_sum * sigmoid_gate * (1.0 + gate_sum * (1.0 - sigmoid_gate))
    ).astype(jnp.bfloat16)
    grad_up_low = (grad_hidden * silu_gate).astype(jnp.bfloat16)
    pieces = (
        lax.all_gather(gate_weight, ("ctx", "fsdp"), axis=0, tiled=True),
        lax.all_gather(up_weight, ("ctx", "fsdp"), axis=0, tiled=True),
    )
    columns = against(grad_gate_low, pieces[0]) + against(grad_up_low, pieces[1])
    part = normed_two
    gate_grads = lax.psum_scatter(
        jnp.concatenate([across(part, grad_gate_low), across(part, grad_up_low)], axis=1),
        ("ctx", "fsdp"),
        scatter_dimension=0,
        tiled=True,
    )
    mlp_gain_local = jnp.sum(columns * normal_two, axis=0)
    grad_resid = grad_stream + norm_back(columns * gain_full, normal_two, inv_two)
    grad_resid_low = grad_resid.astype(jnp.bfloat16)
    grad_mix = against(grad_resid_low, kept)
    grad_mix_low = grad_mix.astype(jnp.bfloat16)
    grad_query_heads, grad_key_heads, grad_value_heads = attend_backward(
        query_heads,
        key_heads,
        value_heads,
        to_groups(grad_mix_low, tok_rows),
        row_max,
        row_total,
        visible,
    )
    grad_query_rot = from_groups(grad_query_heads, tok_rows)
    grad_key_window = from_kv_heads(grad_key_heads)
    grad_value_window = from_kv_heads(grad_value_heads)
    own_start = reach_blocks * tok_rows
    grad_key_total = grad_key_window[own_start:]
    grad_value_total = grad_value_window[own_start:]
    for step in range(1, reach_blocks + 1):
        first_row = (reach_blocks - step) * tok_rows
        sent_pair = jnp.stack(
            [
                grad_key_window[first_row : first_row + tok_rows],
                grad_value_window[first_row : first_row + tok_rows],
            ]
        )
        later = passed_along(sent_pair.astype(jnp.bfloat16), "ctx", -step).astype(sent_pair.dtype)
        grad_key_total = grad_key_total + later[0]
        grad_value_total = grad_value_total + later[1]
    grad_query_low = (
        rotate(grad_query_rot.reshape(tok_rows, HEADS, HEAD_DIM), position, -1.0)
        .reshape(tok_rows, D)
        .astype(jnp.bfloat16)
    )
    grad_key_low = (
        rotate(grad_key_total.reshape(tok_rows, KV_HEADS, HEAD_DIM), position, -1.0)
        .reshape(tok_rows, kv_width)
        .astype(jnp.bfloat16)
    )
    grad_value_low = grad_value_total.astype(jnp.bfloat16)
    grad_normed_one = (
        against(grad_query_low, attn_sums[4])
        + against(grad_key_low, attn_sums[5])
        + against(grad_value_low, attn_sums[6])
    )
    part = normed_one
    mixed_part = attn_mix
    attn_grads = lax.psum_scatter(
        jnp.concatenate(
            [
                across(part, grad_query_low),
                across(part, grad_key_low),
                across(part, grad_value_low),
                across(mixed_part, grad_resid_low),
            ],
            axis=1,
        ),
        ("ctx", "fsdp"),
        scatter_dimension=0,
        tiled=True,
    )
    attn_gain_local = jnp.sum(grad_normed_one * normal_one, axis=0)
    gain_grads = (
        lax.psum_scatter(attn_gain_local, ("ctx", "fsdp"), scatter_dimension=0, tiled=True),
        lax.psum_scatter(mlp_gain_local, ("ctx", "fsdp"), scatter_dimension=0, tiled=True),
    )
    grad_input = grad_resid + norm_back(grad_normed_one * gain_one, normal_one, inv_one)
    return (
        mixed[None],
        grad_input.astype(jnp.bfloat16)[None],
        gain_grads[0],
        attn_grads[:, :D],
        attn_grads[:, D : D + kv_width],
        attn_grads[:, D + kv_width : D + 2 * kv_width],
        attn_grads[:, D + 2 * kv_width :],
        gain_grads[1],
        gate_grads[:, :FF],
        gate_grads[:, FF:],
        grad_down,
    )


def solution(mesh):
    in_specs = (
        P("fsdp", "ctx", None),
        P("fsdp", "ctx", None),
        P("fsdp", None),
        P(("ctx", "fsdp")),
        P(("ctx", "fsdp"), None),
        P(("ctx", "fsdp"), None),
        P(("ctx", "fsdp"), None),
        P(("ctx", "fsdp"), None),
        P(("ctx", "fsdp")),
        P(("ctx", "fsdp"), None),
        P(("ctx", "fsdp"), None),
        P(("ctx", "fsdp"), None),
    )
    out_specs = (
        P("fsdp", "ctx", None),
        P("fsdp", "ctx", None),
        P(("ctx", "fsdp")),
        P(("ctx", "fsdp"), None),
        P(("ctx", "fsdp"), None),
        P(("ctx", "fsdp"), None),
        P(("ctx", "fsdp"), None),
        P(("ctx", "fsdp")),
        P(("ctx", "fsdp"), None),
        P(("ctx", "fsdp"), None),
        P(("ctx", "fsdp"), None),
    )
    return jax.shard_map(local, mesh=mesh, in_specs=in_specs, out_specs=out_specs, check_vma=False)
```

profile of v0, /device:TPU:0, one launch (start us, length us, event | category | flops | bytes accessed | tf_op | source)
XLA Modules:
  0.0 5292.3 jit_solution(8728532019563363663)
XLA Ops:
  12.5 42.3 all-reduce.6
  56.4 13.7 all-gather.10.cloned.1.call-done
  70.1 2.9 copy.121
  74.1 54.2 %all-gather.12.cloned.1.call-done = bf16[2048,512]{1,0:T(8,128)(2,1)} async-done(((bf16[64,512]{1,0:T(8,128)(2,1)}), bf16[2048,512]{1,0:T(8,128)(2,1)}) %all-gather.12.cloned.1.call-update) | async-done | bytes 2097168 | tf_op jit(solution)/shard_map/all_gather | solution.py:166
  130.7 3.0 collective-permute-start.3
  136.8 3.8 collective-permute-start.1
  146.3 7.1 collective-permute-done.2
  156.1 14.7 collective-permute-done.1
  173.5 13.5 collective-permute-done
  201.2 28.3 all-gather.8.cloned.1.call-done
  229.5 12.3 copy.119
  241.8 6.1 fusion.78
  251.3 53.3 %while.32 = (s32[]{:T(128)}, bf16[8,1024,64]{1,2,0:T(8,128)(2,1)}, f32[8,1024,1]{1,2,0:T(1,128)}, f32[8,1024,1]{1,2,0:T(1,128)}, bf16[8,1024,64]{2,1,0:T(8,128)(...) while((s32[]{:T(128)}, bf16[8,1024,64]{1,2,0:T(8,128)(2,1)}, ...), condition=%wide.region_8.9_spmd.clone.clone, body=%wide.region_5.8_spmd.clone.sunk.clone | while | flops 346028032 | bytes 17274976 | solution.py:100
  254.5 2.9 fusion.190
  261.2 2.9 fusion.190
  267.8 2.9 fusion.190
  274.5 2.9 fusion.190
  281.2 2.8 fusion.190
  287.8 2.9 fusion.190
  294.5 2.9 fusion.190
  301.1 2.9 fusion.190
  304.6 3.1 convert_element_type.180
  312.4 6.2 multiply_reduce_fusion.3
  320.1 188.4 %all-gather.18.cloned.1.call-done = bf16[2048,8192]{1,0:T(8,128)(2,1)} async-done(((bf16[64,8192]{1,0:T(8,128)(2,1)}), bf16[2048,8192]{1,0:T(8,128)(2,1)}) %all-gather.18.cloned.1.call-update) | async-done | bytes 33554448 | tf_op jit(solution)/shard_map/all_gather | solution.py:217
  508.5 18.1 fusion.117
  526.7 177.6 %all-gather.16.cloned.1.call-done = bf16[2048,8192]{1,0:T(8,128)(2,1)} async-done(((bf16[64,8192]{1,0:T(8,128)(2,1)}), bf16[2048,8192]{1,0:T(8,128)(2,1)}) %all-gather.16.cloned.1.call-update) | async-done | bytes 33554448 | tf_op jit(solution)/shard_map/all_gather | solution.py:216
  704.2 17.8 fusion.116
  722.0 178.1 %all-gather.20.cloned.1.call-done = bf16[8192,2048]{1,0:T(8,128)(2,1)} async-done(((bf16[256,2048]{1,0:T(8,128)(2,1)}), bf16[8192,2048]{1,0:T(8,128)(2,1)}) %all-gather.20.cloned.1.call-update) | async-done | bytes 33554448 | tf_op jit(solution)/shard_map/all_gather | solution.py:225
  900.1 23.1 multiply_convert_fusion.1
  923.2 25.7 fusion.121
  948.9 25.3 fusion.120
  974.2 86.9 %pad_maximum_fusion = f32[2048,16384]{1,0:T(8,128)} fusion(f32[2048,8192]{1,0:T(8,128)} %fusion.121, f32[2048,8192]{1,0:T(8,128)} %fusion.120), kind=kLoop, calls=%fused_computation.54 | loop fusion | flops 33554432 | bytes 268435456 | tf_op jit(solution)/shard_map/concatenate | solution.py:246
  1061.2 18.9 fusion.118
  1080.1 19.3 multiply_reduce_fusion.1
  1099.4 3.1 multiply_add_fusion
  1102.6 6.0 convolution_convert_fusion
  1109.9 2.8 copy.145
  1112.6 109.5 %while.33 = (s32[]{:T(128)}, f32[8,1024,64]{1,2,0:T(8,128)}, f32[8,1280,64]{1,2,0:T(8,128)}, f32[8,1280,64]{1,2,0:T(8,128)}, bf16[8,1024,64]{2,1,0:T(8,128)(2,1)...) while((s32[]{:T(128)}, f32[8,1024,64]{1,2,0:T(8,128)}, ...), condition=%wide.region_13.14_spmd.clone.clone, body=%wide.region_11.13_spmd.clone.sunk.clone | while | flops 852114432 | bytes 42636408 | solution.py:118
  1115.6 3.3 multiply_reduce_fusion.6
  1129.2 3.2 multiply_reduce_fusion.6
  1142.8 3.2 multiply_reduce_fusion.6
  1156.5 3.2 multiply_reduce_fusion.6
  1170.2 3.2 multiply_reduce_fusion.6
  1183.8 3.2 multiply_reduce_fusion.6
  1197.4 3.2 multiply_reduce_fusion.6
  1211.1 3.3 multiply_reduce_fusion.6
  1232.9 8.2 fusion.96
  1241.1 8.3 fusion.82
  1249.4 4.9 collective-permute-done.5
  1254.5 25.9 collective-permute-done.6
  1280.5 33.7 collective-permute-done.7
  1315.8 2.9 fusion.80
  1318.7 2.8 fusion.84
  1321.5 29.1 pad_maximum_fusion.1
  1350.6 38.5 copy.146
  1389.4 29.0 fusion.72
  1418.4 7.8 fusion.119
  1426.3 17.2 fusion.57
  1451.0 57.5 %all-reduce.5 = (f32[2048]{0:T(1024)S(1)}, f32[2048]{0:T(1024)S(1)}) all-reduce(f32[2048]{0:T(1024)S(1)} %get-tuple-element.316, f32[2048]{0:T(1024)S(1)} %copy-done.34), channel_id=2, replica_groups=mesh['ctx'=8,'fsdp'=4] {'ctx','fsdp'}, use_global_device_ids=true, to_apply=%region_16.17.clone | all-reduce | flops 4096 | bytes 32768
  1509.7 3.2 fusion.70
  1513.0 1480.5 %all-reduce.9.cloned.1.call-done = f32[2048,16384]{1,0:T(8,128)} async-done(((f32[2048,16384]{1,0:T(8,128)}), f32[2048,16384]{1,0:T(8,128)}) %all-reduce.9.cloned.1.call-update) | async-done | bytes 134217744
  2993.5 4.9 fusion.107
  2998.4 879.2 %reduce-scatter.7.cloned.1.call-done = f32[64,5120]{1,0:T(8,128)} async-done(((f32[2048,5120]{1,0:T(8,128)}), f32[64,5120]{1,0:T(8,128)}) %reduce-scatter.7.cloned.1.call-update) | async-done | bytes 1310736
  3881.6 1403.6 %reduce-scatter.5.cloned.1.call-done = f32[256,2048]{1,0:T(8,128)} async-done(((f32[8192,2048]{1,0:T(8,128)}), f32[256,2048]{1,0:T(8,128)}) %reduce-scatter.5.cloned.1.call-update) | async-done | bytes 2097168 | tf_op jit(solution)/shard_map/reduce_scatter | solution.py:232
  (273 shorter events, 188.6 us)
Async XLA Ops:
  7.2 4.8 copy-start.35
  7.2 5.1 copy-start.36
  7.2 47.6 copy-start.37
  7.2 48.1 copy-start
  7.2 62.9 %all-gather.10.cloned.1.call-start = ((), (), s32[]{:S(2)}) async-start(), calls=%async_computation.3 | async-start | bytes 2162688 | tf_op jit(solution)/shard_map/all_gather | solution.py:165
  8.0 120.4 %all-gather.12.cloned.1.call-start = ((), (), s32[]{:S(2)}) async-start(), calls=%async_computation.4 | async-start | bytes 2162688 | tf_op jit(solution)/shard_map/all_gather | solution.py:166
  8.7 220.8 %all-gather.8.cloned.1.call-start = ((), (), s32[]{:S(2)}) async-start(), calls=%async_computation.2 | async-start | bytes 8650752 | tf_op jit(solution)/shard_map/all_gather | solution.py:164
  9.4 302.9 %all-gather.14.cloned.1.call-start = ((), (), s32[]{:S(2)}) async-start(), calls=%async_computation.5 | async-start | bytes 8650752 | tf_op jit(solution)/shard_map/all_gather | solution.py:205
  10.0 498.5 %all-gather.18.cloned.1.call-start = ((), (), s32[]{:S(2)}) async-start(), calls=%async_computation.7 | async-start | bytes 34603008 | tf_op jit(solution)/shard_map/all_gather | solution.py:217
  10.6 693.6 %all-gather.16.cloned.1.call-start = ((), (), s32[]{:S(2)}) async-start(), calls=%async_computation.6 | async-start | bytes 34603008 | tf_op jit(solution)/shard_map/all_gather | solution.py:216
  11.2 888.9 %all-gather.20.cloned.1.call-start = ((), (), s32[]{:S(2)}) async-start(), calls=%async_computation.8 | async-start | bytes 34603008 | tf_op jit(solution)/shard_map/all_gather | solution.py:225
  11.9 2981.6 %all-reduce.9.cloned.1.call-start = ((), (), s32[]{:S(2)}) async-start(), calls=%async_computation.11 | async-start | bytes 268435456
  54.8 187.0 %copy-start.25 = (f32[2048]{0:T(1024)}, f32[2048]{0:T(1024)S(1)}, u32[]{:S(2)}) copy-start(f32[2048]{0:T(1024)S(1)} %convert_element_type.169) | copy-start | bytes 24580
  55.6 72.7 %copy-start.29 = (f32[256]{0:T(256)}, f32[256]{0:T(256)S(1)}, u32[]{:S(2)}) copy-start(f32[256]{0:T(256)S(1)} %add_rsqrt_fusion.1) | copy-start | bytes 3076
  56.4 191.5 %copy-start.22 = (f32[256,32]{0,1:T(8,128)}, f32[256,32]{0,1:T(8,128)S(1)}, u32[]{:S(2)}) copy-start(f32[256,32]{0,1:T(8,128)S(1)} %get-tuple-element.403) | copy-start | bytes 98308
  130.7 13.5 collective-permute-start.3
  133.7 19.6 collective-permute-start.2
  136.8 34.0 collective-permute-start.1
  141.7 176.8 %copy-start.27 = (f32[2048]{0:T(1024)}, f32[2048]{0:T(1024)S(1)}, u32[]{:S(2)}) copy-start(f32[2048]{0:T(1024)S(1)} %convert_element_type.183) | copy-start | bytes 24580
  141.9 45.1 collective-permute-start
  193.7 4.7 copy-start.21
  229.5 12.3 copy-start.30
  304.6 5.5 copy-start.2
  304.6 5.5 copy-start.7
  318.5 1.3 copy-start.4
  318.5 190.0 %copy-start.32 = (f32[256]{0:T(256)}, f32[256]{0:T(256)S(1)}, u32[]{:S(2)}) copy-start(f32[256]{0:T(256)S(1)} %add_rsqrt_fusion) | copy-start | bytes 3076
  526.6 373.5 %copy-start.12 = (bf16[1,256,2048]{2,1,0:T(8,128)(2,1)S(1)}, bf16[1,256,2048]{2,1,0:T(8,128)(2,1)}, u32[]{:S(2)}) copy-start(bf16[1,256,2048]{2,1,0:T(8,128)(2,1)} %param.17) | copy-start | bytes 3145732
  1061.1 2816.5 %reduce-scatter.7.cloned.1.call-start = ((), (), s32[]{:S(2)}) async-start(), calls=%async_computation.10 | async-start | bytes 43253760
  1061.2 18.9 copy-start.5
  1061.2 18.9 copy-start.28
  1061.2 18.9 copy-start.33
  1109.9 2.8 copy-start.3
  1222.1 2.4 copy-start.18
  1222.1 3.3 copy-start.19
  1224.6 90.2 %copy-start.11 = (f32[256,8,64]{0,2,1:T(8,128)}, f32[256,8,64]{0,2,1:T(8,128)S(1)}, u32[]{:S(2)}) copy-start(f32[256,8,64]{0,2,1:T(8,128)S(1)} %slice.213) | copy-start | bytes 1572868
  1225.9 5.7 copy-start.23
  1225.9 5.7 copy-start.24
  1226.0 28.3 collective-permute-start.5
  1227.4 53.0 %collective-permute-start.6 = (bf16[2,256,512]{1,2,0:T(8,128)(2,1)S(1)}, bf16[2,256,512]{1,2,0:T(8,128)(2,1)S(1)}, u32[]{:S(2)}, u32[]{:S(2)}) collective-permute-start(bf16[2,256,512]{1,2,0:T(8,128)(2,1)S(1)} %pad_maximum_fusion.5), channel_id=1, source_target_pairs={{12,0},{16,4},{20,8},{24,12},{28,16},{13,1},{17,5},{21,9},{25,13},... | collective-permute-start | bytes 1572872 | tf_op jit(solution)/shard_map/ppermute | solution.py:22
  1228.7 85.4 %collective-permute-start.7 = (bf16[2,256,512]{1,2,0:T(8,128)(2,1)S(1)}, bf16[2,256,512]{1,2,0:T(8,128)(2,1)S(1)}, u32[]{:S(2)}, u32[]{:S(2)}) collective-permute-start(bf16[2,256,512]{1,2,0:T(8,128)(2,1)S(1)} %pad_maximum_fusion.6), channel_id=1, source_target_pairs={{16,0},{20,4},{24,8},{28,12},{17,1},{21,5},{25,9},{29,13},{18,2},{... | collective-permute-start | bytes 1572872 | tf_op jit(solution)/shard_map/ppermute | solution.py:22
  1230.1 84.2 %collective-permute-start.4 = (bf16[2,256,512]{1,2,0:T(8,128)(2,1)S(1)}, bf16[2,256,512]{1,2,0:T(8,128)(2,1)S(1)}, u32[]{:S(2)}, u32[]{:S(2)}) collective-permute-start(bf16[2,256,512]{1,2,0:T(8,128)(2,1)S(1)} %pad_maximum_fusion.3), channel_id=1, source_target_pairs={{4,0},{8,4},{12,8},{16,12},{20,16},{24,20},{28,24},{5,1},{9,5},{13... | collective-permute-start | bytes 1572872 | tf_op jit(solution)/shard_map/ppermute | solution.py:22
  1231.6 1.3 copy-start.8
  1232.9 8.2 copy-start.13
  1232.9 8.2 copy-start.1
  1232.9 8.2 copy-start.26
  1232.9 8.2 copy-start.31
  1254.5 60.3 %copy-start.14 = (f32[2,256,512]{1,2,0:T(8,128)}, f32[2,256,512]{1,2,0:T(8,128)S(1)}, u32[]{:S(2)}) copy-start(f32[2,256,512]{1,2,0:T(8,128)S(1)} %convert_element_type.195) | copy-start | bytes 3145732
  1280.5 34.3 copy-start.15
  1314.3 1.0 copy-start.16
  1314.4 1.2 copy-start.17
  1389.1 3896.1 %reduce-scatter.5.cloned.1.call-start = ((), (), s32[]{:S(2)}) async-start(), calls=%async_computation.9 | async-start | bytes 69206016 | tf_op jit(solution)/shard_map/reduce_scatter | solution.py:232
  1418.4 7.9 copy-start.6
  1418.4 7.8 copy-start.10
  1443.5 2.4 copy-start.9
  1445.9 2.5 copy-start.20
  1448.5 2.5 copy-start.34
Sparse Core Ops, SparseCore 0:
  10.9 59.1 all-gather.9
  73.0 55.2 all-gather.11
  131.2 98.2 all-gather.7
  232.2 80.1 all-gather.13
  315.1 193.3 all-gather.17
  511.2 192.9 all-gather.15
  707.1 192.9 all-gather.19
  1061.2 1932.2 all-reduce.8
  2995.8 881.7 reduce-scatter.6
  3880.4 1404.7 reduce-scatter.4
where the time goes:
time: 5300 us; the launch traced here: 5290 us
  waiting for transfers between devices  4510 us (85%)
  matrix products  390 us (7%)
  other arithmetic  144 us (3%)
  local copies, waits for them, and re-layouts  115 us (2%)
  blocking collectives  99.8 us (2%)
    unnamed x12, waiting for transfers between devices  2360 us
    reduce_scatter x1, waiting for transfers between devices, local(): lax.psum_scatter(across(hidden, grad_low), ('ctx', 'fsdp'), scatter_dimen...  1400 us
    all_gather x1, waiting for transfers between devices, local(): lax.all_gather(up_weight, ('ctx', 'fsdp'), axis=0, tiled=True)  188 us
    all_gather x1, waiting for transfers between devices, local(): lax.all_gather(down_weight, ('ctx', 'fsdp'), axis=0, tiled=True)  178 us
    all_gather x1, waiting for transfers between devices, local(): lax.all_gather(gate_weight, ('ctx', 'fsdp'), axis=0, tiled=True)  178 us
    dot_general x23, matrix products, across(): lax.dot_general(left, right, (((0,), (0,)), ((), ())), preferred_element_...  139 us
    dot_general x31, matrix products, against(): lax.dot_general(left, right, (((1,), (1,)), ((), ())), preferred_element_...  139 us
    dot_general x23, matrix products, product(): return jnp.dot(left, right, preferred_element_type=jnp.float32)  112 us
  transfers between devices with their start and end apart: 18, of which 16 were waited for; matrix products, arithmetic and copies ran while one was open for 9% of the time, Pallas kernels for 0%

commit v1 on v0

--- a/solution.py
+++ b/solution.py
@@ -122,6 +122,54 @@
     return inverse * (grad_normal - normal * jnp.mean(grad_normal * normal, axis=1, keepdims=True))
 
 
+def swapped(x, axis, mask):
+    size = lax.axis_size(axis)
+    return lax.ppermute(x, axis, [(i, i ^ mask) for i in range(size)])
+
+
+def mask_orders(axis):
+    size = lax.axis_size(axis)
+    masks = [1 << bit for bit in range(size.bit_length() - 1)]
+    return [masks, masks[::-1]]
+
+
+def gather_swapping(x, axis):
+    size = lax.axis_size(axis)
+    orders = mask_orders(axis)
+    place = lax.axis_index(axis)
+    parts = []
+    for part, order in zip(jnp.split(x, len(orders), axis=0), orders):
+        bits = size.bit_length() - 1
+        held = part.reshape((1,) * bits + part.shape)
+        for mask in order:
+            got = swapped(held, axis, mask)
+            dim = bits - mask.bit_length()
+            low = (place & mask) == 0
+            held = jnp.concatenate(
+                [jnp.where(low, held, got), jnp.where(low, got, held)], axis=dim
+            )
+        parts.append(held.reshape((size,) + part.shape))
+    return jnp.concatenate(parts, axis=1)
+
+
+def scatter_swapping(x, axis):
+    size = lax.axis_size(axis)
+    orders = mask_orders(axis)
+    place = lax.axis_index(axis)
+    parts = []
+    for part, order in zip(jnp.split(x, len(orders), axis=1), orders):
+        bits = size.bit_length() - 1
+        held = part.reshape((2,) * bits + part.shape[1:])
+        for mask in order:
+            dim = bits - mask.bit_length()
+            bit = (place & mask) // mask
+            sent = lax.dynamic_slice_in_dim(held, 1 - bit, 1, dim).astype(jnp.bfloat16)
+            own = lax.dynamic_slice_in_dim(held, bit, 1, dim)
+            held = own + swapped(sent, axis, mask).astype(jnp.float32)
+        parts.append(held.reshape(part.shape[1:]))
+    return jnp.concatenate(parts, axis=0)
+
+
 def local(
     tokens,
     cotangent,
@@ -136,8 +184,12 @@
     up_weight,
     down_weight,
 ):
+    both = ("ctx", "fsdp")
+    ctx_size = lax.axis_size("ctx")
+    fsdp_size = lax.axis_size("fsdp")
     stream = tokens[0].astype(jnp.float32)
     tok_rows = stream.shape[0]
+    own_rows = query_weight.shape[0]
     group_size = HEADS // KV_HEADS
     kv_width = KV_HEADS * HEAD_DIM
     reach_blocks = WINDOW // STRETCH
@@ -157,38 +209,45 @@
         & (query_doc[:, None] == key_doc[None, :])
     )
     visible = jnp.tile(visible, (group_size, 1))
+
+    gains = jnp.zeros((own_rows, 128), jnp.bfloat16)
+    gains = gains.at[:, 0].set(attn_gain).at[:, 1].set(mlp_gain)
+    front_all = lax.all_gather(
+        jnp.concatenate([query_weight, key_weight, value_weight, gains], axis=1),
+        both, axis=0, tiled=True,
+    )
+    front_weight = front_all[:, : D + 2 * kv_width]
+    gain_one = front_all[:, D + 2 * kv_width].astype(jnp.float32)
+    gain_two = front_all[:, D + 2 * kv_width + 1].astype(jnp.float32)
+    out_all = lax.all_gather(out_weight, both, axis=0, tiled=True)
+
+    ff_own = FF // ctx_size
+    pair = jnp.stack([gate_weight, up_weight]).reshape(2, own_rows, ctx_size, ff_own)
+    pair = lax.all_to_all(
+        pair.transpose(2, 0, 1, 3), "ctx", split_axis=0, concat_axis=0, tiled=True
+    )
+    pair = gather_swapping(pair.reshape(ctx_size * 2 * own_rows, ff_own), "fsdp")
+    pair = pair.reshape(fsdp_size, ctx_size, 2, own_rows, ff_own).transpose(2, 1, 0, 3, 4)
+    pair = pair.reshape(2, D, ff_own)
+    gate_own, up_own = pair[0], pair[1]
+    down_own = gather_swapping(down_weight, "fsdp").reshape(ff_own, D)
+    cot_all = lax.all_gather(cotangent[0], "ctx", axis=0, tiled=True)
+
     inv_one = lax.rsqrt(jnp.mean(stream * stream, axis=1, keepdims=True) + EPS)
     normal_one = stream * inv_one
-    pieces = (
-        lax.all_gather(attn_gain, ("ctx", "fsdp"), axis=0, tiled=True),
-        lax.all_gather(query_weight, ("ctx", "fsdp"), axis=0, tiled=True),
-        lax.all_gather(key_weight, ("ctx", "fsdp"), axis=0, tiled=True),
-        lax.all_gather(value_weight, ("ctx", "fsdp"), axis=0, tiled=True),
-    )
-    gain_piece = pieces[0].astype(jnp.float32)
-    normed = (normal_one * gain_piece).astype(jnp.bfloat16)
-    gain_full = gain_piece
-    front = (
-        product(normed, pieces[1]),
-        product(normed, pieces[2]),
-        product(normed, pieces[3]),
-        gain_full,
-    )
-    kept = tuple((pieces[1 + slot] for slot in range(3)))
-    attn_sums = front + kept
-    gain_one = attn_sums[3]
     normed_one = (normal_one * gain_one).astype(jnp.bfloat16)
+    front = product(normed_one, front_weight)
     query_rot = (
-        rotate(attn_sums[0].reshape(tok_rows, HEADS, HEAD_DIM), position, 1.0)
+        rotate(front[:, :D].reshape(tok_rows, HEADS, HEAD_DIM), position, 1.0)
         .astype(jnp.bfloat16)
         .reshape(tok_rows, D)
     )
     key_rot = (
-        rotate(attn_sums[1].reshape(tok_rows, KV_HEADS, HEAD_DIM), position, 1.0)
+        rotate(front[:, D : D + kv_width].reshape(tok_rows, KV_HEADS, HEAD_DIM), position, 1.0)
         .astype(jnp.bfloat16)
         .reshape(tok_rows, kv_width)
     )
-    value_low = attn_sums[2].astype(jnp.bfloat16)
+    value_low = front[:, D + kv_width :].astype(jnp.bfloat16)
     key_list = [key_rot]
     value_list = [value_low]
     own_pair = jnp.stack([key_rot, value_low])
@@ -201,58 +260,53 @@
     query_heads = to_groups(query_rot, tok_rows)
     head_out, row_max, row_total = attend_forward(query_heads, key_heads, value_heads, visible)
     attn_mix = from_groups(head_out, tok_rows).astype(jnp.bfloat16)
-    pieces = (
-        lax.all_gather(out_weight, ("ctx", "fsdp"), axis=0, tiled=True),
-        lax.all_gather(mlp_gain, ("ctx", "fsdp"), axis=0, tiled=True),
-    )
-    mixed_part = attn_mix
-    gain_full = pieces[1].astype(jnp.float32)
-    kept = pieces[0]
-    resid = stream + product(mixed_part, pieces[0])
+    resid = stream + product(attn_mix, out_all)
     inv_two = lax.rsqrt(jnp.mean(resid * resid, axis=1, keepdims=True) + EPS)
     normal_two = resid * inv_two
-    normed_two = (normal_two * gain_full).astype(jnp.bfloat16)
-    pieces = (
-        lax.all_gather(gate_weight, ("ctx", "fsdp"), axis=0, tiled=True),
-        lax.all_gather(up_weight, ("ctx", "fsdp"), axis=0, tiled=True),
-    )
-    part = normed_two
-    gate_sum = product(part, pieces[0])
-    up_sum = product(part, pieces[1])
+    normed_two = (normal_two * gain_two).astype(jnp.bfloat16)
+
+    normed_all = lax.all_gather(normed_two, "ctx", axis=0, tiled=True)
+    gate_sum = product(normed_all, gate_own)
+    up_sum = product(normed_all, up_own)
     sigmoid_gate = jax.nn.sigmoid(gate_sum)
     silu_gate = gate_sum * sigmoid_gate
     hidden = (silu_gate * up_sum).astype(jnp.bfloat16)
-    down_sum = product(hidden, lax.all_gather(down_weight, ("ctx", "fsdp"), axis=0, tiled=True))
-    mixed = (resid + down_sum).astype(jnp.bfloat16)
-    grad_low = cotangent[0]
-    grad_stream = grad_low.astype(jnp.float32)
-    grad_hidden = against(
-        grad_low, lax.all_gather(down_weight, ("ctx", "fsdp"), axis=0, tiled=True)
-    )
-    grad_down = lax.psum_scatter(
-        across(hidden, grad_low), ("ctx", "fsdp"), scatter_dimension=0, tiled=True
-    )
+    grad_hidden = against(cot_all, down_own)
     grad_gate_low = (
         grad_hidden * up_sum * sigmoid_gate * (1.0 + gate_sum * (1.0 - sigmoid_gate))
     ).astype(jnp.bfloat16)
     grad_up_low = (grad_hidden * silu_gate).astype(jnp.bfloat16)
-    pieces = (
-        lax.all_gather(gate_weight, ("ctx", "fsdp"), axis=0, tiled=True),
-        lax.all_gather(up_weight, ("ctx", "fsdp"), axis=0, tiled=True),
-    )
-    columns = against(grad_gate_low, pieces[0]) + against(grad_up_low, pieces[1])
-    part = normed_two
-    gate_grads = lax.psum_scatter(
-        jnp.concatenate([across(part, grad_gate_low), across(part, grad_up_low)], axis=1),
-        ("ctx", "fsdp"),
-        scatter_dimension=0,
-        tiled=True,
-    )
+    columns_part = against(grad_gate_low, gate_own) + against(grad_up_low, up_own)
+    columns = lax.psum_scatter(
+        columns_part.astype(jnp.bfloat16), "ctx", scatter_dimension=0, tiled=True
+    ).astype(jnp.float32)
+    down_part = product(hidden, down_own).astype(jnp.bfloat16)
+    down_sum = lax.psum_scatter(down_part, "ctx", scatter_dimension=0, tiled=True)
+    mixed = (resid + down_sum.astype(jnp.float32)).astype(jnp.bfloat16)
+
+    down_terms = across(hidden, cot_all).reshape(fsdp_size, -1, D)
+    grad_down = scatter_swapping(down_terms, "fsdp")
+    pair_terms = jnp.stack([across(normed_all, grad_gate_low), across(normed_all, grad_up_low)])
+    pair_terms = pair_terms.reshape(2, ctx_size, fsdp_size, own_rows, ff_own)
+    pair_terms = pair_terms.transpose(2, 1, 0, 3, 4)
+    pair_sum = scatter_swapping(pair_terms.reshape(fsdp_size, -1, ff_own), "fsdp")
+    pair_sum = pair_sum.astype(jnp.bfloat16).reshape(ctx_size, 2, own_rows, ff_own)
+    pair_sum = lax.all_to_all(pair_sum, "ctx", split_axis=0, concat_axis=0, tiled=True)
+    pair_sum = pair_sum.transpose(1, 2, 0, 3).reshape(2, own_rows, FF).astype(jnp.float32)
+
+    grad_stream = cotangent[0].astype(jnp.float32)
     mlp_gain_local = jnp.sum(columns * normal_two, axis=0)
-    grad_resid = grad_stream + norm_back(columns * gain_full, normal_two, inv_two)
+    grad_resid = grad_stream + norm_back(columns * gain_two, normal_two, inv_two)
     grad_resid_low = grad_resid.astype(jnp.bfloat16)
-    grad_mix = against(grad_resid_low, kept)
+    grad_mix = against(grad_resid_low, out_all)
     grad_mix_low = grad_mix.astype(jnp.bfloat16)
+    out_grad = lax.psum_scatter(
+        lax.psum_scatter(
+            across(attn_mix, grad_resid_low).astype(jnp.bfloat16),
+            "ctx", scatter_dimension=0, tiled=True,
+        ),
+        "fsdp", scatter_dimension=0, tiled=True,
+    ).astype(jnp.float32)
     grad_query_heads, grad_key_heads, grad_value_heads = attend_backward(
         query_heads,
         key_heads,
@@ -290,44 +344,33 @@
         .astype(jnp.bfloat16)
     )
     grad_value_low = grad_value_total.astype(jnp.bfloat16)
-    grad_normed_one = (
-        against(grad_query_low, attn_sums[4])
-        + against(grad_key_low, attn_sums[5])
-        + against(grad_value_low, attn_sums[6])
-    )
-    part = normed_one
-    mixed_part = attn_mix
-    attn_grads = lax.psum_scatter(
-        jnp.concatenate(
-            [
-                across(part, grad_query_low),
-                across(part, grad_key_low),
-                across(part, grad_value_low),
-                across(mixed_part, grad_resid_low),
-            ],
-            axis=1,
-        ),
-        ("ctx", "fsdp"),
-        scatter_dimension=0,
-        tiled=True,
-    )
+    front_low = jnp.concatenate([grad_query_low, grad_key_low, grad_value_low], axis=1)
+    grad_normed_one = against(front_low, front_weight)
     attn_gain_local = jnp.sum(grad_normed_one * normal_one, axis=0)
-    gain_grads = (
-        lax.psum_scatter(attn_gain_local, ("ctx", "fsdp"), scatter_dimension=0, tiled=True),
-        lax.psum_scatter(mlp_gain_local, ("ctx", "fsdp"), scatter_dimension=0, tiled=True),
-    )
+    front_terms = jnp.concatenate(
+        [
+            across(normed_one, front_low),
+            jnp.pad(jnp.stack([attn_gain_local, mlp_gain_local], axis=1), ((0, 0), (0, 126))),
+        ],
+        axis=1,
+    ).astype(jnp.bfloat16)
+    front_grad = lax.psum_scatter(
+        lax.psum_scatter(front_terms, "ctx", scatter_dimension=0, tiled=True),
+        "fsdp", scatter_dimension=0, tiled=True,
+    ).astype(jnp.float32)
     grad_input = grad_resid + norm_back(grad_normed_one * gain_one, normal_one, inv_one)
+    width = D + 2 * kv_width
     return (
         mixed[None],
         grad_input.astype(jnp.bfloat16)[None],
-        gain_grads[0],
-        attn_grads[:, :D],
-        attn_grads[:, D : D + kv_width],
-        attn_grads[:, D + kv_width : D + 2 * kv_width],
-        attn_grads[:, D + 2 * kv_width :],
-        gain_grads[1],
-        gate_grads[:, :FF],
-        gate_grads[:, FF:],
+        front_grad[:, width],
+        front_grad[:, :D],
+        front_grad[:, D : D + kv_width],
+        front_grad[:, D + kv_width : width],
+        out_grad,
+        front_grad[:, width + 1],
+        pair_sum[0],
+        pair_sum[1],
         grad_down,
     )
 

time: 5300 us -> 1250 us (0.24)
  waiting for transfers between devices: 4510 us -> 626 us
  blocking collectives: 99.8 us -> 0 us
  matrix products: 390 us -> 303 us
  starting transfers between devices: 17.7 us -> 81.7 us
    unnamed x12 -> x10, waiting for transfers between devices: 2360 us -> 1.35 us
    reduce_scatter x1 -> x6, waiting for transfers between devices: 1400 us -> 187 us  [the longest x1 88.1 us: local(): lax.psum_scatter(down_part, 'ctx', scatter_dimension=0, tiled=True)]
    all_gather x7 -> x4, waiting for transfers between devices: 642 us -> 95.9 us  [the longest x1 95.9 us: local(): lax.all_gather(jnp.concatenate([query_weight, key_weight, value_weight, g...]
    ppermute x0 -> x16, waiting for transfers between devices: none -> 154 us  [swapped(): return lax.ppermute(x, axis, [(i, i ^ mask) for i in range(size)])]
    all_to_all x0 -> x2, waiting for transfers between devices: none -> 104 us  [the longest x1 101 us: local(): lax.all_to_all(pair.transpose(2, 0, 1, 3), 'ctx', split_axis=0, concat_ax...]
    unnamed x2 -> x0, blocking collectives: 99.8 us -> none
    concatenate x2 -> x16, other arithmetic: 116 us -> 31.8 us  [the longest x1 10.7 us: local(): jnp.concatenate([across(normed_one, front_low), jnp.pad(jnp.stack([attn_g...]
    dot_general x23 -> x21, matrix products: 139 us -> 81.4 us  [across(): lax.dot_general(left, right, (((0,), (0,)), ((), ())), preferred_element_...]
  transfers between devices with their start and end apart: 18 -> 36, of which waited for: 16 -> 24; matrix products, arithmetic and copies ran while one was open for 9% -> 34% of each run, Pallas kernels for 0% -> 0%
where the time goes in v1:
time: 1250 us; the launch traced here: 1240 us
  waiting for transfers between devices  626 us (50%)
  matrix products  303 us (24%)
  local copies, waits for them, and re-layouts  120 us (10%)
  other arithmetic  97.1 us (8%)
  starting transfers between devices  81.7 us (7%)
  between operations  15.6 us (1%)
    ppermute x16, waiting for transfers between devices, swapped(): return lax.ppermute(x, axis, [(i, i ^ mask) for i in range(size)])  154 us
    dot_general x29, matrix products, against(): lax.dot_general(left, right, (((1,), (1,)), ((), ())), preferred_element_...  126 us
    all_to_all x1, waiting for transfers between devices, local(): lax.all_to_all(pair.transpose(2, 0, 1, 3), 'ctx', split_axis=0, concat_ax...  101 us
    dot_general x21, matrix products, product(): return jnp.dot(left, right, preferred_element_type=jnp.float32)  96.1 us
    all_gather x1, waiting for transfers between devices, local(): lax.all_gather(jnp.concatenate([query_weight, key_weight, value_weight, g...  95.9 us
    reduce_scatter x1, waiting for transfers between devices, local(): lax.psum_scatter(down_part, 'ctx', scatter_dimension=0, tiled=True)  88.1 us
    ppermute x8, waiting for transfers between devices, passed_along(): return lax.ppermute(x, axis, pairs)  83.3 us
    dot_general x21, matrix products, across(): lax.dot_general(left, right, (((0,), (0,)), ((), ())), preferred_element_...  81.4 us
  transfers between devices with their start and end apart: 36, of which 24 were waited for; matrix products, arithmetic and copies ran while one was open for 34% of the time, Pallas kernels for 0%

profile of v1, /device:TPU:0, one launch (start us, length us, event | category | flops | bytes accessed | tf_op | source)
XLA Modules:
  0.0 1243.5 jit_solution(6408392209763482411)
XLA Ops:
  18.7 95.9 %all-gather.6.cloned.1.call-done = bf16[2048,3200]{1,0:T(8,128)(2,1)} async-done(((bf16[64,3200]{1,0:T(8,128)(2,1)}), bf16[2048,3200]{1,0:T(8,128)(2,1)}) %all-gather.6.cloned.1.call-update) | async-done | bytes 13107216 | tf_op jit(solution)/shard_map/all_gather | solution.py:215
  116.4 6.5 fusion.52
  134.8 4.3 collective-permute-start
  140.1 2.9 collective-permute-start.1
  154.7 4.7 collective-permute-done
  161.2 12.0 collective-permute-done.1
  175.2 14.3 %collective-permute-done.2 = bf16[2,256,512]{2,1,0:T(8,128)(2,1)} collective-permute-done((bf16[2,256,512]{2,1,0:T(8,128)(2,1)}, bf16[2,256,512]{2,1,0:T(8,128)(2,1)}, u32[]{:S(2)}, u32[]{:S(2)}) %collective-permute-start.2) | collective-permute-done | bytes 524320 | tf_op jit(solution)/shard_map/ppermute | solution.py:22
  194.5 3.2 copy.153
  210.7 3.8 copy.154
  214.5 53.1 %while.34 = (s32[]{:T(128)}, bf16[8,1024,64]{1,2,0:T(8,128)(2,1)}, f32[8,1024,1]{1,2,0:T(1,128)}, f32[8,1024,1]{1,2,0:T(1,128)}, bf16[8,1024,64]{2,1,0:T(8,128)(...) while((s32[]{:T(128)}, bf16[8,1024,64]{1,2,0:T(8,128)(2,1)}, ...), condition=%wide.region_10.11_spmd.clone.clone, body=%wide.region_7.10_spmd.clone.sunk.clone | while | flops 346028032 | bytes 17275476 | solution.py:100
  218.3 2.8 fusion.179
  231.6 2.8 fusion.179
  238.2 2.8 fusion.179
  244.9 2.8 fusion.179
  251.5 2.8 fusion.179
  258.1 2.8 fusion.179
  264.8 2.8 fusion.179
  267.6 3.1 convert_element_type.233
  273.2 6.4 multiply_reduce_fusion.1
  286.0 41.3 %all-to-all-start = ((bf16[8,2,64,1024]{3,2,1,0:T(8,128)(2,1)}), bf16[8,2,64,1024]{3,2,1,0:T(8,128)(2,1)S(1)}, u32[]{:S(2)}, u32[]{:S(2)}) async-start(bf16[8,2,64,1024]{3,2,1,0:T(8,128)(2,1)} %copy.156), calls=%async_computation | async-start | bytes 4194304 | tf_op jit(solution)/shard_map/all_to_all | solution.py:226
  331.0 101.5 %all-to-all-done = bf16[8,2,64,1024]{3,2,1,0:T(8,128)(2,1)S(1)} async-done(((bf16[8,2,64,1024]{3,2,1,0:T(8,128)(2,1)}), bf16[8,2,64,1024]{3,2,1,0:T(8,128)(2,1)S(1)}, u32[]{:S(2)}, u32[]{:S(2)}) %all-to-all-start) | async-done | bytes 2097184 | tf_op jit(solution)/shard_map/all_to_all | solution.py:226
  439.8 20.5 %collective-permute-done.4 = bf16[1,1,512,1024]{3,2,1,0:T(8,128)(2,1)S(1)} collective-permute-done((bf16[1,1,512,1024]{3,2,1,0:T(8,128)(2,1)}, bf16[1,1,512,1024]{3,2,1,0:T(8,128)(2,1)S(1)}, u32[]{:S(2)}, u32[]{:S(2)}) %collective-permute-start.4) | collective-permute-done | bytes 1048608 | tf_op jit(solution)/shard_map/ppermute | solution.py:127
  464.8 18.0 %collective-permute-done.11 = bf16[2,1,128,2048]{3,2,1,0:T(8,128)(2,1)S(1)} collective-permute-done((bf16[2,1,128,2048]{3,2,1,0:T(8,128)(2,1)S(1)}, bf16[2,1,128,2048]{3,2,1,0:T(8,128)(2,1)S(1)}, u32[]{:S(2)}, u32[]{:S(2)}) %collective-permute-start.11) | collective-permute-done | bytes 1048608 | tf_op jit(solution)/shard_map/ppermute | solution.py:127
  487.3 40.8 %collective-permute-done.5 = bf16[1,2,512,1024]{3,2,1,0:T(8,128)(2,1)S(1)} collective-permute-done((bf16[1,2,512,1024]{3,2,1,0:T(8,128)(2,1)S(1)}, bf16[1,2,512,1024]{3,2,1,0:T(8,128)(2,1)S(1)}, u32[]{:S(2)}, u32[]{:S(2)}) %collective-permute-start.5) | collective-permute-done | bytes 2097184 | tf_op jit(solution)/shard_map/ppermute | solution.py:127
  533.4 7.8 pad_maximum_fusion.1
  541.2 3.9 fusion.107
  550.1 14.5 %fusion.118 = f32[2048,1024]{1,0:T(8,128)} fusion(bf16[2048,2048]{1,0:T(8,128)(2,1)} %all-gather.10.cloned.1.call-done, bf16[2048,1024]{1,0:T(8,128)(2,1)} %bitcast.364), kind=kOutput, calls=%fused_computation.257 | convolution fusion | flops 8589934592 | bytes 20971520 | tf_op jit(solution)/shard_map/dot_general | solution.py:26
  564.6 11.0 fusion.117
  575.6 22.4 %fusion.57 = (bf16[2048,1024]{1,0:T(8,128)(2,1)}, bf16[2048,1024]{1,0:T(8,128)(2,1)}, bf16[2048,1024]{1,0:T(8,128)(2,1)}) fusion(f32[2048,1024]{1,0:T(8,128)} %fusion.117, f32[2048,1024]{1,0:T(8,128)} %fusion.118, bf16[1024,2048]{1,0:T(8,128)(2,1)} %bitcast.362, bf16[1,2048,2048]{2,1,0:T(8,128)(2,1)} %all-gather.12.cloned.1.call-done), kind=kOutput, calls=%fused_computation.70 | convolution fusion | flops 8621391872 | bytes 41943040 | tf_op jit(solution)/shard_map/dot_general | solution.py:30
  598.0 14.2 %fusion.119 = f32[2048,2048]{1,0:T(8,128)} fusion(bf16[2048,1024]{1,0:T(8,128)(2,1)} %get-tuple-element.340, bf16[2048,1024]{1,0:T(8,128)(2,1)S(1)} %bitcast.367), kind=kOutput, calls=%fused_computation.258 | convolution fusion | flops 8589934592 | bytes 25165824 | tf_op jit(solution)/shard_map/dot_general | solution.py:30
  612.2 16.1 %add_convert_fusion = bf16[2048,2048]{1,0:T(8,128)(2,1)} fusion(f32[2048,2048]{1,0:T(8,128)} %fusion.119, bf16[2048,1024]{1,0:T(8,128)(2,1)} %get-tuple-element.339, bf16[2048,1024]{1,0:T(8,128)(2,1)S(1)} %bitcast.365), kind=kOutput, calls=%fused_computation.57 | convolution fusion | flops 8598323200 | bytes 33554432 | tf_op jit(solution)/shard_map/dot_general | solution.py:30
  628.4 14.0 %convolution_convert_fusion.2 = bf16[2048,2048]{1,0:T(8,128)(2,1)} fusion(bf16[2048,1024]{1,0:T(8,128)(2,1)} %get-tuple-element.341, bf16[1024,2048]{1,0:T(8,128)(2,1)} %bitcast.363), kind=kOutput, calls=%fused_computation.79 | convolution fusion | flops 8594128896 | bytes 16777216 | tf_op jit(solution)/shard_map/dot_general | solution.py:26
  642.7 72.8 %reduce-scatter.9.cloned.1.call-done = bf16[256,2048]{1,0:T(8,128)(2,1)} async-done(((bf16[2048,2048]{1,0:T(8,128)(2,1)}), bf16[256,2048]{1,0:T(8,128)(2,1)}) %reduce-scatter.9.cloned.1.call-update) | async-done | bytes 1048592 | tf_op jit(solution)/shard_map/reduce_scatter | solution.py:280
  717.6 88.1 %reduce-scatter.7.cloned.1.call-done = bf16[256,2048]{1,0:T(8,128)(2,1)} async-done(((bf16[2048,2048]{1,0:T(8,128)(2,1)}), bf16[256,2048]{1,0:T(8,128)(2,1)}) %reduce-scatter.7.cloned.1.call-update) | async-done | bytes 1048592 | tf_op jit(solution)/shard_map/reduce_scatter | solution.py:284
  805.7 3.8 fusion.71
  810.8 5.7 convolution_convert_fusion.1
  816.5 6.4 convolution_convert_fusion.3
  825.5 100.3 %while.35 = (s32[]{:T(128)}, f32[8,1024,64]{1,2,0:T(8,128)}, f32[8,1280,64]{1,2,0:T(8,128)}, f32[8,1280,64]{1,2,0:T(8,128)}, bf16[8,1024,64]{2,1,0:T(8,128)(2,1)...) while((s32[]{:T(128)}, f32[8,1024,64]{1,2,0:T(8,128)}, ...), condition=%wide.region_17.18_spmd.clone.clone, body=%wide.region_15.17_spmd.clone.sunk.clone | while | flops 852114432 | bytes 42636400 | solution.py:118
  828.0 3.3 multiply_reduce_fusion.4
  840.6 3.2 multiply_reduce_fusion.4
  853.1 3.2 multiply_reduce_fusion.4
  865.6 3.2 multiply_reduce_fusion.4
  878.2 3.2 multiply_reduce_fusion.4
  890.7 3.2 multiply_reduce_fusion.4
  903.2 3.2 multiply_reduce_fusion.4
  915.7 3.2 multiply_reduce_fusion.4
  936.8 12.6 %collective-permute-done.13 = bf16[2,256,512]{1,2,0:T(8,128)(2,1)S(1)} collective-permute-done((bf16[2,256,512]{1,2,0:T(8,128)(2,1)S(1)}, bf16[2,256,512]{1,2,0:T(8,128)(2,1)S(1)}, u32[]{:S(2)}, u32[]{:S(2)}) %collective-permute-start.13) | collective-permute-done | bytes 524320 | tf_op jit(solution)/shard_map/ppermute | solution.py:22
  949.6 5.0 collective-permute-done.14
  954.7 34.8 %collective-permute-done.15 = bf16[2,256,512]{1,2,0:T(8,128)(2,1)S(1)} collective-permute-done((bf16[2,256,512]{1,2,0:T(8,128)(2,1)S(1)}, bf16[2,256,512]{1,2,0:T(8,128)(2,1)S(1)}, u32[]{:S(2)}, u32[]{:S(2)}) %collective-permute-start.15) | collective-permute-done | bytes 524320 | tf_op jit(solution)/shard_map/ppermute | solution.py:22
  992.0 9.7 fusion.79
  1002.0 8.1 convolution_convert_fusion
  1010.1 10.7 fusion.49
  1021.1 12.8 %fusion.120 = f32[2048,1024]{1,0:T(8,128)S(1)} fusion(bf16[2048,2048]{1,0:T(8,128)(2,1)} %all-gather.10.cloned.1.call-done, bf16[2048,1024]{1,0:T(8,128)(2,1)} %get-tuple-element.340), kind=kOutput, calls=%fused_computation.259 | convolution fusion | flops 8589934592 | bytes 20971520 | tf_op jit(solution)/shard_map/dot_general | solution.py:36
  1033.9 11.7 fusion.121
  1049.8 6.8 fusion.105
  1065.0 14.0 %fusion.58 = f32[1024,2048]{1,0:T(8,128)S(1)} fusion(bf16[2048,1024]{1,0:T(8,128)(2,1)} %get-tuple-element.341, bf16[1,2048,2048]{2,1,0:T(8,128)(2,1)} %all-gather.12.cloned.1.call-done), kind=kOutput, calls=%fused_computation.71 | convolution fusion | flops 8589934592 | bytes 20971520 | tf_op jit(solution)/shard_map/dot_general | solution.py:36
  1079.0 24.0 %collective-permute-done.16 = bf16[2,1,512,1024]{3,2,1,0:T(8,128)(2,1)} collective-permute-done((bf16[2,1,512,1024]{3,2,1,0:T(8,128)(2,1)S(1)}, bf16[2,1,512,1024]{3,2,1,0:T(8,128)(2,1)}, u32[]{:S(2)}, u32[]{:S(2)}) %collective-permute-start.16) | collective-permute-done | bytes 2097184 | tf_op jit(solution)/shard_map/ppermute | solution.py:127
  1121.4 8.0 collective-permute-done.17
  1131.7 7.8 collective-permute-done.19
  1141.4 3.6 all-to-all-start.1
  1149.4 6.4 collective-permute-done.20
  1160.8 14.3 %collective-permute-done.22 = bf16[1,2,128,2048]{3,2,1,0:T(8,128)(2,1)} collective-permute-done((bf16[1,2,128,2048]{3,2,1,0:T(8,128)(2,1)}, bf16[1,2,128,2048]{3,2,1,0:T(8,128)(2,1)}, u32[]{:S(2)}, u32[]{:S(2)}) %collective-permute-start.22) | collective-permute-done | bytes 1048608 | tf_op jit(solution)/shard_map/ppermute | solution.py:127
  1178.2 12.4 collective-permute-done.21
  1205.2 26.2 %reduce-scatter.13.cloned.1.call-done = bf16[64,3200]{1,0:T(8,128)(2,1)} async-done(((bf16[256,3200]{1,0:T(8,128)(2,1)}), bf16[64,3200]{1,0:T(8,128)(2,1)}) %reduce-scatter.13.cloned.1.call-update) | async-done | bytes 409616 | tf_op jit(solution)/shard_map/reduce_scatter | solution.py:357
  (386 shorter events, 293.7 us)
Async XLA Ops:
  7.2 109.2 %copy-start.7 = (bf16[1,256,2048]{2,1,0:T(8,128)(2,1)S(1)}, bf16[1,256,2048]{2,1,0:T(8,128)(2,1)}, u32[]{:S(2)}) copy-start(bf16[1,256,2048]{2,1,0:T(8,128)(2,1)} %param.20) | copy-start | bytes 3145732
  7.2 107.3 %all-gather.6.cloned.1.call-start = ((), (), s32[]{:S(2)}) async-start(), calls=%async_computation.8 | async-start | bytes 13516800 | tf_op jit(solution)/shard_map/all_gather | solution.py:215
  13.1 260.1 %all-gather.8.cloned.1.call-start = ((), (), s32[]{:S(2)}) async-start(), calls=%async_computation.9 | async-start | bytes 8650752 | tf_op jit(solution)/shard_map/all_gather | solution.py:222
  13.9 536.2 %all-gather.10.cloned.1.call-start = ((), (), s32[]{:S(2)}) async-start(), calls=%async_computation.10 | async-start | bytes 9437184 | tf_op jit(solution)/shard_map/all_gather | solution.py:268
  17.3 105.7 %copy-start.39 = (f32[256]{0:T(256)}, f32[256]{0:T(256)S(1)}, u32[]{:S(2)}) copy-start(f32[256]{0:T(256)S(1)} %add_rsqrt_fusion.1) | copy-start | bytes 3076
  18.1 133.2 %copy-start.32 = (f32[256,32]{0,1:T(8,128)}, f32[256,32]{0,1:T(8,128)S(1)}, u32[]{:S(2)}) copy-start(f32[256,32]{0,1:T(8,128)S(1)} %get-tuple-element.400) | copy-start | bytes 98308
  116.4 6.6 copy-start.35
  116.4 163.2 %copy-start.37 = (f32[2048]{0:T(1024)}, f32[2048]{0:T(1024)S(1)}, u32[]{:S(2)}) copy-start(f32[2048]{0:T(1024)S(1)} %get-tuple-element.283) | copy-start | bytes 24580
  125.4 22.4 %copy-start.22 = (f32[256,3072]{1,0:T(8,128)S(1)}, f32[256,3072]{1,0:T(8,128)}, u32[]{:S(2)}) copy-start(f32[256,3072]{1,0:T(8,128)} %copy-done.21) | copy-start | bytes 9437188
  134.8 24.6 %collective-permute-start = (bf16[2,256,512]{2,1,0:T(8,128)(2,1)}, bf16[2,256,512]{2,1,0:T(8,128)(2,1)}, u32[]{:S(2)}, u32[]{:S(2)}) collective-permute-start(bf16[2,256,512]{2,1,0:T(8,128)(2,1)} %pad_maximum_fusion.17), channel_id=1, source_target_pairs={{0,16},{4,20},{8,24},{12,28},{1,17},{5,21},{9,25},{13,29},{2,18},{... | collective-permute-start | bytes 1572872 | tf_op jit(solution)/shard_map/ppermute | solution.py:22
  140.1 33.1 %collective-permute-start.1 = (bf16[2,256,512]{2,1,0:T(8,128)(2,1)}, bf16[2,256,512]{2,1,0:T(8,128)(2,1)}, u32[]{:S(2)}, u32[]{:S(2)}) collective-permute-start(bf16[2,256,512]{2,1,0:T(8,128)(2,1)} %pad_maximum_fusion.17), channel_id=1, source_target_pairs={{0,12},{4,16},{8,20},{12,24},{16,28},{1,13},{5,17},{9,21},{13,25},... | collective-permute-start | bytes 1572872 | tf_op jit(solution)/shard_map/ppermute | solution.py:22
  143.0 46.5 %collective-permute-start.2 = (bf16[2,256,512]{2,1,0:T(8,128)(2,1)}, bf16[2,256,512]{2,1,0:T(8,128)(2,1)}, u32[]{:S(2)}, u32[]{:S(2)}) collective-permute-start(bf16[2,256,512]{2,1,0:T(8,128)(2,1)} %pad_maximum_fusion.17), channel_id=1, source_target_pairs={{0,8},{4,12},{8,16},{12,20},{16,24},{20,28},{1,9},{5,13},{9,17},{1... | collective-permute-start | bytes 1572872 | tf_op jit(solution)/shard_map/ppermute | solution.py:22
  145.4 45.9 %collective-permute-start.3 = (bf16[2,256,512]{2,1,0:T(8,128)(2,1)}, bf16[2,256,512]{2,1,0:T(8,128)(2,1)}, u32[]{:S(2)}, u32[]{:S(2)}) collective-permute-start(bf16[2,256,512]{2,1,0:T(8,128)(2,1)} %pad_maximum_fusion.17), channel_id=1, source_target_pairs={{0,4},{4,8},{8,12},{12,16},{16,20},{20,24},{24,28},{1,5},{5,9},{9,... | collective-permute-start | bytes 1572872 | tf_op jit(solution)/shard_map/ppermute | solution.py:22
  175.2 18.2 %copy-start.27 = (bf16[256,8,32]{0,2,1:T(8,128)(2,1)S(1)}, bf16[256,8,32]{0,2,1:T(8,128)(2,1)}, u32[]{:S(2)}) copy-start(bf16[256,8,32]{0,2,1:T(8,128)(2,1)} %copy-done.26) | copy-start | bytes 393220
  175.2 18.2 %copy-start.29 = (bf16[256,8,32]{0,2,1:T(8,128)(2,1)S(1)}, bf16[256,8,32]{0,2,1:T(8,128)(2,1)}, u32[]{:S(2)}) copy-start(bf16[256,8,32]{0,2,1:T(8,128)(2,1)} %copy-done.28) | copy-start | bytes 393220
  267.6 11.9 copy-start
  267.6 11.9 copy-start.4
  286.0 41.9 %copy-start.16 = (bf16[256,2048]{1,0:T(8,128)(2,1)S(1)}, bf16[256,2048]{1,0:T(8,128)(2,1)}, u32[]{:S(2)}) copy-start(bf16[256,2048]{1,0:T(8,128)(2,1)} %param.31) | copy-start | bytes 3145732
  286.0 146.4 %all-to-all-start = ((bf16[8,2,64,1024]{3,2,1,0:T(8,128)(2,1)}), bf16[8,2,64,1024]{3,2,1,0:T(8,128)(2,1)S(1)}, u32[]{:S(2)}, u32[]{:S(2)}) async-start(bf16[8,2,64,1024]{3,2,1,0:T(8,128)(2,1)} %copy.156), calls=%async_computation | async-start | bytes 4194304 | tf_op jit(solution)/shard_map/all_to_all | solution.py:226
  327.3 248.3 %all-gather.12.cloned.1.call-start = ((), (), s32[]{:S(2)}) async-start(), calls=%async_computation.17 | async-start | bytes 9437184 | tf_op jit(solution)/shard_map/all_gather | solution.py:234
  327.9 387.7 %reduce-scatter.9.cloned.1.call-start = ((), (), s32[]{:S(2)}) async-start(), calls=%async_computation.12 | async-start | bytes 9437184 | tf_op jit(solution)/shard_map/reduce_scatter | solution.py:280
  329.0 106.9 %collective-permute-start.10 = (bf16[1,1,128,2048]{3,2,1,0:T(8,128)(2,1)}, bf16[1,1,128,2048]{3,2,1,0:T(8,128)(2,1)}, u32[]{:S(2)}, u32[]{:S(2)}) collective-permute-start(bf16[1,1,128,2048]{3,2,1,0:T(8,128)(2,1)} %get-tuple-element.383), channel_id=1, source_target_pairs={{0,2},{1,3},{2,0},{3,1},{4,6},{5,7},{6,4},{7,5},{8,10},{9,11},{10,... | collective-permute-start | bytes 1572872 | tf_op jit(solution)/shard_map/ppermute | solution.py:127
  330.4 105.5 %collective-permute-start.8 = (bf16[1,1,128,2048]{3,2,1,0:T(8,128)(2,1)}, bf16[1,1,128,2048]{3,2,1,0:T(8,128)(2,1)}, u32[]{:S(2)}, u32[]{:S(2)}) collective-permute-start(bf16[1,1,128,2048]{3,2,1,0:T(8,128)(2,1)} %get-tuple-element.382), channel_id=1, source_target_pairs={{0,1},{1,0},{2,3},{3,2},{4,5},{5,4},{6,7},{7,6},{8,9},{9,8},{10,11... | collective-permute-start | bytes 1572872 | tf_op jit(solution)/shard_map/ppermute | solution.py:127
  434.1 26.2 %collective-permute-start.4 = (bf16[1,1,512,1024]{3,2,1,0:T(8,128)(2,1)}, bf16[1,1,512,1024]{3,2,1,0:T(8,128)(2,1)S(1)}, u32[]{:S(2)}, u32[]{:S(2)}) collective-permute-start(bf16[1,1,512,1024]{3,2,1,0:T(8,128)(2,1)} %bitcast.30), channel_id=1, source_target_pairs={{0,1},{1,0},{2,3},{3,2},{4,5},{5,4},{6,7},{7,6},{8,9},{9,8},{10,11... | collective-permute-start | bytes 3145736 | tf_op jit(solution)/shard_map/ppermute | solution.py:127
  435.5 27.9 %collective-permute-start.6 = (bf16[1,1,512,1024]{3,2,1,0:T(8,128)(2,1)}, bf16[1,1,512,1024]{3,2,1,0:T(8,128)(2,1)S(1)}, u32[]{:S(2)}, u32[]{:S(2)}) collective-permute-start(bf16[1,1,512,1024]{3,2,1,0:T(8,128)(2,1)} %bitcast.368), channel_id=1, source_target_pairs={{0,2},{1,3},{2,0},{3,1},{4,6},{5,7},{6,4},{7,5},{8,10},{9,11},{10,... | collective-permute-start | bytes 3145736 | tf_op jit(solution)/shard_map/ppermute | solution.py:127
  437.4 45.4 %collective-permute-start.11 = (bf16[2,1,128,2048]{3,2,1,0:T(8,128)(2,1)S(1)}, bf16[2,1,128,2048]{3,2,1,0:T(8,128)(2,1)S(1)}, u32[]{:S(2)}, u32[]{:S(2)}) collective-permute-start(bf16[2,1,128,2048]{3,2,1,0:T(8,128)(2,1)S(1)} %pad_maximum_fusion.13), channel_id=1, source_target_pairs={{0,1},{1,0},{2,3},{3,2},{4,5},{5,4},{6,7},{7,6},{8,9},{9,8},{10,11... | collective-permute-start | bytes 3145736 | tf_op jit(solution)/shard_map/ppermute | solution.py:127
  439.2 45.1 %collective-permute-start.9 = (bf16[1,2,128,2048]{3,2,1,0:T(8,128)(2,1)S(1)}, bf16[1,2,128,2048]{3,2,1,0:T(8,128)(2,1)S(1)}, u32[]{:S(2)}, u32[]{:S(2)}) collective-permute-start(bf16[1,2,128,2048]{3,2,1,0:T(8,128)(2,1)S(1)} %pad_maximum_fusion.12), channel_id=1, source_target_pairs={{0,2},{1,3},{2,0},{3,1},{4,6},{5,7},{6,4},{7,5},{8,10},{9,11},{10,... | collective-permute-start | bytes 3145736 | tf_op jit(solution)/shard_map/ppermute | solution.py:127
  461.9 66.3 %collective-permute-start.5 = (bf16[1,2,512,1024]{3,2,1,0:T(8,128)(2,1)S(1)}, bf16[1,2,512,1024]{3,2,1,0:T(8,128)(2,1)S(1)}, u32[]{:S(2)}, u32[]{:S(2)}) collective-permute-start(bf16[1,2,512,1024]{3,2,1,0:T(8,128)(2,1)S(1)} %pad_maximum_fusion.5), channel_id=1, source_target_pairs={{0,2},{1,3},{2,0},{3,1},{4,6},{5,7},{6,4},{7,5},{8,10},{9,11},{10,... | collective-permute-start | bytes 6291464 | tf_op jit(solution)/shard_map/ppermute | solution.py:127
  463.8 66.9 %collective-permute-start.7 = (bf16[2,1,512,1024]{3,2,1,0:T(8,128)(2,1)S(1)}, bf16[2,1,512,1024]{3,2,1,0:T(8,128)(2,1)S(1)}, u32[]{:S(2)}, u32[]{:S(2)}) collective-permute-start(bf16[2,1,512,1024]{3,2,1,0:T(8,128)(2,1)S(1)} %pad_maximum_fusion.6), channel_id=1, source_target_pairs={{0,1},{1,0},{2,3},{3,2},{4,5},{5,4},{6,7},{7,6},{8,9},{9,8},{10,11... | collective-permute-start | bytes 6291464 | tf_op jit(solution)/shard_map/ppermute | solution.py:127
  550.1 14.5 %copy-start.18 = (bf16[1,8,4,64,1024]{4,3,2,1,0:T(8,128)(2,1)S(1)}, bf16[1,8,4,64,1024]{4,3,2,1,0:T(8,128)(2,1)}, u32[]{:S(2)}) copy-start(bf16[1,8,4,64,1024]{4,3,2,1,0:T(8,128)(2,1)} %copy.157) | copy-start | bytes 12582916
  550.1 14.5 %copy-start.43 = (bf16[2048,2048]{1,0:T(8,128)(2,1)S(1)}, bf16[2048,2048]{1,0:T(8,128)(2,1)}, u32[]{:S(2)}) copy-start(bf16[2048,2048]{1,0:T(8,128)(2,1)} %all-gather.10.cloned.1.call-done) | copy-start | bytes 25165828
  575.6 22.4 %copy-start.19 = (bf16[1,8,4,64,1024]{4,3,2,1,0:T(8,128)(2,1)S(1)}, bf16[1,8,4,64,1024]{4,3,2,1,0:T(8,128)(2,1)}, u32[]{:S(2)}) copy-start(bf16[1,8,4,64,1024]{4,3,2,1,0:T(8,128)(2,1)} %copy.157) | copy-start | bytes 12582916
  598.0 14.2 %copy-start.17 = (bf16[1,8,4,64,1024]{4,3,2,1,0:T(8,128)(2,1)S(1)}, bf16[1,8,4,64,1024]{4,3,2,1,0:T(8,128)(2,1)}, u32[]{:S(2)}) copy-start(bf16[1,8,4,64,1024]{4,3,2,1,0:T(8,128)(2,1)} %copy.158) | copy-start | bytes 12582916
  628.3 177.4 %reduce-scatter.7.cloned.1.call-start = ((), (), s32[]{:S(2)}) async-start(), calls=%async_computation.11 | async-start | bytes 9437184 | tf_op jit(solution)/shard_map/reduce_scatter | solution.py:284
  642.4 73.2 %copy-start.3 = (f32[256,2048]{1,0:T(8,128)S(1)}, f32[256,2048]{1,0:T(8,128)}, u32[]{:S(2)}) copy-start(f32[256,2048]{1,0:T(8,128)} %copy-done.2) | copy-start | bytes 6291460
  642.4 73.2 %copy-start.38 = (f32[2048]{0:T(1024)S(1)}, f32[2048]{0:T(1024)}, u32[]{:S(2)}) copy-start(f32[2048]{0:T(1024)} %copy-done.37) | copy-start | bytes 24580
  642.4 73.2 %copy-start.42 = (f32[256]{0:T(256)S(1)}, f32[256]{0:T(256)}, u32[]{:S(2)}) copy-start(f32[256]{0:T(256)} %copy-done.41) | copy-start | bytes 3076
  642.4 478.9 %reduce-scatter.15.cloned.1.call-start = ((), (), s32[]{:S(2)}) async-start(), calls=%async_computation.15 | async-start | bytes 9437184 | tf_op jit(solution)/shard_map/reduce_scatter | solution.py:304
  717.6 93.2 %copy-start.9 = (bf16[256,8,4,64]{0,3,2,1:T(8,128)(2,1)S(1)}, bf16[256,8,4,64]{0,3,2,1:T(8,128)(2,1)}, u32[]{:S(2)}) copy-start(bf16[256,8,4,64]{0,3,2,1:T(8,128)(2,1)} %copy.155) | copy-start | bytes 3145732
  824.5 336.2 %reduce-scatter.11.cloned.1.call-start = ((), (), s32[]{:S(2)}) async-start(), calls=%async_computation.13 | async-start | bytes 14745600 | tf_op jit(solution)/shard_map/reduce_scatter | solution.py:358
  928.8 6.0 copy-start.24
  928.9 7.8 collective-permute-start.12
  930.8 18.6 %collective-permute-start.13 = (bf16[2,256,512]{1,2,0:T(8,128)(2,1)S(1)}, bf16[2,256,512]{1,2,0:T(8,128)(2,1)S(1)}, u32[]{:S(2)}, u32[]{:S(2)}) collective-permute-start(bf16[2,256,512]{1,2,0:T(8,128)(2,1)S(1)} %pad_maximum_fusion.19), channel_id=1, source_target_pairs={{8,0},{12,4},{16,8},{20,12},{24,16},{28,20},{9,1},{13,5},{17,9},{2... | collective-permute-start | bytes 1572872 | tf_op jit(solution)/shard_map/ppermute | solution.py:22
  932.2 22.4 %collective-permute-start.14 = (bf16[2,256,512]{1,2,0:T(8,128)(2,1)S(1)}, bf16[2,256,512]{1,2,0:T(8,128)(2,1)S(1)}, u32[]{:S(2)}, u32[]{:S(2)}) collective-permute-start(bf16[2,256,512]{1,2,0:T(8,128)(2,1)S(1)} %pad_maximum_fusion.20), channel_id=1, source_target_pairs={{12,0},{16,4},{20,8},{24,12},{28,16},{13,1},{17,5},{21,9},{25,13},... | collective-permute-start | bytes 1572872 | tf_op jit(solution)/shard_map/ppermute | solution.py:22
  933.5 55.9 %collective-permute-start.15 = (bf16[2,256,512]{1,2,0:T(8,128)(2,1)S(1)}, bf16[2,256,512]{1,2,0:T(8,128)(2,1)S(1)}, u32[]{:S(2)}, u32[]{:S(2)}) collective-permute-start(bf16[2,256,512]{1,2,0:T(8,128)(2,1)S(1)} %pad_maximum_fusion.21), channel_id=1, source_target_pairs={{16,0},{20,4},{24,8},{28,12},{17,1},{21,5},{25,9},{29,13},{18,2},{... | collective-permute-start | bytes 1572872 | tf_op jit(solution)/shard_map/ppermute | solution.py:22
  1020.9 182.6 %reduce-scatter.17.cloned.1.call-start = ((), (), s32[]{:S(2)}) async-start(), calls=%async_computation.16 | async-start | bytes 1310720 | tf_op jit(solution)/shard_map/reduce_scatter | solution.py:303
  1021.1 12.8 %copy-start.44 = (bf16[2048,1024]{1,0:T(8,128)(2,1)S(1)}, bf16[2048,1024]{1,0:T(8,128)(2,1)}, u32[]{:S(2)}) copy-start(bf16[2048,1024]{1,0:T(8,128)(2,1)} %get-tuple-element.339) | copy-start | bytes 12582916
  1059.1 43.9 %collective-permute-start.16 = (bf16[2,1,512,1024]{3,2,1,0:T(8,128)(2,1)S(1)}, bf16[2,1,512,1024]{3,2,1,0:T(8,128)(2,1)}, u32[]{:S(2)}, u32[]{:S(2)}) collective-permute-start(bf16[2,1,512,1024]{3,2,1,0:T(8,128)(2,1)S(1)} %dynamic-slice_convert_fusion.1), channel_id=1, source_target_pairs={{0,1},{1,0},{2,3},{3,2},{4,5},{5,4},{6,7},{7,6},{8,9},{9,8},{10,11... | collective-permute-start | bytes 6291464 | tf_op jit(solution)/shard_map/ppermute | solution.py:127
  1060.7 42.3 %slice-start.2 = ((s8[8388608]{0:T(1024)(128)(4,1)}), s8[4194304]{0:T(1024)(128)(4,1)S(1)}, s32[]{:S(2)}) async-start(s8[8388608]{0:T(1024)(128)(4,1)} %bitcast.336), calls=%async_computation.20 | async-start | bytes 8388608
  1060.7 48.0 %slice-start = ((s8[8388608]{0:T(1024)(128)(4,1)}), s8[4194304]{0:T(1024)(128)(4,1)S(1)}, s32[]{:S(2)}) async-start(s8[8388608]{0:T(1024)(128)(4,1)} %bitcast.332), calls=%async_computation.18 | async-start | bytes 8388608
  1063.4 39.6 %slice-start.3 = ((s8[8388608]{0:T(1024)(128)(4,1)}), s8[4194304]{0:T(1024)(128)(4,1)S(1)}, s32[]{:S(2)}) async-start(s8[8388608]{0:T(1024)(128)(4,1)} %bitcast.336), calls=%async_computation.21 | async-start | bytes 8388608
  1063.4 45.3 %slice-start.1 = ((s8[8388608]{0:T(1024)(128)(4,1)}), s8[4194304]{0:T(1024)(128)(4,1)S(1)}, s32[]{:S(2)}) async-start(s8[8388608]{0:T(1024)(128)(4,1)} %bitcast.332), calls=%async_computation.19 | async-start | bytes 8388608
  1063.4 45.3 %collective-permute-start.18 = (bf16[1,2,512,1024]{3,2,1,0:T(8,128)(2,1)S(1)}, bf16[1,2,512,1024]{3,2,1,0:T(8,128)(2,1)}, u32[]{:S(2)}, u32[]{:S(2)}) collective-permute-start(bf16[1,2,512,1024]{3,2,1,0:T(8,128)(2,1)S(1)} %dynamic-slice_convert_fusion), channel_id=1, source_target_pairs={{0,2},{1,3},{2,0},{3,1},{4,6},{5,7},{6,4},{7,5},{8,10},{9,11},{10,... | collective-permute-start | bytes 6291464 | tf_op jit(solution)/shard_map/ppermute | solution.py:127
  1105.7 5.8 copy-start.10
  1107.0 22.5 %collective-permute-start.17 = (bf16[1,1,512,1024]{3,2,1,0:T(8,128)(2,1)}, bf16[1,1,512,1024]{3,2,1,0:T(8,128)(2,1)}, u32[]{:S(2)}, u32[]{:S(2)}) collective-permute-start(bf16[1,1,512,1024]{3,2,1,0:T(8,128)(2,1)} %dynamic-slice_convert_fusion.5), channel_id=1, source_target_pairs={{0,2},{1,3},{2,0},{3,1},{4,6},{5,7},{6,4},{7,5},{8,10},{9,11},{10,... | collective-permute-start | bytes 3145736 | tf_op jit(solution)/shard_map/ppermute | solution.py:127
  1113.4 26.1 %collective-permute-start.19 = (bf16[1,1,512,1024]{3,2,1,0:T(8,128)(2,1)S(1)}, bf16[1,1,512,1024]{3,2,1,0:T(8,128)(2,1)S(1)}, u32[]{:S(2)}, u32[]{:S(2)}) collective-permute-start(bf16[1,1,512,1024]{3,2,1,0:T(8,128)(2,1)S(1)} %dynamic-slice_convert_fusion.4), channel_id=1, source_target_pairs={{0,1},{1,0},{2,3},{3,2},{4,5},{5,4},{6,7},{7,6},{8,9},{9,8},{10,11... | collective-permute-start | bytes 3145736 | tf_op jit(solution)/shard_map/ppermute | solution.py:127
  1120.6 35.2 %collective-permute-start.20 = (bf16[2,1,128,2048]{3,2,1,0:T(8,128)(2,1)}, bf16[2,1,128,2048]{3,2,1,0:T(8,128)(2,1)}, u32[]{:S(2)}, u32[]{:S(2)}) collective-permute-start(bf16[2,1,128,2048]{3,2,1,0:T(8,128)(2,1)} %dynamic-slice_convert_fusion.3), channel_id=1, source_target_pairs={{0,1},{1,0},{2,3},{3,2},{4,5},{5,4},{6,7},{7,6},{8,9},{9,8},{10,11... | collective-permute-start | bytes 3145736 | tf_op jit(solution)/shard_map/ppermute | solution.py:127
  1121.4 18.1 %copy-start.12 = (f32[1,2,512,1024]{3,2,1,0:T(8,128)S(1)}, f32[1,2,512,1024]{3,2,1,0:T(8,128)}, u32[]{:S(2)}) copy-start(f32[1,2,512,1024]{3,2,1,0:T(8,128)} %copy-done.11) | copy-start | bytes 12582916
  1141.4 54.8 %all-to-all-start.1 = ((bf16[8,2,64,1024]{3,2,1,0:T(8,128)(2,1)}), bf16[8,2,64,1024]{3,2,1,0:T(8,128)(2,1)S(1)}, u32[]{:S(2)}, u32[]{:S(2)}) async-start(bf16[8,2,64,1024]{3,2,1,0:T(8,128)(2,1)} %bitcast.350), calls=%async_computation.7 | async-start | bytes 4194304 | tf_op jit(solution)/shard_map/all_to_all | solution.py:294
  1145.0 86.3 %reduce-scatter.13.cloned.1.call-start = ((), (), s32[]{:S(2)}) async-start(), calls=%async_computation.14 | async-start | bytes 2048000 | tf_op jit(solution)/shard_map/reduce_scatter | solution.py:357
  1147.8 27.3 %collective-permute-start.22 = (bf16[1,2,128,2048]{3,2,1,0:T(8,128)(2,1)}, bf16[1,2,128,2048]{3,2,1,0:T(8,128)(2,1)}, u32[]{:S(2)}, u32[]{:S(2)}) collective-permute-start(bf16[1,2,128,2048]{3,2,1,0:T(8,128)(2,1)} %dynamic-slice_convert_fusion.2), channel_id=1, source_target_pairs={{0,2},{1,3},{2,0},{3,1},{4,6},{5,7},{6,4},{7,5},{8,10},{9,11},{10,... | collective-permute-start | bytes 3145736 | tf_op jit(solution)/shard_map/ppermute | solution.py:127
  1160.1 30.4 %collective-permute-start.21 = (bf16[1,1,128,2048]{3,2,1,0:T(8,128)(2,1)}, bf16[1,1,128,2048]{3,2,1,0:T(8,128)(2,1)}, u32[]{:S(2)}, u32[]{:S(2)}) collective-permute-start(bf16[1,1,128,2048]{3,2,1,0:T(8,128)(2,1)} %dynamic-slice_convert_fusion.7), channel_id=1, source_target_pairs={{0,2},{1,3},{2,0},{3,1},{4,6},{5,7},{6,4},{7,5},{8,10},{9,11},{10,... | collective-permute-start | bytes 1572872 | tf_op jit(solution)/shard_map/ppermute | solution.py:127
  1160.8 29.7 %copy-start.15 = (f32[2,1,128,2048]{3,2,1,0:T(8,128)S(1)}, f32[2,1,128,2048]{3,2,1,0:T(8,128)}, u32[]{:S(2)}) copy-start(f32[2,1,128,2048]{3,2,1,0:T(8,128)} %copy-done.14) | copy-start | bytes 6291460
  1177.5 14.4 %collective-permute-start.23 = (bf16[1,1,128,2048]{3,2,1,0:T(8,128)(2,1)S(1)}, bf16[1,1,128,2048]{3,2,1,0:T(8,128)(2,1)S(1)}, u32[]{:S(2)}, u32[]{:S(2)}) collective-permute-start(bf16[1,1,128,2048]{3,2,1,0:T(8,128)(2,1)S(1)} %dynamic-slice_convert_fusion.6), channel_id=1, source_target_pairs={{0,1},{1,0},{2,3},{3,2},{4,5},{5,4},{6,7},{7,6},{8,9},{9,8},{10,11... | collective-permute-start | bytes 1572872 | tf_op jit(solution)/shard_map/ppermute | solution.py:127
  (21 other events, 34.9 us)
Sparse Core Ops, SparseCore 0:
  13.2 101.2 all-gather.5
  117.4 94.6 all-gather.7
  282.2 163.0 all-gather.9
  446.8 80.1 all-gather.11
  628.4 87.0 reduce-scatter.8
  717.7 87.9 reduce-scatter.6
  824.6 87.9 reduce-scatter.14
  1021.0 133.6 reduce-scatter.10
  1157.5 39.2 reduce-scatter.16
  1199.9 31.3 reduce-scatter.12

commit v2 on v1

v2 whole, which is shorter than its diff:
```python
import functools

import jax
import jax.numpy as jnp
from jax import lax
from jax.experimental import pallas as pl
from jax.experimental.pallas import tpu as pltpu
from jax.sharding import PartitionSpec as P

D = 2048
FF = 8192
HEADS = 32
KV_HEADS = 8
HEAD_DIM = 64
WINDOW = 1024
STRETCH = 256
QTILE = 128
LANES = 128
EPS = 1e-05
THETA = 500000.0


def passed_along(x, axis, by):
    size = lax.axis_size(axis)
    pairs = [(i, i + by) for i in range(size) if 0 <= i + by < size]
    return lax.ppermute(x, axis, pairs)


def product(left, right):
    return jnp.dot(left, right, preferred_element_type=jnp.float32)


def against(left, right):
    return lax.dot_general(
        left, right, (((1,), (1,)), ((), ())), preferred_element_type=jnp.float32
    )


def across(left, right):
    return lax.dot_general(
        left, right, (((0,), (0,)), ((), ())), preferred_element_type=jnp.float32
    )


def doc_segment(doc_lengths, index):
    doc_ends = jnp.cumsum(doc_lengths)
    return jnp.sum((index[:, None] >= doc_ends[None, :]).astype(jnp.int32), axis=1)


def doc_position(doc_lengths, index, segment):
    doc_ends = jnp.cumsum(doc_lengths)
    doc_starts = doc_ends - doc_lengths
    member = segment[:, None] == jnp.arange(doc_lengths.shape[0], dtype=jnp.int32)[None, :]
    return index - jnp.sum(jnp.where(member, doc_starts[None, :], 0), axis=1)


def swap_halves(u):
    half = HEAD_DIM // 2
    width = u.shape[1]
    lane = lax.broadcasted_iota(jnp.int32, u.shape, 1)
    ahead = pltpu.roll(u, width - half, 1)
    behind = pltpu.roll(u, half, 1)
    return jnp.where(lane % HEAD_DIM < half, ahead, behind)


def turn(u, cosine, sine):
    copies = u.shape[1] // cosine.shape[1]
    cosine = jnp.concatenate([cosine] * copies, axis=1)
    sine = jnp.concatenate([sine] * copies, axis=1)
    return u * cosine + swap_halves(u) * sine


def nt(left, right):
    return lax.dot_general(left, right, (((1,), (1,)), ((), ())), preferred_element_type=jnp.float32)


def nn(left, right):
    return lax.dot_general(left, right, (((1,), (0,)), ((), ())), preferred_element_type=jnp.float32)


def attend_forward_kernel(q_ref, k_ref, v_ref, bias_ref, cos_ref, sin_ref, o_ref, qr_ref, lse_ref):
    rows = q_ref.shape[0]
    group = HEADS // KV_HEADS
    span = k_ref.shape[0] - rows + QTILE
    rotated = turn(q_ref[...], cos_ref[...], sin_ref[...])
    qr_ref[...] = rotated.astype(jnp.bfloat16)
    scaled = (qr_ref[...].astype(jnp.float32) * HEAD_DIM ** (-0.5)).astype(jnp.bfloat16)
    for tile in range(rows // QTILE):
        first = tile * QTILE
        bias = bias_ref[first : first + span, first : first + QTILE]
        for kv in range(LANES // HEAD_DIM):
            lo = kv * HEAD_DIM
            keys = k_ref[first : first + span, lo : lo + HEAD_DIM]
            values = v_ref[first : first + span, lo : lo + HEAD_DIM]
            values_t = values.T
            raises, totals = [], []
            for h in range(group):
                head = kv * group + h
                q_h = scaled[first : first + QTILE, head * HEAD_DIM : (head + 1) * HEAD_DIM]
                s = nt(keys, q_h) + bias
                top = jnp.max(s, axis=0, keepdims=True)
                raised = jnp.exp(s - top)
                total = jnp.sum(raised, axis=0, keepdims=True)
                lse_ref[head : head + 1, first : first + QTILE] = top + jnp.log(total)
                raises.append(raised.astype(jnp.bfloat16))
                totals.append(total)
            o_wide = nn(values_t, jnp.concatenate(raises, axis=1)) / jnp.concatenate(totals, axis=1)
            o_t = jnp.concatenate(
                [o_wide[:, h * QTILE : (h + 1) * QTILE] for h in range(group)], axis=0
            )
            o_ref[first : first + QTILE, kv * group * HEAD_DIM : (kv + 1) * group * HEAD_DIM] = (
                o_t.T.astype(jnp.bfloat16)
            )


def attend_forward(q, k, v, bias, cosine, sine):
    rows, width = q.shape
    steps = KV_HEADS * HEAD_DIM // LANES
    qw = width // steps
    heads = HEADS // steps
    window = k.shape[0]
    return pl.pallas_call(
        attend_forward_kernel,
        grid=(steps,),
        in_specs=[
            pl.BlockSpec((rows, qw), lambda i: (0, i)),
            pl.BlockSpec((window, LANES), lambda i: (0, i)),
            pl.BlockSpec((window, LANES), lambda i: (0, i)),
            pl.BlockSpec((window, rows), lambda i: (0, 0)),
            pl.BlockSpec((rows, LANES), lambda i: (0, 0)),
            pl.BlockSpec((rows, LANES), lambda i: (0, 0)),
        ],
        out_specs=[
            pl.BlockSpec((rows, qw), lambda i: (0, i)),
            pl.BlockSpec((rows, qw), lambda i: (0, i)),
            pl.BlockSpec((heads, rows), lambda i: (i, 0)),
        ],
        out_shape=[
            jax.ShapeDtypeStruct((rows, width), jnp.bfloat16),
            jax.ShapeDtypeStruct((rows, width), jnp.bfloat16),
            jax.ShapeDtypeStruct((HEADS, rows), jnp.float32),
        ],
        compiler_params=pltpu.CompilerParams(vmem_limit_bytes=48 * 1024 * 1024),
        cost_estimate=pl.CostEstimate(flops=40_000_000_000, bytes_accessed=10_000_000, transcendentals=0),
    )(q, k, v, bias, cosine, sine)


def attend_backward_kernel(qr_ref, k_ref, v_ref, do_ref, o_ref, lse_ref, bias_ref, cos_ref, sin_ref, dq_ref, dk_ref, dv_ref):
    rows = qr_ref.shape[0]
    group = HEADS // KV_HEADS
    span = k_ref.shape[0] - rows + QTILE
    scale = HEAD_DIM ** (-0.5)
    dk_ref[...] = jnp.zeros_like(dk_ref)
    dv_ref[...] = jnp.zeros_like(dv_ref)
    scaled = (qr_ref[...].astype(jnp.float32) * scale).astype(jnp.bfloat16)
    wide = LANES // HEAD_DIM * group * HEAD_DIM
    owner = lax.broadcasted_iota(jnp.int32, (8, wide), 1) // HEAD_DIM
    pick = (owner == lax.broadcasted_iota(jnp.int32, (8, wide), 0)).astype(jnp.float32)
    for tile in range(rows // QTILE):
        first = tile * QTILE
        bias = bias_ref[first : first + span, first : first + QTILE]
        both = do_ref[first : first + QTILE, :].astype(jnp.float32) * o_ref[
            first : first + QTILE, :
        ].astype(jnp.float32)
        delta = lax.dot_general(
            pick, both, (((1,), (1,)), ((), ())),
            precision=lax.Precision.HIGHEST, preferred_element_type=jnp.float32,
        )
        dk_pair, dv_pair, dqs = [], [], []
        for kv in range(LANES // HEAD_DIM):
            lo = kv * HEAD_DIM
            keys = k_ref[first : first + span, lo : lo + HEAD_DIM]
            values = v_ref[first : first + span, lo : lo + HEAD_DIM]
            keys_t = keys.T
            probs, slopes, qs, dos = [], [], [], []
            for h in range(group):
                head = kv * group + h
                cols = slice(head * HEAD_DIM, (head + 1) * HEAD_DIM)
                q_h = scaled[first : first + QTILE, cols]
                do_h = do_ref[first : first + QTILE, cols]
                s = nt(keys, q_h) + bias
                p = jnp.exp(s - lse_ref[head : head + 1, first : first + QTILE])
                dp = nt(values, do_h)
                ds = (p * (dp - delta[head : head + 1, :])).astype(jnp.bfloat16)
                probs.append(p.astype(jnp.bfloat16))
                slopes.append(ds)
                qs.append(q_h)
                dos.append(do_h)
            p_all = jnp.concatenate(probs, axis=1)
            ds_all = jnp.concatenate(slopes, axis=1)
            dv_pair.append(nn(p_all, jnp.concatenate(dos, axis=0)))
            dk_pair.append(nn(ds_all, jnp.concatenate(qs, axis=0)))
            dq_t = nn(keys_t, ds_all) * scale
            dqs.extend(dq_t[:, h * QTILE : (h + 1) * QTILE] for h in range(group))
        dk_ref[first : first + span, :] += jnp.concatenate(dk_pair, axis=1)
        dv_ref[first : first + span, :] += jnp.concatenate(dv_pair, axis=1)
        dq = jnp.concatenate(dqs, axis=0).T
        dq_ref[first : first + QTILE, :] = turn(
            dq, cos_ref[first : first + QTILE, :], -sin_ref[first : first + QTILE, :]
        ).astype(jnp.bfloat16)


def attend_backward(qr, k, v, do, o, lse, bias, cosine, sine):
    rows, width = qr.shape
    steps = KV_HEADS * HEAD_DIM // LANES
    qw = width // steps
    heads = HEADS // steps
    window = k.shape[0]
    wide = pl.BlockSpec((rows, qw), lambda i: (0, i))
    tall = pl.BlockSpec((window, LANES), lambda i: (0, i))
    table = pl.BlockSpec((rows, LANES), lambda i: (0, 0))
    return pl.pallas_call(
        attend_backward_kernel,
        grid=(steps,),
        in_specs=[
            wide, tall, tall, wide, wide,
            pl.BlockSpec((heads, rows), lambda i: (i, 0)),
            pl.BlockSpec((window, rows), lambda i: (0, 0)),
            table, table,
        ],
        out_specs=[wide, tall, tall],
        out_shape=[
            jax.ShapeDtypeStruct((rows, width), jnp.bfloat16),
            jax.ShapeDtypeStruct(k.shape, jnp.float32),
            jax.ShapeDtypeStruct(k.shape, jnp.float32),
        ],
        compiler_params=pltpu.CompilerParams(vmem_limit_bytes=48 * 1024 * 1024),
        cost_estimate=pl.CostEstimate(flops=80_000_000_000, bytes_accessed=20_000_000, transcendentals=0),
    )(qr, k, v, do, o, lse, bias, cosine, sine)


def turn_tables(position):
    half_dim = HEAD_DIM // 2
    frequency = THETA ** (-2.0 * jnp.arange(half_dim, dtype=jnp.float32) / HEAD_DIM)
    angles = position.astype(jnp.float32)[:, None] * frequency[None, :]
    cosine, sine = jnp.cos(angles), jnp.sin(angles)
    copies = LANES // HEAD_DIM
    return (
        jnp.concatenate([cosine, cosine] * copies, axis=1),
        jnp.concatenate([-sine, sine] * copies, axis=1),
    )


def rope(u, cosine, sine):
    half = HEAD_DIM // 2
    parts = u.reshape(u.shape[0], -1, 2, half)
    swapped_parts = parts[:, :, ::-1, :].reshape(u.shape)
    copies = u.shape[1] // LANES
    return u * jnp.tile(cosine, (1, copies)) + swapped_parts * jnp.tile(sine, (1, copies))


def norm_back(grad_normal, normal, inverse):
    return inverse * (grad_normal - normal * jnp.mean(grad_normal * normal, axis=1, keepdims=True))


def after(x, *others):
    return lax.optimization_barrier((x,) + others)[0]


def peer_of(chip_mask, side_mask, fsdp_mask):
    ctx = lax.axis_index("ctx")
    return (ctx ^ (2 * chip_mask + side_mask), lax.axis_index("fsdp") ^ fsdp_mask)


def greet(peers):
    barrier = pltpu.get_barrier_semaphore()
    for peer in peers:
        pl.semaphore_signal(
            barrier, inc=1, device_id=peer_of(*peer), device_id_type=pl.DeviceIdType.MESH
        )
    pl.semaphore_wait(barrier, len(peers))


def run_copies(copies, send_sems, recv_sems):
    started, arrived = {}, set()

    def arrive(name):
        if name not in arrived:
            arrived.add(name)
            started[name].wait_recv()

    for at, (name, awaited, source, target, peer) in enumerate(copies):
        for other in awaited:
            arrive(other)
        started[name] = pltpu.make_async_remote_copy(
            src_ref=source,
            dst_ref=target,
            send_sem=send_sems.at[at],
            recv_sem=recv_sems.at[at],
            device_id=peer_of(*peer),
            device_id_type=pl.DeviceIdType.MESH,
        )
        started[name].start()
    for name in started:
        arrive(name)
    for name in started:
        started[name].wait_send()


def doubling(name, size, order, awaited, block, target):
    hops, held = [], {0: awaited}
    for mask in order:
        hop, got = [], {}
        for r, needs in held.items():
            key = (name, r, mask)
            hop.append((key, needs, block(r), target(r), (0, 0, mask)))
            got[r ^ mask] = (key,)
        held.update(got)
        hops.append(hop)
    return hops, held


def front_masks(ctx_size, fsdp_size, paired):
    chips = ctx_size // 2
    peers = [
        (m, s, 0)
        for m in range(chips)
        for s in range(2)
        if (m or s) and (paired or not m or not s)
    ]
    return peers + [(0, 0, m) for m in range(1, fsdp_size)]


def front_copies(parts, wholes, pair_ref, pair_all, down_ref, down_all, sizes):
    ctx_size, fsdp_size = sizes
    chips = ctx_size // 2
    ctx, fsdp = lax.axis_index("ctx"), lax.axis_index("fsdp")
    chip, side = ctx // 2, ctx % 2
    masks = [1 << bit for bit in range(fsdp_size.bit_length() - 1)]
    orders = [masks, masks[::-1]]
    copies = []
    for n, (own, whole) in enumerate(zip(parts, wholes)):
        for m in range(1, chips):
            copies.append((("z", n, m), (), own, whole.at[chip, side, fsdp], (m, 0, 0)))
    exchange = []
    if pair_ref is not None:
        ff_own = pair_ref.shape[2] // ctx_size
        for m in range(chips):
            for s in range(2):
                if m or s:
                    other = ctx ^ (2 * m + s)
                    columns = pl.ds(pl.multiple_of(other * ff_own, ff_own), ff_own)
                    exchange.append(
                        (
                            ("pair", m, s), (), pair_ref.at[:, :, columns],
                            pair_all.at[:, ctx, fsdp], (m, s, 0),
                        )
                    )
    queues = []
    if down_ref is not None:
        width = down_ref.shape[1] // 2
        lists = []
        for h, order in enumerate(orders):
            cols = pl.ds(h * width, width)
            target = lambda r, cols=cols: down_all.at[fsdp ^ r, :, cols]
            block = lambda r, cols=cols: (
                down_all.at[fsdp ^ r, :, cols] if r else down_ref.at[:, cols]
            )
            lists.append(doubling(("down", h), fsdp_size, order, (), block, target)[0])
        stages = [[copy for pieces in zip(*hop) for copy in pieces] for hop in zip(*lists)]
        queues.append(stages + [[]])
    for n, (own, whole) in enumerate(zip(parts, wholes)):
        width = own.shape[1]
        cut = (width // 2 + LANES - 1) // LANES * LANES
        halves = [(0, cut), (cut, width - cut)]
        for m in range(chips):
            first = (("z", n, m),) if m else ()
            lists, last = [], []
            for h, ((lo, span), order) in enumerate(zip(halves, orders)):
                cols = pl.ds(lo, span)

                def block(r, m=m, cols=cols, own=own, whole=whole):
                    if m == 0 and r == 0:
                        return own.at[:, cols]
                    return whole.at[chip ^ m, side, fsdp ^ r, :, cols]

                def target(r, m=m, cols=cols, whole=whole):
                    return whole.at[chip ^ m, side, fsdp ^ r, :, cols]

                hops, held = doubling(("f", n, m, h), fsdp_size, order, first, block, target)
                lists.append(hops)
                last.extend(key for keys in held.values() for key in keys)
            stages = [[copy for pieces in zip(*hop) for copy in pieces] for hop in zip(*lists)]
            row = whole.at[chip ^ m, side]
            if m:
                stages.append([(("core", n, m), tuple(last), row, row, (0, 1, 0))])
            else:
                stages.append(
                    [
                        (
                            ("core", n, m, r), tuple(last),
                            row.at[fsdp ^ r] if r else own, row.at[fsdp ^ r], (0, 1, 0),
                        )
                        for r in range(fsdp_size)
                    ]
                )
            queues.append(stages)
    sharing = []
    lag = 2
    for turn in range(len(queues) + lag * (len(orders[0]) + 1)):
        for stage in range(len(orders[0]) + 1):
            at = turn - lag * stage
            if 0 <= at < len(queues):
                sharing.extend(queues[at][stage])
        if turn == chips:
            sharing.extend(exchange)
    return copies + sharing


def front_kernel(sizes, count, paired, *refs):
    parts, refs = refs[:count], refs[count:]
    pair_ref, down_ref, refs = (refs[0], refs[1], refs[3:]) if paired else (None, None, refs)
    wholes, refs = refs[:count], refs[count:]
    pair_all, down_all, refs = (refs[0], refs[1], refs[2:]) if paired else (None, None, refs)
    send_sems, recv_sems, own_sems = refs
    greet(front_masks(*sizes, paired))
    ctx, fsdp = lax.axis_index("ctx"), lax.axis_index("fsdp")
    kept = []
    for n, (own, whole) in enumerate(zip(parts, wholes)):
        kept.append(
            pltpu.make_async_copy(own, whole.at[ctx // 2, ctx % 2, fsdp], own_sems.at[n])
        )
    if paired:
        ff_own = pair_ref.shape[2] // sizes[0]
        columns = pl.ds(pl.multiple_of(ctx * ff_own, ff_own), ff_own)
        kept.append(
            pltpu.make_async_copy(
                pair_ref.at[:, :, columns], pair_all.at[:, ctx, fsdp], own_sems.at[count]
            )
        )
        kept.append(
            pltpu.make_async_copy(down_ref, down_all.at[fsdp], own_sems.at[count + 1])
        )
    for copy in kept:
        copy.start()
    copies = front_copies(parts, wholes, pair_ref, pair_all, down_ref, down_all, sizes)
    run_copies(copies, send_sems, recv_sems)
    for copy in kept:
        copy.wait()


def gather_front(parts, pair, down, earlier, sizes, collective_id):
    ctx_size, fsdp_size = sizes
    chips = ctx_size // 2
    rows = parts[0].shape[0]
    paired = pair is not None
    count = len(parts) * (chips - 1 + chips * (2 * (fsdp_size - 1) + 1) + fsdp_size - 1)
    shapes = [
        jax.ShapeDtypeStruct((chips, 2, fsdp_size, rows, part.shape[1]), part.dtype)
        for part in parts
    ]
    if paired:
        count += ctx_size - 1 + 2 * (fsdp_size - 1)
        shapes.append(
            jax.ShapeDtypeStruct(
                (2, ctx_size, fsdp_size, rows, pair.shape[2] // ctx_size), pair.dtype
            )
        )
        shapes.append(jax.ShapeDtypeStruct((fsdp_size,) + down.shape, down.dtype))
    hbm = pl.BlockSpec(memory_space=pl.ANY)
    vmem = pl.BlockSpec(memory_space=pltpu.VMEM)
    return pl.pallas_call(
        functools.partial(front_kernel, sizes, len(parts), paired),
        in_specs=[vmem] * len(shapes) + ([hbm] if paired else []),
        out_specs=[hbm] * len(shapes),
        out_shape=shapes,
        scratch_shapes=[
            pltpu.SemaphoreType.DMA((count,)),
            pltpu.SemaphoreType.DMA((count,)),
            pltpu.SemaphoreType.DMA((len(shapes),)),
        ],
        compiler_params=pltpu.CompilerParams(collective_id=collective_id, has_side_effects=True),
        cost_estimate=pl.CostEstimate(flops=90_000_000_000, bytes_accessed=30_000_000, transcendentals=0),
    )(*parts, *([pair, down, earlier] if paired else []))


def hidden_kernel(sizes, pair_in, pair_all, send_sems, recv_sems):
    ctx_size, fsdp_size = sizes
    fsdp = lax.axis_index("fsdp")
    masks = [1 << bit for bit in range(fsdp_size.bit_length() - 1)]
    greet([(0, 0, m) for m in masks])
    lists = []
    for h, order in enumerate([masks, masks[::-1]]):
        view = lambda r, h=h: pair_all.at[h, :, fsdp ^ r]
        lists.append(doubling(("pair", h), fsdp_size, order, (), view, view)[0])
    copies = []
    for hop in zip(*lists):
        for pieces in zip(*hop):
            copies.extend(pieces)
    run_copies(copies, send_sems, recv_sems)


def gather_hidden(pair_all, sizes):
    count = 2 * (sizes[1] - 1)
    hbm = pl.BlockSpec(memory_space=pl.ANY)
    return pl.pallas_call(
        functools.partial(hidden_kernel, sizes),
        in_specs=[hbm],
        out_specs=hbm,
        out_shape=jax.ShapeDtypeStruct(pair_all.shape, pair_all.dtype),
        input_output_aliases={0: 0},
        scratch_shapes=[pltpu.SemaphoreType.DMA((count,)), pltpu.SemaphoreType.DMA((count,))],
        compiler_params=pltpu.CompilerParams(collective_id=2, has_side_effects=True),
        cost_estimate=pl.CostEstimate(flops=60_000_000_000, bytes_accessed=30_000_000, transcendentals=0),
    )(pair_all)


def hop_slots(size, order):
    slots, held = [], list(range(size))
    for mask in order:
        held = [r for r in held if not r & mask]
        slots.append(held)
    return slots


def remote(source, target, send_sem, recv_sem, peer):
    return pltpu.make_async_remote_copy(
        src_ref=source,
        dst_ref=target,
        send_sem=send_sem,
        recv_sem=recv_sem,
        device_id=peer_of(*peer),
        device_id_type=pl.DeviceIdType.MESH,
    )


def reduce_kernel(
    sizes, chunk, products, extras, lefts, right, extra, total, terms, core_got, line_sent, line_got,
    core_send, core_recv, hop_send, hop_recv, line_send, line_recv, *hop_buffers
):
    ctx_size, fsdp_size = sizes
    chips = ctx_size // 2
    rows = total.shape[0]
    count = products + extras
    half = chunk // 2
    masks = [1 << bit for bit in range(fsdp_size.bit_length() - 1)]
    orders = [masks, masks[::-1]]
    bits = len(masks)
    hops = [
        [hop_buffers[(h * bits + j) * 2 : (h * bits + j) * 2 + 2] for j in range(bits)]
        for h in range(2)
    ]
    slots = [hop_slots(fsdp_size, order) for order in orders]
    ctx, fsdp = lax.axis_index("ctx"), lax.axis_index("fsdp")
    chip, side = ctx // 2, ctx % 2
    greet(
        [(0, 1, 0)] + [(0, 0, m) for m in masks] + [(m, 0, 0) for m in range(1, chips)]
    )

    def core_copy(i):
        return remote(
            terms.at[i, :, 1 - side], core_got.at[i], core_send.at[i], core_recv.at[i], (0, 1, 0)
        )

    def hop_copy(h, j, i):
        sent, got = hops[h][j]
        return remote(
            sent.at[i], got.at[i], hop_send.at[h, j, i], hop_recv.at[h, j, i], (0, 0, orders[h][j])
        )

    def line_copy(m, i):
        return remote(
            line_sent.at[i, m - 1], line_got.at[i, m - 1],
            line_send.at[i, m - 1], line_recv.at[i, m - 1], (m, 0, 0),
        )

    def held(h, upto, i, z, r):
        cols = pl.ds(h * half, half)
        value = terms[i, z, side, fsdp ^ r, :, cols].astype(jnp.float32)
        value += core_got[i, z, fsdp ^ r, :, cols].astype(jnp.float32)
        for j in range(upto):
            value += hops[h][j][1][i, slots[h][j].index(r), z].astype(jnp.float32)
        return value

    def step(t, carry):
        @pl.when(t < products)
        def _():
            per_left = products // lefts.shape[0]
            cols = pl.ds(pl.multiple_of(t * chunk, chunk), chunk)
            term = jnp.dot(
                lefts[t // per_left], right[:, cols], preferred_element_type=jnp.float32
            )
            terms[t] = term.astype(jnp.bfloat16).reshape(terms.shape[1:])

        if extras:
            @pl.when((t >= products) & (t < count))
            def _():
                terms[t] = extra[t - products].reshape(terms.shape[1:])

        @pl.when(t < count)
        def _():
            core_copy(t).start()

        for j in range(bits):
            @pl.when((t >= j + 1) & (t < count + j + 1))
            def _(j=j):
                i = t - (j + 1)
                if j == 0:
                    core_copy(i).wait_recv()
                for h in range(2):
                    if j:
                        hop_copy(h, j - 1, i).wait_recv()
                    for s, r in enumerate(slots[h][j]):
                        for z in range(chips):
                            hops[h][j][0][i, s, z] = held(h, j, i, z, r | orders[h][j]).astype(
                                jnp.bfloat16
                            )
                    hop_copy(h, j, i).start()

        @pl.when((t >= bits + 1) & (t < count + bits + 1))
        def _():
            i = t - (bits + 1)
            for h in range(2):
                hop_copy(h, bits - 1, i).wait_recv()
                for m in range(1, chips):
                    line_sent[i, m - 1, :, h * half : (h + 1) * half] = held(
                        h, bits, i, chip ^ m, 0
                    ).astype(jnp.bfloat16)
            for m in range(1, chips):
                line_copy(m, i).start()

        @pl.when(t >= bits + 2)
        def _():
            i = t - (bits + 2)
            for m in range(1, chips):
                line_copy(m, i).wait_recv()
            for h in range(2):
                value = held(h, bits, i, chip, 0)
                for m in range(1, chips):
                    value += line_got[i, m - 1, :, h * half : (h + 1) * half].astype(jnp.float32)
                total[:, pl.ds(pl.multiple_of(i * chunk + h * half, half), half)] = value

        return carry

    lax.fori_loop(0, count + bits + 2, step, 0)

    def finish(i, carry):
        core_copy(i).wait_send()
        for h in range(2):
            for j in range(bits):
                hop_copy(h, j, i).wait_send()
        for m in range(1, chips):
            line_copy(m, i).wait_send()
        return carry

    lax.fori_loop(0, count, finish, 0)


def reduce_rows(lefts, right, extra, chunk, sizes, collective_id):
    ctx_size, fsdp_size = sizes
    chips = ctx_size // 2
    depth = lefts.shape[1]
    rows = depth // (ctx_size * fsdp_size)
    products = right.shape[1] // chunk
    extras = 0 if extra is None else extra.shape[0]
    if extra is None:
        extra = jnp.zeros((1, 16, LANES), jnp.bfloat16)
    count = products + extras
    bits = fsdp_size.bit_length() - 1
    half = chunk // 2
    buffers = []
    for _ in range(2):
        for j in range(bits):
            shape = (count, fsdp_size >> (j + 1), chips, rows, half)
            buffers += [pltpu.VMEM(shape, jnp.bfloat16)] * 2
    line = pltpu.VMEM((count, max(chips - 1, 1), rows, chunk), jnp.bfloat16)
    vmem = pl.BlockSpec(memory_space=pltpu.VMEM)
    return pl.pallas_call(
        functools.partial(reduce_kernel, sizes, chunk, products, extras),
        in_specs=[vmem] * 3,
        out_specs=vmem,
        out_shape=jax.ShapeDtypeStruct((rows, count * chunk), jnp.float32),
        scratch_shapes=[
            pltpu.VMEM((count, chips, 2, fsdp_size, rows, chunk), jnp.bfloat16),
            pltpu.VMEM((count, chips, fsdp_size, rows, chunk), jnp.bfloat16),
            line,
            line,
            pltpu.SemaphoreType.DMA((count,)),
            pltpu.SemaphoreType.DMA((count,)),
            pltpu.SemaphoreType.DMA((2, bits, count)),
            pltpu.SemaphoreType.DMA((2, bits, count)),
            pltpu.SemaphoreType.DMA((count, max(chips - 1, 1))),
            pltpu.SemaphoreType.DMA((count, max(chips - 1, 1))),
        ]
        + buffers,
        compiler_params=pltpu.CompilerParams(
            collective_id=collective_id, has_side_effects=True, vmem_limit_bytes=56 * 1024 * 1024
        ),
        cost_estimate=pl.CostEstimate(flops=80_000_000_000, bytes_accessed=30_000_000, transcendentals=0),
    )(lefts, right, extra)


def hidden_grad_kernel(
    sizes, normed, gate, up, pair_sum, terms, pair_sent, pair_got, pair_send, pair_recv
):
    ctx_size, fsdp_size = sizes
    count, span = terms.shape[1], normed.shape[1] // terms.shape[1]
    masks = [1 << bit for bit in range(fsdp_size.bit_length() - 1)]
    orders = [masks, masks[::-1]]
    bits = len(masks)
    slots = [hop_slots(fsdp_size, order) for order in orders]
    fsdp = lax.axis_index("fsdp")
    greet([(0, 0, m) for m in masks])
    first = [sum(fsdp_size >> (k + 1) for k in range(j)) for j in range(bits)]

    def pair_copy(h, j, i):
        rows = pl.ds(first[j], fsdp_size >> (j + 1))
        return remote(
            pair_sent.at[h, i, rows], pair_got.at[h, i, rows],
            pair_send.at[h, j, i], pair_recv.at[h, j, i], (0, 0, orders[h][j]),
        )

    def pair_held(h, upto, i, r):
        value = terms[h, i, fsdp ^ r].astype(jnp.float32)
        for j in range(upto):
            value += pair_got[h, i, first[j] + slots[h][j].index(r)].astype(jnp.float32)
        return value

    def step(t, carry):
        @pl.when(t < count)
        def _():
            columns = normed[:, pl.ds(pl.multiple_of(t * span, span), span)]
            for h, grad in enumerate((gate, up)):
                term = across(columns, grad[...])
                terms[h, t] = term.astype(jnp.bfloat16).reshape(terms.shape[2:])

        for j in range(bits):
            @pl.when((t >= j) & (t < count + j))
            def _(j=j):
                i = t - j
                for h in range(2):
                    if j:
                        pair_copy(h, j - 1, i).wait_recv()
                    for s, r in enumerate(slots[h][j]):
                        pair_sent[h, i, first[j] + s] = pair_held(
                            h, j, i, r | orders[h][j]
                        ).astype(jnp.bfloat16)
                    pair_copy(h, j, i).start()

        @pl.when(t >= bits)
        def _():
            i = t - bits
            for h in range(2):
                pair_copy(h, bits - 1, i).wait_recv()
                pair_sum[i, h] = pair_held(h, bits, i, 0).astype(jnp.bfloat16)

        return carry

    lax.fori_loop(0, count + bits, step, 0)

    def finish(i, carry):
        for h in range(2):
            for j in range(bits):
                pair_copy(h, j, i).wait_send()
        return carry

    lax.fori_loop(0, count, finish, 0)


def reduce_hidden(normed, gate, up, sizes):
    ctx_size, fsdp_size = sizes
    bits = fsdp_size.bit_length() - 1
    rows, columns = normed.shape[1] // (ctx_size * fsdp_size), gate.shape[1]
    pair = pltpu.VMEM((2, ctx_size, fsdp_size - 1, rows, columns), jnp.bfloat16)
    vmem = pl.BlockSpec(memory_space=pltpu.VMEM)
    return pl.pallas_call(
        functools.partial(hidden_grad_kernel, sizes),
        in_specs=[vmem] * 3,
        out_specs=vmem,
        out_shape=jax.ShapeDtypeStruct((ctx_size, 2, rows, columns), jnp.bfloat16),
        scratch_shapes=[
            pltpu.VMEM((2, ctx_size, fsdp_size, rows, columns), jnp.bfloat16), pair, pair,
        ]
        + [pltpu.SemaphoreType.DMA((2, bits, ctx_size))] * 2,
        compiler_params=pltpu.CompilerParams(
            collective_id=3, has_side_effects=True, vmem_limit_bytes=60 * 1024 * 1024
        ),
        cost_estimate=pl.CostEstimate(flops=60_000_000_000, bytes_accessed=30_000_000, transcendentals=0),
    )(normed, gate, up)


def local(
    tokens,
    cotangent,
    lengths,
    attn_gain,
    query_weight,
    key_weight,
    value_weight,
    out_weight,
    mlp_gain,
    gate_weight,
    up_weight,
    down_weight,
):
    both = ("ctx", "fsdp")
    ctx_size = lax.axis_size("ctx")
    fsdp_size = lax.axis_size("fsdp")
    chips = ctx_size // 2
    stream = tokens[0].astype(jnp.float32)
    tok_rows = stream.shape[0]
    own_rows = query_weight.shape[0]
    kv_width = KV_HEADS * HEAD_DIM
    ff_own = FF // ctx_size
    reach_blocks = WINDOW // STRETCH
    ctx_place = lax.axis_index("ctx")
    doc_lengths = lengths[0]
    query_index = ctx_place * tok_rows + jnp.arange(tok_rows, dtype=jnp.int32)
    key_index = (ctx_place - reach_blocks) * tok_rows + jnp.arange(
        (reach_blocks + 1) * tok_rows, dtype=jnp.int32
    )
    query_doc = doc_segment(doc_lengths, query_index)
    key_doc = doc_segment(doc_lengths, key_index)
    position = doc_position(doc_lengths, query_index, query_doc)
    visible = (key_index[:, None] >= 0) & (key_index[:, None] <= query_index[None, :])
    visible = (
        visible
        & (query_index[None, :] - key_index[:, None] < WINDOW)
        & (query_doc[None, :] == key_doc[:, None])
    )
    bias = jnp.where(visible, 0.0, -1e30).astype(jnp.float32)
    cosine, sine = turn_tables(position)

    cot_all = lax.all_gather(cotangent[0], "ctx", axis=0, tiled=True)

    sizes = (ctx_size, fsdp_size)
    gains = jnp.zeros((own_rows, LANES), jnp.bfloat16)
    gains = gains.at[:, 0].set(attn_gain).at[:, 1].set(mlp_gain)
    (kv_all,) = gather_front(
        (jnp.concatenate([key_weight, value_weight, gains], axis=1),), None, None, None, sizes, 1
    )
    kv_all = kv_all.reshape(D, -1)
    gain_one = kv_all[:, 2 * kv_width].astype(jnp.float32)
    gain_two = kv_all[:, 2 * kv_width + 1].astype(jnp.float32)

    inv_one = lax.rsqrt(jnp.mean(stream * stream, axis=1, keepdims=True) + EPS)
    normal_one = stream * inv_one
    normed_one = (normal_one * gain_one).astype(jnp.bfloat16)
    kv_front = product(normed_one, kv_all)
    key_low = rope(kv_front[:, :kv_width], cosine, sine).astype(jnp.bfloat16)
    value_low = kv_front[:, kv_width : 2 * kv_width].astype(jnp.bfloat16)
    own_pair = jnp.concatenate([key_low, value_low], axis=1)
    query_all, out_all, pair_all, down_own = gather_front(
        (after(query_weight, own_pair), out_weight),
        jnp.stack([gate_weight, up_weight]),
        down_weight, cot_all, sizes, 6,
    )
    down_own = down_own.reshape(ff_own, D)
    query_all = query_all.reshape(D, D)
    out_all = out_all.reshape(D, D)
    blocks = [own_pair]
    for step in range(1, reach_blocks + 1):
        blocks.insert(0, passed_along(own_pair, "ctx", step))
    window = jnp.concatenate(blocks, axis=0)
    key_window, value_window = window[:, :kv_width], window[:, kv_width:]
    query_front = product(normed_one, query_all)
    attn_mix, query_low, log_total = attend_forward(
        query_front, key_window, value_window, bias, cosine, sine
    )
    resid = stream + product(attn_mix, out_all)
    inv_two = lax.rsqrt(jnp.mean(resid * resid, axis=1, keepdims=True) + EPS)
    normal_two = resid * inv_two
    normed_two = (normal_two * gain_two).astype(jnp.bfloat16)

    normed_all = lax.all_gather(normed_two, "ctx", axis=0, tiled=True)
    pair = gather_hidden(after(pair_all, normed_two), sizes)
    pair = pair.reshape(2, D, ff_own)
    gate_own, up_own = pair[0], pair[1]
    gate_sum = product(normed_all, gate_own)
    up_sum = product(normed_all, up_own)
    sigmoid_gate = jax.nn.sigmoid(gate_sum)
    silu_gate = gate_sum * sigmoid_gate
    hidden = (silu_gate * up_sum).astype(jnp.bfloat16)
    down_part = product(hidden, down_own).astype(jnp.bfloat16)
    grad_hidden = against(cot_all, down_own)
    grad_gate_low = (
        grad_hidden * up_sum * sigmoid_gate * (1.0 + gate_sum * (1.0 - sigmoid_gate))
    ).astype(jnp.bfloat16)
    grad_up_low = (grad_hidden * silu_gate).astype(jnp.bfloat16)
    columns_part = against(grad_gate_low, gate_own) + against(grad_up_low, up_own)
    half = D // 2
    first_sum = lax.psum_scatter(
        down_part[:, :half], "ctx", scatter_dimension=0, tiled=True
    )
    columns = lax.psum_scatter(
        after(columns_part.astype(jnp.bfloat16), first_sum), "ctx", scatter_dimension=0, tiled=True
    )
    down_terms = across(hidden, cot_all).astype(jnp.bfloat16)
    pair_sum = reduce_hidden(
        normed_all, after(grad_gate_low, down_terms), grad_up_low, sizes
    )
    grad_down = lax.psum_scatter(
        after(down_terms, columns, pair_sum), "fsdp", scatter_dimension=0, tiled=True
    )
    second_sum = lax.psum_scatter(
        after(down_part[:, half:], grad_down), "ctx", scatter_dimension=0, tiled=True
    )
    down_sum = jnp.concatenate([first_sum, second_sum], axis=1)
    columns = columns.astype(jnp.float32)
    mixed = (resid + down_sum.astype(jnp.float32)).astype(jnp.bfloat16)

    pair_sum = lax.all_to_all(pair_sum, "ctx", split_axis=0, concat_axis=0, tiled=True)
    grad_stream = cotangent[0].astype(jnp.float32)
    mlp_gain_local = jnp.sum(columns * normal_two, axis=0)
    grad_resid = grad_stream + norm_back(columns * gain_two, normal_two, inv_two)
    grad_resid_low = grad_resid.astype(jnp.bfloat16)
    grad_mix_low = against(grad_resid_low, out_all).astype(jnp.bfloat16)
    grad_query_low, grad_key_window, grad_value_window = attend_backward(
        query_low, key_window, value_window, grad_mix_low, attn_mix, log_total, bias, cosine, sine
    )
    wide_grad = reduce_rows(
        jnp.stack([normed_one.T, attn_mix.T]),
        after(jnp.concatenate([grad_query_low, grad_resid_low], axis=1), second_sum),
        None, 512, sizes, 4,
    )
    own_start = reach_blocks * tok_rows
    grad_pair = jnp.concatenate([grad_key_window, grad_value_window], axis=1)
    grad_pair_total = after(grad_pair[own_start:], wide_grad)
    grad_pair_low = grad_pair[:own_start].astype(jnp.bfloat16)
    for step in range(1, reach_blocks + 1):
        first_row = (reach_blocks - step) * tok_rows
        later = passed_along(grad_pair_low[first_row : first_row + tok_rows], "ctx", -step)
        grad_pair_total = grad_pair_total + later.astype(jnp.float32)
    grad_key_low = rope(grad_pair_total[:, :kv_width], cosine, -sine).astype(jnp.bfloat16)
    grad_value_low = grad_pair_total[:, kv_width:].astype(jnp.bfloat16)
    kv_low = jnp.concatenate([grad_key_low, grad_value_low], axis=1)
    grad_normed_one = against(grad_query_low, query_all) + against(
        jnp.pad(kv_low, ((0, 0), (0, LANES))), kv_all
    )
    attn_gain_local = jnp.sum(grad_normed_one * normal_one, axis=0)
    gain_terms = jnp.stack([attn_gain_local, mlp_gain_local], axis=1).astype(jnp.bfloat16)
    gain_terms = jnp.pad(gain_terms, ((0, 0), (0, 2 * LANES - 2)))[None]
    kv_grad = reduce_rows(normed_one.T[None], kv_low, gain_terms, 2 * LANES, sizes, 5)
    pair_sum = after(pair_sum, kv_grad)
    pair_sum = pair_sum.transpose(1, 2, 0, 3).reshape(2, own_rows, FF).astype(jnp.float32)
    grad_input = grad_resid + norm_back(grad_normed_one * gain_one, normal_one, inv_one)
    return (
        mixed[None],
        grad_input.astype(jnp.bfloat16)[None],
        kv_grad[:, 2 * kv_width],
        wide_grad[:, :D],
        kv_grad[:, :kv_width],
        kv_grad[:, kv_width : 2 * kv_width],
        wide_grad[:, D:],
        kv_grad[:, 2 * kv_width + 1],
        pair_sum[0],
        pair_sum[1],
        grad_down.astype(jnp.float32),
    )


def solution(mesh):
    in_specs = (
        P("fsdp", "ctx", None),
        P("fsdp", "ctx", None),
        P("fsdp", None),
        P(("ctx", "fsdp")),
        P(("ctx", "fsdp"), None),
        P(("ctx", "fsdp"), None),
        P(("ctx", "fsdp"), None),
        P(("ctx", "fsdp"), None),
        P(("ctx", "fsdp")),
        P(("ctx", "fsdp"), None),
        P(("ctx", "fsdp"), None),
        P(("ctx", "fsdp"), None),
    )
    out_specs = (
        P("fsdp", "ctx", None),
        P("fsdp", "ctx", None),
        P(("ctx", "fsdp")),
        P(("ctx", "fsdp"), None),
        P(("ctx", "fsdp"), None),
        P(("ctx", "fsdp"), None),
        P(("ctx", "fsdp"), None),
        P(("ctx", "fsdp")),
        P(("ctx", "fsdp"), None),
        P(("ctx", "fsdp"), None),
        P(("ctx", "fsdp"), None),
    )
    return jax.shard_map(local, mesh=mesh, in_specs=in_specs, out_specs=out_specs, check_vma=False)
```

time: 1250 us -> 904 us (0.72)
  waiting for transfers between devices: 626 us -> 90 us
  Pallas kernels: 0 us -> 524 us
  matrix products: 303 us -> 139 us
  other arithmetic: 97.1 us -> 36.3 us
  starting transfers between devices: 81.7 us -> 25.1 us
  local copies, waits for them, and re-layouts: 120 us -> 67.7 us
    pallas_call x0 -> x8, Pallas kernels: none -> 524 us  [the longest x2 177 us: gather_front(): pl.pallas_call(functools.partial(front_kernel, sizes, len(parts), paired)...]
    ppermute x16 -> x0, waiting for transfers between devices: 154 us -> none  [swapped(): return lax.ppermute(x, axis, [(i, i ^ mask) for i in range(size)])]
    reduce_scatter x6 -> x4, waiting for transfers between devices: 187 us -> 42.8 us  [the longest x1 24.2 us: local(): lax.psum_scatter(after(down_terms, columns, pair_sum), 'fsdp', scatter_di...]
    all_to_all x1 -> x0, waiting for transfers between devices: 101 us -> none  [local(): lax.all_to_all(pair.transpose(2, 0, 1, 3), 'ctx', split_axis=0, concat_ax...]
    all_gather x2 -> x0, waiting for transfers between devices: 95.9 us -> none  [the longest x1 95.9 us: local(): lax.all_gather(jnp.concatenate([query_weight, key_weight, value_weight, g...]
    dot_general x21 -> x1, matrix products: 81.4 us -> 14.5 us  [across(): lax.dot_general(left, right, (((0,), (0,)), ((), ())), preferred_element_...]
    dot_general x29 -> x6, matrix products: 126 us -> 71.7 us  [against(): lax.dot_general(left, right, (((1,), (1,)), ((), ())), preferred_element_...]
    dot_general x21 -> x6, matrix products: 96.1 us -> 53.2 us  [product(): return jnp.dot(left, right, preferred_element_type=jnp.float32)]
  transfers between devices with their start and end apart: 36 -> 15, of which waited for: 24 -> 6; matrix products, arithmetic and copies ran while one was open for 34% -> 16% of each run, Pallas kernels for 0% -> 41%
where the time goes in v2:
time: 904 us; the launch traced here: 898 us
  Pallas kernels  524 us (58%)
  matrix products  139 us (15%)
  waiting for transfers between devices  90 us (10%)
  local copies, waits for them, and re-layouts  67.7 us (7%)
  other arithmetic  36.3 us (4%)
  starting transfers between devices  25.1 us (3%)
  between operations  15.4 us (2%)
    pallas_call x2, Pallas kernels, gather_front(): pl.pallas_call(functools.partial(front_kernel, sizes, len(parts), paired)...  177 us
    pallas_call x2, Pallas kernels, reduce_rows(): pl.pallas_call(functools.partial(reduce_kernel, sizes, chunk, products, e...  147 us
    pallas_call x1, Pallas kernels, reduce_hidden(): pl.pallas_call(functools.partial(hidden_grad_kernel, sizes), in_specs=[vm...  79.8 us
    dot_general x6, matrix products, against(): lax.dot_general(left, right, (((1,), (1,)), ((), ())), preferred_element_...  71.7 us
    pallas_call x1, Pallas kernels, gather_hidden(): pl.pallas_call(functools.partial(hidden_kernel, sizes), in_specs=[hbm], o...  71 us
    dot_general x6, matrix products, product(): return jnp.dot(left, right, preferred_element_type=jnp.float32)  53.2 us
    ppermute x8, waiting for transfers between devices, passed_along(): return lax.ppermute(x, axis, pairs)  42.7 us
    pallas_call x1, Pallas kernels, attend_backward(): pl.pallas_call(attend_backward_kernel, grid=(steps,), in_specs=[wide, tal...  30 us
  transfers between devices with their start and end apart: 15, of which 6 were waited for; matrix products, arithmetic and copies ran while one was open for 16% of the time, Pallas kernels for 41%

profile of v2, /device:TPU:0, one launch (start us, length us, event | category | flops | bytes accessed | tf_op | source)
XLA Modules:
  0.0 898.4 jit_solution(10822225168262002667)
XLA Ops:
  9.3 1.5 copy.120
  13.2 39.7 %shard_map.203 = bf16[4,2,4,64,1152]{4,3,2,1,0:T(8,128)(2,1)} custom-call(bf16[64,1152]{1,0:T(8,128)(2,1)} %pad_maximum_fusion.5.refs_0_), custom_call_target="tpu_custom_call" | custom-call | flops 89999998976 | bytes 30000000 | tf_op jit(solution)/shard_map/pallas_call | solution.py:462
  52.9 1.5 slice_convert_fusion.1
  55.1 4.0 fusion.42
  64.7 8.7 collective-permute-start
  73.4 2.1 collective-permute-start.1
  75.5 2.5 collective-permute-start.2
  78.0 1.9 collective-permute-start.3
  80.0 3.1 pad_maximum_fusion.refs_2_
  83.0 1.9 fusion.30.bias_ref
  85.3 10.8 %collective-permute-done = bf16[256,1024]{1,0:T(8,128)(2,1)} collective-permute-done((bf16[256,1024]{1,0:T(8,128)(2,1)S(1)}, bf16[256,1024]{1,0:T(8,128)(2,1)}, u32[]{:S(2)}, u32[]{:S(2)}) %collective-permute-start) | collective-permute-done | bytes 524320 | tf_op jit(solution)/shard_map/ppermute | solution.py:26
  97.2 21.4 %collective-permute-done.1 = bf16[256,1024]{1,0:T(8,128)(2,1)} collective-permute-done((bf16[256,1024]{1,0:T(8,128)(2,1)S(1)}, bf16[256,1024]{1,0:T(8,128)(2,1)}, u32[]{:S(2)}, u32[]{:S(2)}) %collective-permute-start.1) | collective-permute-done | bytes 524320 | tf_op jit(solution)/shard_map/ppermute | solution.py:26
  119.6 10.5 %collective-permute-done.2 = bf16[256,1024]{1,0:T(8,128)(2,1)} collective-permute-done((bf16[256,1024]{1,0:T(8,128)(2,1)S(1)}, bf16[256,1024]{1,0:T(8,128)(2,1)}, u32[]{:S(2)}, u32[]{:S(2)}) %collective-permute-start.2) | collective-permute-done | bytes 524320 | tf_op jit(solution)/shard_map/ppermute | solution.py:26
  131.6 137.2 %shard_map.204 = (bf16[4,2,4,64,2048]{4,3,2,1,0:T(8,128)(2,1)}, bf16[4,2,4,64,2048]{4,3,2,1,0:T(8,128)(2,1)}, bf16[2,8,4,64,1024]{4,3,2,1,0:T(8,128)(2,1)}, bf16[4,256,2048]{2,1,0:T(8,128)(2,1)}) custom-call(bf16[64,2048]{1,0:T(8,128)(2,1)} %refs_0_, bf16[64,2048]{1,0:T(8,128)(2,1)} %refs_1_.1, bf16[2,64,8192]{2,1,0:T(8,128)(2,1)} %pad_maximum_fusion.refs_2_, ...), custom_call_target="tpu_custom_call" | custom-call | flops 89999998976 | bytes 30000000 | tf_op jit(solution)/shard_map/pallas_call | solution.py:462
  268.8 7.6 fusion.40.q_ref
  276.4 19.5 %shard_map.205 = (bf16[256,2048]{1,0:T(8,128)(2,1)S(1)}, bf16[256,2048]{1,0:T(8,128)(2,1)S(1)}, f32[32,256]{1,0:T(8,128)S(1)}) custom-call(f32[256,2048]{1,0:T(8,128)} %fusion.40.q_ref, bf16[1280,512]{1,0:T(8,128)(2,1)S(1)} %get-tuple-element.152.k_ref, bf16[1280,512]{1,0:T(8,128)(2,1)S(1)} %get-tuple-element.151.v_ref, f32[1280,256]{1,0:T(8,128)} %fusion.30.bias_ref, ...), custom_call_target="tpu_custom_call" | custom-call | flops 40000000000 | bytes 10000000 | tf_op jit(solution)/shard_map/pallas_call | solution.py:122
  296.0 3.4 multiply_reduce_fusion
  299.4 1.3 copy-done.8
  300.7 1.3 multiply_convert_fusion.1
  302.1 71.0 %shard_map.206 = bf16[2,8,4,64,1024]{4,3,2,1,0:T(8,128)(2,1)} custom-call(bf16[2,8,4,64,1024]{4,3,2,1,0:T(8,128)(2,1)} %get-tuple-element.59.pair_in), custom_call_target="tpu_custom_call", output_to_operand_aliasing={{}: (0, {})} | custom-call | flops 60000002048 | bytes 30000000 | tf_op jit(solution)/shard_map/pallas_call | solution.py:496
  373.1 6.2 fusion.55
  379.3 3.7 all-gather.4.cloned.1.call-done
  383.0 14.7 %fusion.62 = f32[2048,1024]{1,0:T(8,128)} fusion(bf16[2048,2048]{0,1:T(8,128)(2,1)} %all-gather.4.cloned.1.call-done, bf16[2048,1024]{1,0:T(8,128)(2,1)} %bitcast.164), kind=kOutput, calls=%fused_computation.127 | convolution fusion | flops 8589934592 | bytes 20971520 | tf_op jit(solution)/shard_map/dot_general | solution.py:30
  397.7 11.6 %fusion.61 = f32[2048,1024]{1,0:T(8,128)} fusion(bf16[2048,2048]{0,1:T(8,128)(2,1)S(1)} %copy-done.17, bf16[2048,1024]{1,0:T(8,128)(2,1)S(1)} %bitcast.167), kind=kOutput, calls=%fused_computation.126 | convolution fusion | flops 8589934592 | bytes 20971520 | tf_op jit(solution)/shard_map/dot_general | solution.py:30
  409.3 22.1 %fusion.3 = (bf16[2048,1024]{1,0:T(8,128)(2,1)}, bf16[2048,1024]{1,0:T(8,128)(2,1)}, bf16[2048,1024]{1,0:T(8,128)(2,1)}) fusion(f32[2048,1024]{1,0:T(8,128)} %fusion.61, f32[2048,1024]{1,0:T(8,128)} %fusion.62, bf16[1024,2048]{1,0:T(8,128)(2,1)} %bitcast.198, bf16[1,2048,2048]{2,1,0:T(8,128)(2,1)} %all-gather.6.cloned.1.call-done), kind=kOutput, calls=%fused_computation.6 | convolution fusion | flops 8621391872 | bytes 41943040 | tf_op jit(solution)/shard_map/dot_general | solution.py:34
  431.4 12.0 %convolution_convert_fusion = bf16[2048,2048]{0,1:T(8,128)(2,1)S(1)} fusion(bf16[2048,1024]{1,0:T(8,128)(2,1)} %get-tuple-element.138, bf16[1024,2048]{1,0:T(8,128)(2,1)} %bitcast.199), kind=kOutput, calls=%fused_computation.10 | convolution fusion | flops 8594128896 | bytes 16777216 | tf_op jit(solution)/shard_map/dot_general | solution.py:30
  443.3 3.7 fusion.54
  447.1 15.6 %fusion.63 = f32[2048,2048]{0,1:T(8,128)} fusion(bf16[2048,1024]{1,0:T(8,128)(2,1)} %get-tuple-element.62.gate, bf16[2048,1024]{1,0:T(8,128)(2,1)} %bitcast.166), kind=kOutput, calls=%fused_computation.128 | convolution fusion | flops 8589934592 | bytes 25165824 | tf_op jit(solution)/shard_map/dot_general | solution.py:34
  462.7 14.1 %add_convert_fusion = bf16[2048,2048]{0,1:T(8,128)(2,1)} fusion(f32[2048,2048]{0,1:T(8,128)} %fusion.63, bf16[2048,1024]{1,0:T(8,128)(2,1)S(1)} %copy-done.56, bf16[2048,1024]{1,0:T(8,128)(2,1)S(1)} %bitcast.165), kind=kOutput, calls=%fused_computation | convolution fusion | flops 8598323200 | bytes 33554432 | tf_op jit(solution)/shard_map/dot_general | solution.py:34
  476.8 18.6 %reduce-scatter.5.cloned.1.call-done = bf16[256,1024]{0,1:T(8,128)(2,1)} async-done(((bf16[2048,1024]{0,1:T(8,128)(2,1)}), bf16[256,1024]{0,1:T(8,128)(2,1)}) %reduce-scatter.5.cloned.1.call-update) | async-done | bytes 524304 | tf_op jit(solution)/shard_map/reduce_scatter | solution.py:882
  495.5 14.5 %convolution_convert_fusion.1 = bf16[1024,2048]{1,0:T(8,128)(2,1)} fusion(bf16[2048,1024]{1,0:T(8,128)(2,1)} %get-tuple-element.138, bf16[1,2048,2048]{2,1,0:T(8,128)(2,1)} %all-gather.6.cloned.1.call-done), kind=kOutput, calls=%fused_computation.12 | convolution fusion | flops 8592031744 | bytes 16777216 | tf_op jit(solution)/shard_map/dot_general | solution.py:40
  510.0 12.4 %copy.133.normed = bf16[2048,2048]{1,0:T(8,128)(2,1)} copy(bf16[2048,2048]{0,1:T(8,128)(2,1)} %all-gather.4.cloned.1.call-done) | data formatting | bytes 16777216 | tf_op jit(solution)/shard_map/all_gather | solution.py:865
  522.4 79.8 %shard_map.207 = bf16[8,2,64,1024]{3,2,1,0:T(8,128)(2,1)} custom-call(bf16[2048,2048]{1,0:T(8,128)(2,1)} %copy.133.normed, bf16[2048,1024]{1,0:T(8,128)(2,1)} %get-tuple-element.62.gate, bf16[2048,1024]{1,0:T(8,128)(2,1)} %get-tuple-element.136.up), custom_call_target="tpu_custom_call" | custom-call | flops 60000002048 | bytes 30000000 | tf_op jit(solution)/shard_map/pallas_call | solution.py:766
  602.3 2.4 copy.134
  604.7 2.6 fusion.34.lefts
  607.3 1.3 copy.135
  608.6 3.1 pad_maximum_fusion.1.lefts
  611.6 4.5 all-to-all-start
  616.2 3.2 fusion.17
  620.1 1.9 fusion.52
  622.9 6.8 convolution_convert_fusion.2.do_ref
  629.8 24.2 %reduce-scatter.9.cloned.1.call-done = bf16[256,2048]{1,0:T(8,128)(2,1)} async-done(((bf16[1024,2048]{1,0:T(8,128)(2,1)}), bf16[256,2048]{1,0:T(8,128)(2,1)}) %reduce-scatter.9.cloned.1.call-update) | async-done | bytes 1048592 | tf_op jit(solution)/shard_map/reduce_scatter | solution.py:892
  656.4 30.0 %shard_map.208 = (bf16[256,2048]{1,0:T(8,128)(2,1)S(1)}, f32[1280,512]{1,0:T(8,128)}, f32[1280,512]{1,0:T(8,128)}) custom-call(bf16[256,2048]{1,0:T(8,128)(2,1)S(1)} %copy-done.7, bf16[1280,512]{1,0:T(8,128)(2,1)S(1)} %get-tuple-element.152.k_ref, bf16[1280,512]{1,0:T(8,128)(2,1)} %copy-done, bf16[256,2048]{1,0:T(8,128)(2,1)S(1)} %copy-done.5, ...), custom_call_target="tpu_custom_call" | custom-call | flops 80000000000 | bytes 20000000 | tf_op jit(solution)/shard_map/pallas_call | solution.py:212
  686.4 2.5 constant_dynamic-update-slice_fusion.6
  690.7 1.9 convert.22
  692.6 1.3 copy.136
  693.9 3.0 fusion.57
  698.3 1.3 collective-permute-start.5
  702.4 7.3 fusion.64
  709.6 1.6 convert_element_type.165
  711.2 3.2 copy.137.right
  714.9 107.2 %shard_map.209 = f32[64,4096]{1,0:T(8,128)} custom-call(bf16[2,2048,256]{2,1,0:T(8,128)(2,1)} %pad_maximum_fusion.1.lefts, bf16[256,4096]{1,0:T(8,128)(2,1)} %copy.137.right, bf16[1,16,128]{2,1,0:T(8,128)(2,1)} %broadcast_in_dim.36.extra), custom_call_target="tpu_custom_call" | custom-call | flops 80000000000 | bytes 30000000 | tf_op jit(solution)/shard_map/pallas_call | solution.py:668
  822.2 1.9 convert_add_fusion
  825.6 1.4 fusion.37
  827.3 5.9 fusion.24
  834.7 40.1 %shard_map.210 = f32[64,1280]{1,0:T(8,128)} custom-call(bf16[1,2048,256]{2,1,0:T(8,128)(2,1)} %fusion.34.lefts, bf16[256,1024]{1,0:T(8,128)(2,1)} %copy-done.33, bf16[1,2048,256]{2,1,0:T(8,128)(2,1)} %pad_bitcast_fusion.extra), custom_call_target="tpu_custom_call" | custom-call | flops 80000000000 | bytes 30000000 | tf_op jit(solution)/shard_map/pallas_call | solution.py:668
  874.7 1.5 slice_reduce_fusion
  876.3 1.7 fusion.60
  879.0 2.0 convert_bitcast_fusion
  881.7 1.5 copy.159
  883.2 1.5 copy.160
  886.5 2.0 fusion.33
  888.5 1.4 copy.145
  889.9 1.4 copy.146
  (203 shorter events, 32.0 us)
Async XLA Ops:
  7.2 3.6 copy-start.52
  7.2 4.4 copy-start.53
  7.2 5.3 copy-start.42
  7.2 5.3 copy-start.41
  7.2 124.3 %all-gather.6.cloned.1.call-start = ((), (), s32[]{:S(2)}) async-start(), calls=%async_computation.10 | async-start | bytes 9437184 | tf_op jit(solution)/shard_map/all_gather | solution.py:824
  8.0 375.1 %all-gather.4.cloned.1.call-start = ((), (), s32[]{:S(2)}) async-start(), calls=%async_computation.5 | async-start | bytes 9437184 | tf_op jit(solution)/shard_map/all_gather | solution.py:865
  10.8 44.3 %copy-start.11 = (bf16[1,256,2048]{1,2,0:T(8,128)(2,1)}, bf16[1,256,2048]{1,2,0:T(8,128)(2,1)S(1)}, u32[]{:S(2)}) copy-start(bf16[1,256,2048]{1,2,0:T(8,128)(2,1)S(1)} %copy.120) | copy-start | bytes 3145732
  54.8 214.0 %copy-start.35 = (f32[2048,1]{0,1:T(1,128)}, f32[2048,1]{0,1:T(1,128)S(1)}, u32[]{:S(2)}) copy-start(f32[2048,1]{0,1:T(1,128)S(1)} %copy.161) | copy-start | bytes 24580
  55.1 213.7 %copy-start.43 = (f32[256]{0:T(256)}, f32[256]{0:T(256)S(1)}, u32[]{:S(2)}) copy-start(f32[256]{0:T(256)S(1)} %add_rsqrt_fusion.1) | copy-start | bytes 3076
  55.1 5.1 copy-start.54
  64.7 31.4 %collective-permute-start = (bf16[256,1024]{1,0:T(8,128)(2,1)S(1)}, bf16[256,1024]{1,0:T(8,128)(2,1)}, u32[]{:S(2)}, u32[]{:S(2)}) collective-permute-start(bf16[256,1024]{1,0:T(8,128)(2,1)S(1)} %pad_maximum_fusion.3), channel_id=1, source_target_pairs={{0,16},{4,20},{8,24},{12,28},{1,17},{5,21},{9,25},{13,29},{2,18},{... | collective-permute-start | bytes 1572872 | tf_op jit(solution)/shard_map/ppermute | solution.py:26
  73.4 45.2 %collective-permute-start.1 = (bf16[256,1024]{1,0:T(8,128)(2,1)S(1)}, bf16[256,1024]{1,0:T(8,128)(2,1)}, u32[]{:S(2)}, u32[]{:S(2)}) collective-permute-start(bf16[256,1024]{1,0:T(8,128)(2,1)S(1)} %pad_maximum_fusion.3), channel_id=1, source_target_pairs={{0,12},{4,16},{8,20},{12,24},{16,28},{1,13},{5,17},{9,21},{13,25},... | collective-permute-start | bytes 1572872 | tf_op jit(solution)/shard_map/ppermute | solution.py:26
  75.5 54.7 %collective-permute-start.2 = (bf16[256,1024]{1,0:T(8,128)(2,1)S(1)}, bf16[256,1024]{1,0:T(8,128)(2,1)}, u32[]{:S(2)}, u32[]{:S(2)}) collective-permute-start(bf16[256,1024]{1,0:T(8,128)(2,1)S(1)} %pad_maximum_fusion.3), channel_id=1, source_target_pairs={{0,8},{4,12},{8,16},{12,20},{16,24},{20,28},{1,9},{5,13},{9,17},{1... | collective-permute-start | bytes 1572872 | tf_op jit(solution)/shard_map/ppermute | solution.py:26
  78.0 53.3 %collective-permute-start.3 = (bf16[256,1024]{1,0:T(8,128)(2,1)S(1)}, bf16[256,1024]{1,0:T(8,128)(2,1)S(1)}, u32[]{:S(2)}, u32[]{:S(2)}) collective-permute-start(bf16[256,1024]{1,0:T(8,128)(2,1)S(1)} %pad_maximum_fusion.3), channel_id=1, source_target_pairs={{0,4},{4,8},{8,12},{12,16},{16,20},{20,24},{24,28},{1,5},{5,9},{9,... | collective-permute-start | bytes 1572872 | tf_op jit(solution)/shard_map/ppermute | solution.py:26
  85.3 214.1 %copy-start.38 = (f32[2048,1]{0,1:T(1,128)}, f32[2048,1]{0,1:T(1,128)S(1)}, u32[]{:S(2)}) copy-start(f32[2048,1]{0,1:T(1,128)S(1)} %copy.162) | copy-start | bytes 24580
  131.5 144.9 %copy-start = (bf16[1280,512]{1,0:T(8,128)(2,1)}, bf16[1280,512]{1,0:T(8,128)(2,1)S(1)}, u32[]{:S(2)}) copy-start(bf16[1280,512]{1,0:T(8,128)(2,1)S(1)} %get-tuple-element.151.v_ref) | copy-start | bytes 3932164
  268.8 27.2 %slice-start = ((s8[8388608]{0:T(1024)(128)(4,1)}), s8[4194304]{0:T(1024)(128)(4,1)S(1)}, s32[]{:S(2)}) async-start(s8[8388608]{0:T(1024)(128)(4,1)} %bitcast.195), calls=%async_computation.11 | async-start | bytes 8388608
  276.4 19.5 %copy-start.12 = (bf16[1,256,2048]{1,2,0:T(8,128)(2,1)S(1)}, bf16[1,256,2048]{1,2,0:T(8,128)(2,1)}, u32[]{:S(2)}) copy-start(bf16[1,256,2048]{1,2,0:T(8,128)(2,1)} %copy-done.11) | copy-start | bytes 3145732
  276.4 19.6 %slice-start.1 = ((s8[8388608]{0:T(1024)(128)(4,1)}), s8[4194304]{0:T(1024)(128)(4,1)S(1)}, s32[]{:S(2)}) async-start(s8[8388608]{0:T(1024)(128)(4,1)} %bitcast.195), calls=%async_computation.12 | async-start | bytes 8388608
  295.9 3.5 copy-start.1
  295.9 3.5 copy-start.6
  299.4 73.7 %copy-start.47 = (f32[256]{0:T(256)}, f32[256]{0:T(256)S(1)}, u32[]{:S(2)}) copy-start(f32[256]{0:T(256)S(1)} %add_rsqrt_fusion) | copy-start | bytes 3076
  302.1 193.4 %reduce-scatter.5.cloned.1.call-start = ((), (), s32[]{:S(2)}) async-start(), calls=%async_computation.6 | async-start | bytes 4718592 | tf_op jit(solution)/shard_map/reduce_scatter | solution.py:882
  383.0 14.7 %copy-start.17 = (bf16[2048,2048]{0,1:T(8,128)(2,1)S(1)}, bf16[2048,2048]{0,1:T(8,128)(2,1)}, u32[]{:S(2)}) copy-start(bf16[2048,2048]{0,1:T(8,128)(2,1)} %all-gather.4.cloned.1.call-done) | copy-start | bytes 25165828
  383.0 14.7 %copy-start.25 = (bf16[1,8,4,64,1024]{4,3,2,1,0:T(8,128)(2,1)S(1)}, bf16[1,8,4,64,1024]{4,3,2,1,0:T(8,128)(2,1)}, u32[]{:S(2)}) copy-start(bf16[1,8,4,64,1024]{4,3,2,1,0:T(8,128)(2,1)} %get-tuple-element.141) | copy-start | bytes 12582916
  447.1 155.2 %reduce-scatter.7.cloned.1.call-start = ((), (), s32[]{:S(2)}) async-start(), calls=%async_computation.7 | async-start | bytes 9437184 | tf_op jit(solution)/shard_map/reduce_scatter | solution.py:885
  447.1 15.6 %copy-start.24 = (bf16[1,8,4,64,1024]{4,3,2,1,0:T(8,128)(2,1)S(1)}, bf16[1,8,4,64,1024]{4,3,2,1,0:T(8,128)(2,1)}, u32[]{:S(2)}) copy-start(bf16[1,8,4,64,1024]{4,3,2,1,0:T(8,128)(2,1)} %get-tuple-element.142) | copy-start | bytes 12582916
  447.1 15.6 %copy-start.56 = (bf16[2048,1024]{1,0:T(8,128)(2,1)S(1)}, bf16[2048,1024]{1,0:T(8,128)(2,1)}, u32[]{:S(2)}) copy-start(bf16[2048,1024]{1,0:T(8,128)(2,1)} %get-tuple-element.136.up) | copy-start | bytes 12582916
  495.5 158.5 %reduce-scatter.9.cloned.1.call-start = ((), (), s32[]{:S(2)}) async-start(), calls=%async_computation.8 | async-start | bytes 5242880 | tf_op jit(solution)/shard_map/reduce_scatter | solution.py:892
  602.2 2.4 copy-start.36
  602.2 2.4 copy-start.44
  602.3 5.0 copy-start.2
  611.6 4.6 copy-start.39
  611.6 4.6 copy-start.48
  611.6 267.4 %all-to-all-start = ((bf16[8,2,64,1024]{3,2,1,0:T(8,128)(2,1)}), bf16[8,2,64,1024]{3,2,1,0:T(8,128)(2,1)}, u32[]{:S(2)}, u32[]{:S(2)}) async-start(bf16[8,2,64,1024]{3,2,1,0:T(8,128)(2,1)} %shard_map.207), calls=%async_computation.4 | async-start | bytes 4194304 | tf_op jit(solution)/shard_map/all_to_all | solution.py:902
  616.1 95.1 %reduce-scatter.11.cloned.1.call-start = ((), (), s32[]{:S(2)}) async-start(), calls=%async_computation.9 | async-start | bytes 4718592 | tf_op jit(solution)/shard_map/reduce_scatter | solution.py:895
  616.2 3.9 copy-start.9
  616.2 3.9 copy-start.14
  686.4 2.5 copy-start.3
  686.4 3.0 copy-start.26
  690.7 1.9 copy-start.4
  693.9 8.3 copy-start.21
  693.9 8.3 copy-start.23
  697.0 125.2 %collective-permute-start.4 = (bf16[256,1024]{1,0:T(8,128)(2,1)}, bf16[256,1024]{1,0:T(8,128)(2,1)}, u32[]{:S(2)}, u32[]{:S(2)}) collective-permute-start(bf16[256,1024]{1,0:T(8,128)(2,1)} %get-tuple-element.147), channel_id=1, source_target_pairs={{4,0},{8,4},{12,8},{16,12},{20,16},{24,20},{28,24},{5,1},{9,5},{13... | collective-permute-start | bytes 1572872 | tf_op jit(solution)/shard_map/ppermute | solution.py:26
  698.3 123.9 %collective-permute-start.5 = (bf16[256,1024]{1,0:T(8,128)(2,1)}, bf16[256,1024]{1,0:T(8,128)(2,1)}, u32[]{:S(2)}, u32[]{:S(2)}) collective-permute-start(bf16[256,1024]{1,0:T(8,128)(2,1)} %get-tuple-element.150), channel_id=1, source_target_pairs={{8,0},{12,4},{16,8},{20,12},{24,16},{28,20},{9,1},{13,5},{17,9},{2... | collective-permute-start | bytes 1572872 | tf_op jit(solution)/shard_map/ppermute | solution.py:26
  699.6 122.6 %collective-permute-start.6 = (bf16[256,1024]{1,0:T(8,128)(2,1)}, bf16[256,1024]{1,0:T(8,128)(2,1)}, u32[]{:S(2)}, u32[]{:S(2)}) collective-permute-start(bf16[256,1024]{1,0:T(8,128)(2,1)} %get-tuple-element.149), channel_id=1, source_target_pairs={{12,0},{16,4},{20,8},{24,12},{28,16},{13,1},{17,5},{21,9},{25,13},... | collective-permute-start | bytes 1572872 | tf_op jit(solution)/shard_map/ppermute | solution.py:26
  700.9 121.3 %collective-permute-start.7 = (bf16[256,1024]{1,0:T(8,128)(2,1)}, bf16[256,1024]{1,0:T(8,128)(2,1)}, u32[]{:S(2)}, u32[]{:S(2)}) collective-permute-start(bf16[256,1024]{1,0:T(8,128)(2,1)} %get-tuple-element.148), channel_id=1, source_target_pairs={{16,0},{20,4},{24,8},{28,12},{17,1},{21,5},{25,9},{29,13},{18,2},{... | collective-permute-start | bytes 1572872 | tf_op jit(solution)/shard_map/ppermute | solution.py:26
  702.4 7.3 copy-start.29
  714.9 107.2 %copy-start.22 = (f32[256,1024]{1,0:T(8,128)S(1)}, f32[256,1024]{1,0:T(8,128)}, u32[]{:S(2)}) copy-start(f32[256,1024]{1,0:T(8,128)} %slice.149) | copy-start | bytes 3145732
  824.5 2.6 copy-start.13
  824.5 2.6 copy-start.37
  825.5 1.8 copy-start.55
  827.3 5.9 copy-start.33
  834.7 43.3 %copy-start.30 = (f32[64,4096]{1,0:T(8,128)S(1)}, f32[64,4096]{1,0:T(8,128)}, u32[]{:S(2)}) copy-start(f32[64,4096]{1,0:T(8,128)} %shard_map.209) | copy-start | bytes 3145732
  881.7 3.0 copy-start.27
  881.7 3.0 copy-start.31
  881.7 3.0 copy-start.32
  881.7 3.0 copy-start.49
  881.7 3.0 copy-start.51
  883.2 2.8 copy-start.10
  883.2 3.0 copy-start.15
  883.2 3.3 copy-start.16
  883.2 3.3 copy-start.40
  883.2 3.3 copy-start.46
  (10 other events, 11.6 us)
Sparse Core Ops, SparseCore 0:
  9.7 109.6 all-gather.5
  302.2 80.8 all-gather.3
  447.2 48.2 reduce-scatter.4
  497.6 87.7 reduce-scatter.6
  602.4 51.4 reduce-scatter.8
  656.2 50.4 reduce-scatter.10

commit v3 on v2

--- a/solution.py
+++ b/solution.py
@@ -78,7 +78,9 @@
     return lax.dot_general(left, right, (((1,), (0,)), ((), ())), preferred_element_type=jnp.float32)
 
 
-def attend_forward_kernel(q_ref, k_ref, v_ref, bias_ref, cos_ref, sin_ref, o_ref, qr_ref, lse_ref):
+def attend_forward_kernel(
+    q_ref, k_ref, v_ref, bias_ref, cos_ref, sin_ref, o_ref, qr_ref, lse_ref
+):
     rows = q_ref.shape[0]
     group = HEADS // KV_HEADS
     span = k_ref.shape[0] - rows + QTILE
@@ -145,7 +147,10 @@
     )(q, k, v, bias, cosine, sine)
 
 
-def attend_backward_kernel(qr_ref, k_ref, v_ref, do_ref, o_ref, lse_ref, bias_ref, cos_ref, sin_ref, dq_ref, dk_ref, dv_ref):
+def attend_backward_kernel(
+    qr_ref, k_ref, v_ref, do_ref, o_ref, lse_ref, bias_ref, cos_ref, sin_ref, earlier,
+    dq_ref, dk_ref, dv_ref
+):
     rows = qr_ref.shape[0]
     group = HEADS // KV_HEADS
     span = k_ref.shape[0] - rows + QTILE
@@ -200,7 +205,7 @@
         ).astype(jnp.bfloat16)
 
 
-def attend_backward(qr, k, v, do, o, lse, bias, cosine, sine):
+def attend_backward(qr, k, v, do, o, lse, bias, cosine, sine, earlier):
     rows, width = qr.shape
     steps = KV_HEADS * HEAD_DIM // LANES
     qw = width // steps
@@ -217,6 +222,7 @@
             pl.BlockSpec((heads, rows), lambda i: (i, 0)),
             pl.BlockSpec((window, rows), lambda i: (0, 0)),
             table, table,
+            pl.BlockSpec(memory_space=pl.ANY),
         ],
         out_specs=[wide, tall, tall],
         out_shape=[
@@ -226,7 +232,7 @@
         ],
         compiler_params=pltpu.CompilerParams(vmem_limit_bytes=48 * 1024 * 1024),
         cost_estimate=pl.CostEstimate(flops=80_000_000_000, bytes_accessed=20_000_000, transcendentals=0),
-    )(qr, k, v, do, o, lse, bias, cosine, sine)
+    )(qr, k, v, do, o, lse, bias, cosine, sine, earlier)
 
 
 def turn_tables(position):
@@ -297,17 +303,32 @@
         started[name].wait_send()
 
 
-def doubling(name, size, order, awaited, block, target):
+def doubling(name, size, order, awaited, block, target, along=2):
     hops, held = [], {0: awaited}
     for mask in order:
         hop, got = [], {}
         for r, needs in held.items():
             key = (name, r, mask)
-            hop.append((key, needs, block(r), target(r), (0, 0, mask)))
+            peer = tuple(mask if place == along else 0 for place in range(3))
+            hop.append((key, needs, block(r), target(r), peer))
             got[r ^ mask] = (key,)
         held.update(got)
         hops.append(hop)
     return hops, held
+
+
+def line_gather(name, own, whole, sizes):
+    chips = sizes[0] // 2
+    ctx = lax.axis_index("ctx")
+    chip, side = ctx // 2, ctx % 2
+    far_first = [1 << bit for bit in range(chips.bit_length() - 1)][::-1]
+    target = lambda r: whole.at[chip ^ r, side]
+    block = lambda r: target(r) if r else own
+    hops, held = doubling((name, "z"), chips, far_first, (), block, target, 0)
+    last = [
+        ((name, "core", r), held[r], block(r), target(r), (0, 1, 0)) for r in range(chips)
+    ]
+    return hops + [last]
 
 
 def front_masks(ctx_size, fsdp_size, paired):
@@ -316,22 +337,33 @@
         (m, s, 0)
         for m in range(chips)
         for s in range(2)
-        if (m or s) and (paired or not m or not s)
+        if (m or s) and (paired or m + s == 1 or (not s and not m & (m - 1)))
     ]
     return peers + [(0, 0, m) for m in range(1, fsdp_size)]
 
 
-def front_copies(parts, wholes, pair_ref, pair_all, down_ref, down_all, sizes):
+def front_copies(parts, wholes, pair_ref, pair_all, down_ref, down_all, line, sizes):
     ctx_size, fsdp_size = sizes
     chips = ctx_size // 2
     ctx, fsdp = lax.axis_index("ctx"), lax.axis_index("fsdp")
     chip, side = ctx // 2, ctx % 2
     masks = [1 << bit for bit in range(fsdp_size.bit_length() - 1)]
     orders = [masks, masks[::-1]]
-    copies = []
+    far_first = [1 << bit for bit in range(chips.bit_length() - 1)][::-1]
+    copies, arrival = [], {}
+    lines = []
     for n, (own, whole) in enumerate(zip(parts, wholes)):
-        for m in range(1, chips):
-            copies.append((("z", n, m), (), own, whole.at[chip, side, fsdp], (m, 0, 0)))
+        view = lambda r, own=own, whole=whole: (
+            whole.at[chip ^ r, side, fsdp] if r else own
+        )
+        target = lambda r, whole=whole: whole.at[chip ^ r, side, fsdp]
+        hops, held = doubling(("z", n), chips, far_first, (), view, target, 0)
+        lines.append(hops)
+        for r, keys in held.items():
+            arrival[n, r] = keys
+    for hop in zip(*lines):
+        for pieces in hop:
+            copies.extend(pieces)
     exchange = []
     if pair_ref is not None:
         ff_own = pair_ref.shape[2] // ctx_size
@@ -364,7 +396,7 @@
         cut = (width // 2 + LANES - 1) // LANES * LANES
         halves = [(0, cut), (cut, width - cut)]
         for m in range(chips):
-            first = (("z", n, m),) if m else ()
+            first = arrival[n, m]
             lists, last = [], []
             for h, ((lo, span), order) in enumerate(zip(halves, orders)):
                 cols = pl.ds(lo, span)
@@ -396,7 +428,7 @@
                 )
             queues.append(stages)
     sharing = []
-    lag = 2
+    lag, done = 2, 0
     for turn in range(len(queues) + lag * (len(orders[0]) + 1)):
         for stage in range(len(orders[0]) + 1):
             at = turn - lag * stage
@@ -404,105 +436,187 @@
                 sharing.extend(queues[at][stage])
         if turn == chips:
             sharing.extend(exchange)
+            for hop in line[:1]:
+                sharing.extend(hop)
+        if turn > chips and (turn - chips) % 4 == 0 and (turn - chips) // 4 < len(line) - 1:
+            sharing.extend(line[(turn - chips) // 4])
+            done = (turn - chips) // 4
+    for hop in line[done + 1 :]:
+        sharing.extend(hop)
     return copies + sharing
 
 
 def front_kernel(sizes, count, paired, *refs):
     parts, refs = refs[:count], refs[count:]
-    pair_ref, down_ref, refs = (refs[0], refs[1], refs[3:]) if paired else (None, None, refs)
+    if paired:
+        pair_ref, down_ref, cot_ref, kv_ref, zero_ref, *refs = refs
+    else:
+        pair_ref = down_ref = None
     wholes, refs = refs[:count], refs[count:]
-    pair_all, down_all, refs = (refs[0], refs[1], refs[2:]) if paired else (None, None, refs)
-    send_sems, recv_sems, own_sems = refs
+    if paired:
+        pair_all, down_all, cot_all, window, *refs = refs
+    else:
+        pair_all = down_all = None
+    send_sems, recv_sems, own_sems, halo_send, halo_recv = refs
     greet(front_masks(*sizes, paired))
     ctx, fsdp = lax.axis_index("ctx"), lax.axis_index("fsdp")
+    reach = halo_send.shape[0]
+    halos = []
+    if paired:
+        for step in range(1, reach + 1):
+            copy = pltpu.make_async_remote_copy(
+                src_ref=kv_ref,
+                dst_ref=window.at[reach - step],
+                send_sem=halo_send.at[step - 1],
+                recv_sem=halo_recv.at[step - 1],
+                device_id=(lax.rem(ctx + step, sizes[0]), fsdp),
+                device_id_type=pl.DeviceIdType.MESH,
+            )
+            halos.append((step, copy))
+            pl.when(ctx + step < sizes[0])(copy.start)
     kept = []
     for n, (own, whole) in enumerate(zip(parts, wholes)):
         kept.append(
             pltpu.make_async_copy(own, whole.at[ctx // 2, ctx % 2, fsdp], own_sems.at[n])
         )
+    empty = []
     if paired:
         ff_own = pair_ref.shape[2] // sizes[0]
         columns = pl.ds(pl.multiple_of(ctx * ff_own, ff_own), ff_own)
-        kept.append(
-            pltpu.make_async_copy(
-                pair_ref.at[:, :, columns], pair_all.at[:, ctx, fsdp], own_sems.at[count]
+        for n, (source, target) in enumerate(
+            (
+                (pair_ref.at[:, :, columns], pair_all.at[:, ctx, fsdp]),
+                (down_ref, down_all.at[fsdp]),
+                (cot_ref, cot_all.at[ctx // 2, ctx % 2]),
+                (kv_ref, window.at[reach]),
             )
-        )
-        kept.append(
-            pltpu.make_async_copy(down_ref, down_all.at[fsdp], own_sems.at[count + 1])
-        )
+        ):
+            kept.append(pltpu.make_async_copy(source, target, own_sems.at[count + n]))
+        for step in range(1, reach + 1):
+            copy = pltpu.make_async_copy(
+                zero_ref, window.at[reach - step], own_sems.at[count + 3 + step]
+            )
+            empty.append((step, copy))
     for copy in kept:
         copy.start()
-    copies = front_copies(parts, wholes, pair_ref, pair_all, down_ref, down_all, sizes)
+    for step, copy in empty:
+        pl.when(ctx - step < 0)(copy.start)
+    line = line_gather("cot", cot_ref, cot_all, sizes) if paired else []
+    copies = front_copies(parts, wholes, pair_ref, pair_all, down_ref, down_all, line, sizes)
     run_copies(copies, send_sems, recv_sems)
     for copy in kept:
         copy.wait()
-
-
-def gather_front(parts, pair, down, earlier, sizes, collective_id):
+    for step, copy in empty:
+        pl.when(ctx - step < 0)(copy.wait)
+    for step, copy in halos:
+        pl.when(ctx - step >= 0)(copy.wait_recv)
+    for step, copy in halos:
+        pl.when(ctx + step < sizes[0])(copy.wait_send)
+
+
+def gather_front(parts, pair, down, cot, key_value, sizes, collective_id):
     ctx_size, fsdp_size = sizes
     chips = ctx_size // 2
     rows = parts[0].shape[0]
     paired = pair is not None
+    reach = WINDOW // STRETCH
     count = len(parts) * (chips - 1 + chips * (2 * (fsdp_size - 1) + 1) + fsdp_size - 1)
     shapes = [
         jax.ShapeDtypeStruct((chips, 2, fsdp_size, rows, part.shape[1]), part.dtype)
         for part in parts
     ]
+    arrays = list(parts)
     if paired:
-        count += ctx_size - 1 + 2 * (fsdp_size - 1)
-        shapes.append(
-            jax.ShapeDtypeStruct(
-                (2, ctx_size, fsdp_size, rows, pair.shape[2] // ctx_size), pair.dtype
-            )
-        )
-        shapes.append(jax.ShapeDtypeStruct((fsdp_size,) + down.shape, down.dtype))
+        count += ctx_size - 1 + 2 * (fsdp_size - 1) + 2 * chips - 1
+        columns = pair.shape[2] // ctx_size
+        shapes += [
+            jax.ShapeDtypeStruct((2, ctx_size, fsdp_size, rows, columns), pair.dtype),
+            jax.ShapeDtypeStruct((fsdp_size,) + down.shape, down.dtype),
+            jax.ShapeDtypeStruct((chips, 2) + cot.shape, cot.dtype),
+            jax.ShapeDtypeStruct((reach + 1,) + key_value.shape, key_value.dtype),
+        ]
+        arrays += [pair, down, cot, key_value, jnp.zeros_like(key_value)]
     hbm = pl.BlockSpec(memory_space=pl.ANY)
     vmem = pl.BlockSpec(memory_space=pltpu.VMEM)
     return pl.pallas_call(
         functools.partial(front_kernel, sizes, len(parts), paired),
-        in_specs=[vmem] * len(shapes) + ([hbm] if paired else []),
+        in_specs=[vmem] * len(arrays),
         out_specs=[hbm] * len(shapes),
         out_shape=shapes,
         scratch_shapes=[
             pltpu.SemaphoreType.DMA((count,)),
             pltpu.SemaphoreType.DMA((count,)),
-            pltpu.SemaphoreType.DMA((len(shapes),)),
+            pltpu.SemaphoreType.DMA((len(shapes) + reach,)),
+            pltpu.SemaphoreType.DMA((reach,)),
+            pltpu.SemaphoreType.DMA((reach,)),
         ],
         compiler_params=pltpu.CompilerParams(collective_id=collective_id, has_side_effects=True),
-        cost_estimate=pl.CostEstimate(flops=90_000_000_000, bytes_accessed=30_000_000, transcendentals=0),
-    )(*parts, *([pair, down, earlier] if paired else []))
-
-
-def hidden_kernel(sizes, pair_in, pair_all, send_sems, recv_sems):
+        cost_estimate=pl.CostEstimate(
+            flops=90_000_000_000, bytes_accessed=1_000_000, transcendentals=0
+        ),
+    )(*arrays)
+
+
+def hidden_kernel(sizes, pieces, pair_in, normed_ref, pair_all, normed_all, send_sems, recv_sems, own_sem):
     ctx_size, fsdp_size = sizes
-    fsdp = lax.axis_index("fsdp")
+    ctx, fsdp = lax.axis_index("ctx"), lax.axis_index("fsdp")
     masks = [1 << bit for bit in range(fsdp_size.bit_length() - 1)]
-    greet([(0, 0, m) for m in masks])
+    far = [1 << bit for bit in range((ctx_size // 2).bit_length() - 1)]
+    greet([(0, 0, m) for m in masks] + [(m, 0, 0) for m in far] + [(0, 1, 0)])
+    mine = pltpu.make_async_copy(normed_ref, normed_all.at[ctx // 2, ctx % 2], own_sem)
+    mine.start()
     lists = []
     for h, order in enumerate([masks, masks[::-1]]):
         view = lambda r, h=h: pair_all.at[h, :, fsdp ^ r]
         lists.append(doubling(("pair", h), fsdp_size, order, (), view, view)[0])
-    copies = []
-    for hop in zip(*lists):
-        for pieces in zip(*hop):
-            copies.extend(pieces)
+    rows = normed_ref.shape[0] // pieces
+    lines = []
+    for n in range(pieces):
+        strip = pl.ds(n * rows, rows)
+        lines.append(
+            line_gather(("normed", n), normed_ref.at[strip], normed_all.at[:, :, strip], sizes)
+        )
+    copies = [copy for line in lines for copy in line[0]]
+    pair_hops = [
+        [copy for pieces in zip(*(hops[n] for hops in lists)) for copy in pieces]
+        for n in range(len(masks))
+    ]
+    copies += pair_hops[0]
+    depth = len(lines[0])
+    for turn in range(pieces + depth - 2):
+        for stage in range(1, depth):
+            if 0 <= turn - stage + 1 < pieces:
+                copies.extend(lines[turn - stage + 1][stage])
+        if turn == pieces // 2:
+            for hop in pair_hops[1:]:
+                copies.extend(hop)
     run_copies(copies, send_sems, recv_sems)
-
-
-def gather_hidden(pair_all, sizes):
-    count = 2 * (sizes[1] - 1)
+    mine.wait()
+
+
+def gather_hidden(pair_all, normed, sizes):
+    ctx_size, fsdp_size = sizes
+    chips = ctx_size // 2
+    pieces = 4
+    count = 2 * (fsdp_size - 1) + pieces * (2 * chips - 1)
     hbm = pl.BlockSpec(memory_space=pl.ANY)
     return pl.pallas_call(
-        functools.partial(hidden_kernel, sizes),
-        in_specs=[hbm],
-        out_specs=hbm,
-        out_shape=jax.ShapeDtypeStruct(pair_all.shape, pair_all.dtype),
+        functools.partial(hidden_kernel, sizes, pieces),
+        in_specs=[hbm, pl.BlockSpec(memory_space=pltpu.VMEM)],
+        out_specs=[hbm, hbm],
+        out_shape=[
+            jax.ShapeDtypeStruct(pair_all.shape, pair_all.dtype),
+            jax.ShapeDtypeStruct((chips, 2) + normed.shape, normed.dtype),
+        ],
         input_output_aliases={0: 0},
-        scratch_shapes=[pltpu.SemaphoreType.DMA((count,)), pltpu.SemaphoreType.DMA((count,))],
+        scratch_shapes=[
+            pltpu.SemaphoreType.DMA((count,)),
+            pltpu.SemaphoreType.DMA((count,)),
+            pltpu.SemaphoreType.DMA,
+        ],
         compiler_params=pltpu.CompilerParams(collective_id=2, has_side_effects=True),
-        cost_estimate=pl.CostEstimate(flops=60_000_000_000, bytes_accessed=30_000_000, transcendentals=0),
-    )(pair_all)
+        cost_estimate=pl.CostEstimate(flops=90_000_000_000, bytes_accessed=30_000_000, transcendentals=0),
+    )(pair_all, normed)
 
 
 def hop_slots(size, order):
@@ -525,9 +639,12 @@
 
 
 def reduce_kernel(
-    sizes, chunk, products, extras, lefts, right, extra, total, terms, core_got, line_sent, line_got,
-    core_send, core_recv, hop_send, hop_recv, line_send, line_recv, *hop_buffers
+    sizes, chunk, products, extras, carried, lefts, right, extra, *refs
 ):
+    total, refs = refs[carried], refs[1 + 2 * carried :]
+    terms, core_got, line_sent, line_got = refs[:4]
+    core_send, core_recv, hop_send, hop_recv, line_send, line_recv = refs[4:10]
+    hop_buffers = refs[10:]
     ctx_size, fsdp_size = sizes
     chips = ctx_size // 2
     rows = total.shape[0]
@@ -544,7 +661,9 @@
     ctx, fsdp = lax.axis_index("ctx"), lax.axis_index("fsdp")
     chip, side = ctx // 2, ctx % 2
     greet(
-        [(0, 1, 0)] + [(0, 0, m) for m in masks] + [(m, 0, 0) for m in range(1, chips)]
+        [(0, 1, 0)]
+        + [(0, 0, m) for m in masks]
+        + [(1 << bit, 0, 0) for bit in range(chips.bit_length() - 1)]
     )
 
     def core_copy(i):
@@ -558,11 +677,25 @@
             sent.at[i], got.at[i], hop_send.at[h, j, i], hop_recv.at[h, j, i], (0, 0, orders[h][j])
         )
 
-    def line_copy(m, i):
+    near_first = [1 << bit for bit in range(chips.bit_length() - 1)]
+    line_slots = hop_slots(chips, near_first)
+    line_first = [sum(chips >> (k + 1) for k in range(j)) for j in range(len(near_first))]
+
+    def line_copy(j, i):
+        blocks = pl.ds(line_first[j], chips >> (j + 1))
         return remote(
-            line_sent.at[i, m - 1], line_got.at[i, m - 1],
-            line_send.at[i, m - 1], line_recv.at[i, m - 1], (m, 0, 0),
+            line_sent.at[i, blocks], line_got.at[i, blocks],
+            line_send.at[i, j], line_recv.at[i, j], (near_first[j], 0, 0),
         )
+
+    def line_held(h, upto, i, r):
+        cols = slice(h * half, (h + 1) * half)
+        value = held(h, bits, i, chip ^ r, 0)
+        for j in range(upto):
+            value += line_got[i, line_first[j] + line_slots[j].index(r), :, cols].astype(
+                jnp.float32
+            )
+        return value
 
     def held(h, upto, i, z, r):
         cols = pl.ds(h * half, half)
@@ -571,6 +704,9 @@
         for j in range(upto):
             value += hops[h][j][1][i, slots[h][j].index(r), z].astype(jnp.float32)
         return value
+
+    slack = 3
+    last = bits + 1 + slack * len(near_first)
 
     def step(t, carry):
         @pl.when(t < products)
@@ -607,46 +743,48 @@
                             )
                     hop_copy(h, j, i).start()
 
-        @pl.when((t >= bits + 1) & (t < count + bits + 1))
+        for j in range(len(near_first)):
+            lag = bits + 1 + slack * j
+
+            @pl.when((t >= lag) & (t < count + lag))
+            def _(j=j, lag=lag):
+                i = t - lag
+                if j:
+                    line_copy(j - 1, i).wait_recv()
+                for h in range(2):
+                    if j == 0:
+                        hop_copy(h, bits - 1, i).wait_recv()
+                    for s, r in enumerate(line_slots[j]):
+                        line_sent[i, line_first[j] + s, :, h * half : (h + 1) * half] = line_held(
+                            h, j, i, r | near_first[j]
+                        ).astype(jnp.bfloat16)
+                line_copy(j, i).start()
+
+        @pl.when(t >= last)
         def _():
-            i = t - (bits + 1)
+            i = t - last
+            line_copy(len(near_first) - 1, i).wait_recv()
             for h in range(2):
-                hop_copy(h, bits - 1, i).wait_recv()
-                for m in range(1, chips):
-                    line_sent[i, m - 1, :, h * half : (h + 1) * half] = held(
-                        h, bits, i, chip ^ m, 0
-                    ).astype(jnp.bfloat16)
-            for m in range(1, chips):
-                line_copy(m, i).start()
-
-        @pl.when(t >= bits + 2)
-        def _():
-            i = t - (bits + 2)
-            for m in range(1, chips):
-                line_copy(m, i).wait_recv()
-            for h in range(2):
-                value = held(h, bits, i, chip, 0)
-                for m in range(1, chips):
-                    value += line_got[i, m - 1, :, h * half : (h + 1) * half].astype(jnp.float32)
+                value = line_held(h, len(near_first), i, 0)
                 total[:, pl.ds(pl.multiple_of(i * chunk + h * half, half), half)] = value
 
         return carry
 
-    lax.fori_loop(0, count + bits + 2, step, 0)
+    lax.fori_loop(0, count + last, step, 0)
 
     def finish(i, carry):
         core_copy(i).wait_send()
         for h in range(2):
             for j in range(bits):
                 hop_copy(h, j, i).wait_send()
-        for m in range(1, chips):
-            line_copy(m, i).wait_send()
+        for j in range(len(near_first)):
+            line_copy(j, i).wait_send()
         return carry
 
     lax.fori_loop(0, count, finish, 0)
 
 
-def reduce_rows(lefts, right, extra, chunk, sizes, collective_id):
+def reduce_rows(lefts, right, extra, carried, chunk, sizes, collective_id):
     ctx_size, fsdp_size = sizes
     chips = ctx_size // 2
     depth = lefts.shape[1]
@@ -665,11 +803,14 @@
             buffers += [pltpu.VMEM(shape, jnp.bfloat16)] * 2
     line = pltpu.VMEM((count, max(chips - 1, 1), rows, chunk), jnp.bfloat16)
     vmem = pl.BlockSpec(memory_space=pltpu.VMEM)
+    hbm = pl.BlockSpec(memory_space=pl.ANY)
     return pl.pallas_call(
-        functools.partial(reduce_kernel, sizes, chunk, products, extras),
-        in_specs=[vmem] * 3,
-        out_specs=vmem,
-        out_shape=jax.ShapeDtypeStruct((rows, count * chunk), jnp.float32),
+        functools.partial(reduce_kernel, sizes, chunk, products, extras, len(carried)),
+        in_specs=[vmem] * 3 + [hbm] * len(carried),
+        out_specs=[vmem] + [hbm] * len(carried),
+        out_shape=[jax.ShapeDtypeStruct((rows, count * chunk), jnp.float32)]
+        + [jax.ShapeDtypeStruct(array.shape, array.dtype) for array in carried],
+        input_output_aliases={3 + n: 1 + n for n in range(len(carried))},
         scratch_shapes=[
             pltpu.VMEM((count, chips, 2, fsdp_size, rows, chunk), jnp.bfloat16),
             pltpu.VMEM((count, chips, fsdp_size, rows, chunk), jnp.bfloat16),
@@ -679,19 +820,20 @@
             pltpu.SemaphoreType.DMA((count,)),
             pltpu.SemaphoreType.DMA((2, bits, count)),
             pltpu.SemaphoreType.DMA((2, bits, count)),
-            pltpu.SemaphoreType.DMA((count, max(chips - 1, 1))),
-            pltpu.SemaphoreType.DMA((count, max(chips - 1, 1))),
+            pltpu.SemaphoreType.DMA((count, chips.bit_length() - 1)),
+            pltpu.SemaphoreType.DMA((count, chips.bit_length() - 1)),
         ]
         + buffers,
         compiler_params=pltpu.CompilerParams(
             collective_id=collective_id, has_side_effects=True, vmem_limit_bytes=56 * 1024 * 1024
         ),
         cost_estimate=pl.CostEstimate(flops=80_000_000_000, bytes_accessed=30_000_000, transcendentals=0),
-    )(lefts, right, extra)
+    )(lefts, right, extra, *carried)
 
 
 def hidden_grad_kernel(
-    sizes, normed, gate, up, pair_sum, terms, pair_sent, pair_got, pair_send, pair_recv
+    sizes, normed, gate, up, carried_in, pair_sum, carried,
+    terms, pair_sent, pair_got, pair_send, pair_recv
 ):
     ctx_size, fsdp_size = sizes
     count, span = terms.shape[1], normed.shape[1] // terms.shape[1]
@@ -719,9 +861,9 @@
     def step(t, carry):
         @pl.when(t < count)
         def _():
-            columns = normed[:, pl.ds(pl.multiple_of(t * span, span), span)]
+            rows = pl.ds(pl.multiple_of(t * span, span), span)
             for h, grad in enumerate((gate, up)):
-                term = across(columns, grad[...])
+                term = across(normed[:, rows], grad[...])
                 terms[h, t] = term.astype(jnp.bfloat16).reshape(terms.shape[2:])
 
         for j in range(bits):
@@ -757,17 +899,22 @@
     lax.fori_loop(0, count, finish, 0)
 
 
-def reduce_hidden(normed, gate, up, sizes):
+def reduce_hidden(normed, gate, up, carried, sizes):
     ctx_size, fsdp_size = sizes
     bits = fsdp_size.bit_length() - 1
     rows, columns = normed.shape[1] // (ctx_size * fsdp_size), gate.shape[1]
     pair = pltpu.VMEM((2, ctx_size, fsdp_size - 1, rows, columns), jnp.bfloat16)
     vmem = pl.BlockSpec(memory_space=pltpu.VMEM)
+    hbm = pl.BlockSpec(memory_space=pl.ANY)
     return pl.pallas_call(
         functools.partial(hidden_grad_kernel, sizes),
-        in_specs=[vmem] * 3,
-        out_specs=vmem,
-        out_shape=jax.ShapeDtypeStruct((ctx_size, 2, rows, columns), jnp.bfloat16),
+        in_specs=[vmem] * 3 + [hbm],
+        out_specs=[vmem, hbm],
+        out_shape=[
+            jax.ShapeDtypeStruct((ctx_size, 2, rows, columns), jnp.bfloat16),
+            jax.ShapeDtypeStruct(carried.shape, carried.dtype),
+        ],
+        input_output_aliases={3: 1},
         scratch_shapes=[
             pltpu.VMEM((2, ctx_size, fsdp_size, rows, columns), jnp.bfloat16), pair, pair,
         ]
@@ -776,7 +923,136 @@
             collective_id=3, has_side_effects=True, vmem_limit_bytes=60 * 1024 * 1024
         ),
         cost_estimate=pl.CostEstimate(flops=60_000_000_000, bytes_accessed=30_000_000, transcendentals=0),
-    )(normed, gate, up)
+    )(normed, gate, up, carried)
+
+
+def out_norm_kernel(mix, weight, stream, gain, resid, normed, total):
+    i, steps = pl.program_id(0), pl.num_programs(0)
+    span = weight.shape[1]
+    cols = pl.ds(pl.multiple_of(i * span, span), span)
+    total[:, cols] = stream[:, cols].astype(jnp.float32) + product(mix[...], weight[...])
+
+    @pl.when(i == steps - 1)
+    def _():
+        h = total[...]
+        resid[...] = h
+        inverse = lax.rsqrt(jnp.mean(h * h, axis=1, keepdims=True) + EPS)
+        normed[...] = (h * inverse * gain[...]).astype(jnp.bfloat16)
+
+
+def out_norm(mix, weight, stream, gain):
+    rows, width = mix.shape
+    steps = 4
+    whole = pl.BlockSpec((rows, width), lambda i: (0, 0))
+    return pl.pallas_call(
+        out_norm_kernel,
+        grid=(steps,),
+        in_specs=[
+            whole,
+            pl.BlockSpec((width, width // steps), lambda i: (0, i)),
+            whole,
+            pl.BlockSpec((1, width), lambda i: (0, 0)),
+        ],
+        out_specs=[whole, whole],
+        out_shape=[
+            jax.ShapeDtypeStruct((rows, width), jnp.float32),
+            jax.ShapeDtypeStruct((rows, width), jnp.bfloat16),
+        ],
+        scratch_shapes=[pltpu.VMEM((rows, width), jnp.float32)],
+        compiler_params=pltpu.CompilerParams(vmem_limit_bytes=40 * 1024 * 1024),
+        cost_estimate=pl.CostEstimate(
+            flops=2 * rows * width * width, bytes_accessed=14_000_000, transcendentals=0
+        ),
+    )(mix, weight, stream, gain)
+
+
+def norm_back_kernel(columns, resid, gain, cot, weight, grad_ref, low_ref, mix_ref, gain_ref):
+    @pl.when(pl.program_id(0) == 0)
+    def _():
+        h = resid[...]
+        inverse = lax.rsqrt(jnp.mean(h * h, axis=1, keepdims=True) + EPS)
+        normal = h * inverse
+        slope = columns[...].astype(jnp.float32)
+        gain_ref[...] = jnp.sum(slope * normal, axis=0, keepdims=True)
+        grad = cot[...].astype(jnp.float32) + norm_back(slope * gain[...], normal, inverse)
+        grad_ref[...] = grad
+        low_ref[...] = grad.astype(jnp.bfloat16)
+
+    mix_ref[...] = against(low_ref[...], weight[...]).astype(jnp.bfloat16)
+
+
+def norm_back_mix(columns, resid, gain, cot, weight):
+    rows, width = resid.shape
+    steps = 4
+    whole = pl.BlockSpec((rows, width), lambda i: (0, 0))
+    line = pl.BlockSpec((1, width), lambda i: (0, 0))
+    return pl.pallas_call(
+        norm_back_kernel,
+        grid=(steps,),
+        in_specs=[
+            whole, whole, line, whole,
+            pl.BlockSpec((width // steps, width), lambda i: (i, 0)),
+        ],
+        out_specs=[whole, whole, pl.BlockSpec((rows, width // steps), lambda i: (0, i)), line],
+        out_shape=[
+            jax.ShapeDtypeStruct((rows, width), jnp.float32),
+            jax.ShapeDtypeStruct((rows, width), jnp.bfloat16),
+            jax.ShapeDtypeStruct((rows, width), jnp.bfloat16),
+            jax.ShapeDtypeStruct((1, width), jnp.float32),
+        ],
+        compiler_params=pltpu.CompilerParams(vmem_limit_bytes=40 * 1024 * 1024),
+        cost_estimate=pl.CostEstimate(
+            flops=2 * rows * width * width, bytes_accessed=16_000_000, transcendentals=0
+        ),
+    )(columns, resid, gain, cot, weight)
+
+
+def hidden_layer_kernel(
+    normed, cot, gate_weight, up_weight, down_weight,
+    hidden_ref, dgate_ref, dup_ref, down_ref, columns_ref
+):
+    x = normed[...]
+    gate = product(x, gate_weight[...])
+    up = product(x, up_weight[...])
+    grad = against(cot[...], down_weight[...])
+    sigmoid = jax.nn.sigmoid(gate)
+    silu = gate * sigmoid
+    hidden = (silu * up).astype(jnp.bfloat16)
+    dgate = (grad * up * sigmoid * (1.0 + gate * (1.0 - sigmoid))).astype(jnp.bfloat16)
+    dup = (grad * silu).astype(jnp.bfloat16)
+    hidden_ref[...] = hidden
+    dgate_ref[...] = dgate
+    dup_ref[...] = dup
+    columns = against(dgate, gate_weight[...]) + against(dup, up_weight[...])
+    columns_ref[...] = columns.astype(jnp.bfloat16)
+    down_ref[...] = product(hidden, down_weight[...]).astype(jnp.bfloat16)
+
+
+def hidden_layer(normed, cot, pair, down_weight):
+    tokens, width = normed.shape
+    share = pair.shape[2]
+    tile = min(256, tokens)
+    wide = pl.BlockSpec((tile, width), lambda i: (i, 0))
+    thin = pl.BlockSpec((tile, share), lambda i: (i, 0))
+    once = pl.Buffered(buffer_count=1)
+    weights = [
+        pl.BlockSpec((None,) + pair.shape[1:], lambda i, n=n: (n, 0, 0), pipeline_mode=once)
+        for n in range(2)
+    ]
+    down = pl.BlockSpec(down_weight.shape, lambda i: (0, 0), pipeline_mode=once)
+    thin_out = jax.ShapeDtypeStruct((tokens, share), jnp.bfloat16)
+    wide_out = jax.ShapeDtypeStruct((tokens, width), jnp.bfloat16)
+    return pl.pallas_call(
+        hidden_layer_kernel,
+        grid=(tokens // tile,),
+        in_specs=[wide, wide] + weights + [down],
+        out_specs=[thin, thin, thin, wide, wide],
+        out_shape=[thin_out] * 3 + [wide_out] * 2,
+        compiler_params=pltpu.CompilerParams(vmem_limit_bytes=56 * 1024 * 1024),
+        cost_estimate=pl.CostEstimate(
+            flops=16 * tokens * width * share, bytes_accessed=30_000_000, transcendentals=0
+        ),
+    )(normed, cot, pair, pair, down_weight)
 
 
 def local(
@@ -821,13 +1097,11 @@
     bias = jnp.where(visible, 0.0, -1e30).astype(jnp.float32)
     cosine, sine = turn_tables(position)
 
-    cot_all = lax.all_gather(cotangent[0], "ctx", axis=0, tiled=True)
-
     sizes = (ctx_size, fsdp_size)
     gains = jnp.zeros((own_rows, LANES), jnp.bfloat16)
     gains = gains.at[:, 0].set(attn_gain).at[:, 1].set(mlp_gain)
     (kv_all,) = gather_front(
-        (jnp.concatenate([key_weight, value_weight, gains], axis=1),), None, None, None, sizes, 1
+        (jnp.concatenate([key_weight, value_weight, gains], axis=1),), None, None, None, None, sizes, 1
     )
     kv_all = kv_all.reshape(D, -1)
     gain_one = kv_all[:, 2 * kv_width].astype(jnp.float32)
@@ -840,79 +1114,45 @@
     key_low = rope(kv_front[:, :kv_width], cosine, sine).astype(jnp.bfloat16)
     value_low = kv_front[:, kv_width : 2 * kv_width].astype(jnp.bfloat16)
     own_pair = jnp.concatenate([key_low, value_low], axis=1)
-    query_all, out_all, pair_all, down_own = gather_front(
-        (after(query_weight, own_pair), out_weight),
-        jnp.stack([gate_weight, up_weight]),
-        down_weight, cot_all, sizes, 6,
-    )
-    down_own = down_own.reshape(ff_own, D)
+    query_all, out_all, pair_all, down_own, cot_all, window = gather_front(
+        (query_weight, out_weight), jnp.stack([gate_weight, up_weight]), down_weight,
+        cotangent[0], own_pair, sizes, 6,
+    )
+    cot_all = cot_all.reshape(ctx_size * tok_rows, D)
     query_all = query_all.reshape(D, D)
     out_all = out_all.reshape(D, D)
-    blocks = [own_pair]
-    for step in range(1, reach_blocks + 1):
-        blocks.insert(0, passed_along(own_pair, "ctx", step))
-    window = jnp.concatenate(blocks, axis=0)
+    down_own = down_own.reshape(ff_own, D)
+    window = window.reshape(-1, 2 * kv_width)
     key_window, value_window = window[:, :kv_width], window[:, kv_width:]
     query_front = product(normed_one, query_all)
     attn_mix, query_low, log_total = attend_forward(
         query_front, key_window, value_window, bias, cosine, sine
     )
-    resid = stream + product(attn_mix, out_all)
-    inv_two = lax.rsqrt(jnp.mean(resid * resid, axis=1, keepdims=True) + EPS)
-    normal_two = resid * inv_two
-    normed_two = (normal_two * gain_two).astype(jnp.bfloat16)
-
-    normed_all = lax.all_gather(normed_two, "ctx", axis=0, tiled=True)
-    pair = gather_hidden(after(pair_all, normed_two), sizes)
+    resid, normed_two = out_norm(attn_mix, out_all, tokens[0], gain_two[None])
+    pair, normed_all = gather_hidden(pair_all, normed_two, sizes)
     pair = pair.reshape(2, D, ff_own)
-    gate_own, up_own = pair[0], pair[1]
-    gate_sum = product(normed_all, gate_own)
-    up_sum = product(normed_all, up_own)
-    sigmoid_gate = jax.nn.sigmoid(gate_sum)
-    silu_gate = gate_sum * sigmoid_gate
-    hidden = (silu_gate * up_sum).astype(jnp.bfloat16)
-    down_part = product(hidden, down_own).astype(jnp.bfloat16)
-    grad_hidden = against(cot_all, down_own)
-    grad_gate_low = (
-        grad_hidden * up_sum * sigmoid_gate * (1.0 + gate_sum * (1.0 - sigmoid_gate))
-    ).astype(jnp.bfloat16)
-    grad_up_low = (grad_hidden * silu_gate).astype(jnp.bfloat16)
-    columns_part = against(grad_gate_low, gate_own) + against(grad_up_low, up_own)
-    half = D // 2
-    first_sum = lax.psum_scatter(
-        down_part[:, :half], "ctx", scatter_dimension=0, tiled=True
-    )
-    columns = lax.psum_scatter(
-        after(columns_part.astype(jnp.bfloat16), first_sum), "ctx", scatter_dimension=0, tiled=True
-    )
+    normed_all = normed_all.reshape(ctx_size * tok_rows, D)
+    hidden, grad_gate_low, grad_up_low, down_part, columns = hidden_layer(
+        normed_all, cot_all, pair, down_own
+    )
+    columns = lax.psum_scatter(columns, "ctx", scatter_dimension=0, tiled=True)
+    pair_sum, down_part = reduce_hidden(normed_all, grad_gate_low, grad_up_low, down_part, sizes)
     down_terms = across(hidden, cot_all).astype(jnp.bfloat16)
-    pair_sum = reduce_hidden(
-        normed_all, after(grad_gate_low, down_terms), grad_up_low, sizes
-    )
-    grad_down = lax.psum_scatter(
-        after(down_terms, columns, pair_sum), "fsdp", scatter_dimension=0, tiled=True
-    )
-    second_sum = lax.psum_scatter(
-        after(down_part[:, half:], grad_down), "ctx", scatter_dimension=0, tiled=True
-    )
-    down_sum = jnp.concatenate([first_sum, second_sum], axis=1)
-    columns = columns.astype(jnp.float32)
-    mixed = (resid + down_sum.astype(jnp.float32)).astype(jnp.bfloat16)
-
+    down_sum = lax.psum_scatter(down_part, "ctx", scatter_dimension=0, tiled=True)
+    grad_resid, grad_resid_low, grad_mix_low, mlp_gain_local = norm_back_mix(
+        columns, resid, gain_two[None], cotangent[0], out_all
+    )
+    grad_query_low, grad_key_window, grad_value_window = attend_backward(
+        query_low, key_window, value_window, grad_mix_low, attn_mix, log_total, bias, cosine, sine,
+        pair_sum,
+    )
+    wide_grad, pair_sum, down_terms = reduce_rows(
+        jnp.stack([normed_one.T, attn_mix.T]),
+        jnp.concatenate([grad_query_low, grad_resid_low], axis=1),
+        None, (pair_sum, down_terms), 512, sizes, 4,
+    )
+    grad_down = lax.psum_scatter(down_terms, "fsdp", scatter_dimension=0, tiled=True)
     pair_sum = lax.all_to_all(pair_sum, "ctx", split_axis=0, concat_axis=0, tiled=True)
-    grad_stream = cotangent[0].astype(jnp.float32)
-    mlp_gain_local = jnp.sum(columns * normal_two, axis=0)
-    grad_resid = grad_stream + norm_back(columns * gain_two, normal_two, inv_two)
-    grad_resid_low = grad_resid.astype(jnp.bfloat16)
-    grad_mix_low = against(grad_resid_low, out_all).astype(jnp.bfloat16)
-    grad_query_low, grad_key_window, grad_value_window = attend_backward(
-        query_low, key_window, value_window, grad_mix_low, attn_mix, log_total, bias, cosine, sine
-    )
-    wide_grad = reduce_rows(
-        jnp.stack([normed_one.T, attn_mix.T]),
-        after(jnp.concatenate([grad_query_low, grad_resid_low], axis=1), second_sum),
-        None, 512, sizes, 4,
-    )
     own_start = reach_blocks * tok_rows
     grad_pair = jnp.concatenate([grad_key_window, grad_value_window], axis=1)
     grad_pair_total = after(grad_pair[own_start:], wide_grad)
@@ -928,10 +1168,14 @@
         jnp.pad(kv_low, ((0, 0), (0, LANES))), kv_all
     )
     attn_gain_local = jnp.sum(grad_normed_one * normal_one, axis=0)
-    gain_terms = jnp.stack([attn_gain_local, mlp_gain_local], axis=1).astype(jnp.bfloat16)
+    gain_terms = jnp.stack([attn_gain_local, mlp_gain_local[0]], axis=1).astype(jnp.bfloat16)
     gain_terms = jnp.pad(gain_terms, ((0, 0), (0, 2 * LANES - 2)))[None]
-    kv_grad = reduce_rows(normed_one.T[None], kv_low, gain_terms, 2 * LANES, sizes, 5)
+    (kv_grad,) = reduce_rows(
+        normed_one.T[None], kv_low, gain_terms, (), 2 * LANES, sizes, 5
+    )
     pair_sum = after(pair_sum, kv_grad)
+    mixed = after(resid, kv_grad) + after(down_sum, kv_grad).astype(jnp.float32)
+    mixed = mixed.astype(jnp.bfloat16)
     pair_sum = pair_sum.transpose(1, 2, 0, 3).reshape(2, own_rows, FF).astype(jnp.float32)
     grad_input = grad_resid + norm_back(grad_normed_one * gain_one, normal_one, inv_one)
     return (

time: 904 us -> 839 us (0.928)
  Pallas kernels: 524 us -> 697 us
  matrix products: 139 us -> 35.3 us
  waiting for transfers between devices: 90 us -> 0.4 us
  local copies, waits for them, and re-layouts: 67.7 us -> 40.5 us
  starting transfers between devices: 25.1 us -> 10.3 us
    pallas_call x1 -> x4, Pallas kernels: 71 us -> 178 us  [the longest x1 105 us: gather_hidden(): pl.pallas_call(functools.partial(hidden_kernel, sizes, pieces), in_specs=...]
    dot_general x6 -> x2, matrix products: 71.7 us -> 9.6 us  [against(): lax.dot_general(left, right, (((1,), (1,)), ((), ())), preferred_element_...]
    pallas_call x2, Pallas kernels: 177 us -> 230 us  [gather_front(): pl.pallas_call(functools.partial(front_kernel, sizes, len(parts), paired)...]
    ppermute x8 -> x4, waiting for transfers between devices: 42.7 us -> 0.01 us  [passed_along(): return lax.ppermute(x, axis, pairs)]
    reduce_scatter x4 -> x3, waiting for transfers between devices: 42.8 us -> 0.33 us  [the longest x1 0.33 us: local(): columns = lax.psum_scatter(columns, 'ctx', scatter_dimension=0, tiled=True)]
    dot_general x6 -> x2, matrix products: 53.2 us -> 11.2 us  [product(): return jnp.dot(left, right, preferred_element_type=jnp.float32)]
    pallas_call x2, Pallas kernels: 147 us -> 164 us  [reduce_rows(): pl.pallas_call(functools.partial(reduce_kernel, sizes, chunk, products, e...]
    ppermute x8 -> x4, starting transfers between devices: 20.3 us -> 5.42 us  [passed_along(): return lax.ppermute(x, axis, pairs)]
  transfers between devices with their start and end apart: 15 -> 8, of which waited for: 6 -> 1; matrix products, arithmetic and copies ran while one was open for 16% -> 8% of each run, Pallas kernels for 41% -> 33%
where the time goes in v3:
time: 839 us; the launch traced here: 831 us
  Pallas kernels  697 us (83%)
  local copies, waits for them, and re-layouts  40.5 us (5%)
  matrix products  35.3 us (4%)
  other arithmetic  33.5 us (4%)
  between operations  15 us (2%)
  starting transfers between devices  10.3 us (1%)
    pallas_call x2, Pallas kernels, gather_front(): pl.pallas_call(functools.partial(front_kernel, sizes, len(parts), paired)...  230 us
    pallas_call x2, Pallas kernels, reduce_rows(): pl.pallas_call(functools.partial(reduce_kernel, sizes, chunk, products, e...  164 us
    pallas_call x1, Pallas kernels, gather_hidden(): pl.pallas_call(functools.partial(hidden_kernel, sizes, pieces), in_specs=...  105 us
    pallas_call x1, Pallas kernels, reduce_hidden(): pl.pallas_call(functools.partial(hidden_grad_kernel, sizes), in_specs=[vm...  74 us
    pallas_call x1, Pallas kernels, hidden_layer(): pl.pallas_call(hidden_layer_kernel, grid=(tokens // tile,), in_specs=[wid...  62.4 us
    pallas_call x1, Pallas kernels, attend_backward(): pl.pallas_call(attend_backward_kernel, grid=(steps,), in_specs=[wide, tal...  30 us
    unnamed x105, local copies, waits for them, and re-layouts  21.9 us
    pallas_call x1, Pallas kernels, attend_forward(): pl.pallas_call(attend_forward_kernel, grid=(steps,), in_specs=[pl.BlockSp...  19.7 us
  transfers between devices with their start and end apart: 8, of which 1 were waited for; matrix products, arithmetic and copies ran while one was open for 8% of the time, Pallas kernels for 33%

profile of v3, /device:TPU:0, one launch (start us, length us, event | category | flops | bytes accessed | tf_op | source)
XLA Modules:
  0.0 831.5 jit_solution(13720643827912539194)
XLA Ops:
  8.5 1.3 fusion.29
  9.9 1.3 fusion.30
  11.5 1.5 pad_maximum_fusion.5.refs_0_
  13.1 37.3 %shard_map.203 = bf16[4,2,4,64,1152]{4,3,2,1,0:T(8,128)(2,1)} custom-call(bf16[64,1152]{1,0:T(8,128)(2,1)} %pad_maximum_fusion.5.refs_0_), custom_call_target="tpu_custom_call" | custom-call | flops 89999998976 | bytes 1000000 | tf_op jit(solution)/shard_map/pallas_call | solution.py:541
  50.3 2.3 fusion.34
  53.9 4.0 fusion.26
  57.9 0.9 copy-done.30
  60.3 0.9 fusion.33
  62.1 1.3 fusion.23
  63.4 0.9 pad_maximum_fusion.3.refs_5_
  64.3 1.5 pad_maximum_fusion.refs_2_
  65.8 0.9 broadcast_in_dim.37.refs_6_
  66.6 193.2 %shard_map.204 = (bf16[4,2,4,64,2048]{4,3,2,1,0:T(8,128)(2,1)}, bf16[4,2,4,64,2048]{4,3,2,1,0:T(8,128)(2,1)}, bf16[2,8,4,64,1024]{4,3,2,1,0:T(8,128)(2,1)}, bf16...) custom-call(bf16[64,2048]{1,0:T(8,128)(2,1)} %refs_0_.1, ...), custom_call_target="tpu_custom_call" | custom-call | flops 89999998976 | bytes 1000000 | tf_op jit(solution)/shard_map/pallas_call | solution.py:541
  259.9 7.2 fusion.24.q_ref
  267.4 1.7 copy.114
  269.1 1.9 fusion.14.bias_ref
  271.0 19.7 %shard_map.205 = (bf16[256,2048]{1,0:T(8,128)(2,1)S(1)}, bf16[256,2048]{1,0:T(8,128)(2,1)S(1)}, f32[32,256]{1,0:T(8,128)S(1)}) custom-call(f32[256,2048]{1,0:T(8,128)} %fusion.24.q_ref, bf16[1280,512]{1,0:T(8,128)(2,1)S(1)} %get-tuple-element.173.k_ref, bf16[1280,512]{1,0:T(8,128)(2,1)S(1)} %get-tuple-element.172.v_ref, f32[1280,256]{1,0:T(8,128)} %fusion.14.bias_ref, ...), custom_call_target="tpu_custom_call" | custom-call | flops 40000000000 | bytes 10000000 | tf_op jit(solution)/shard_map/pallas_call | solution.py:124
  290.8 1.9 copy-done.1
  292.7 4.0 shard_map.206
  296.8 1.0 copy-done.16
  297.7 104.6 %shard_map.207 = (bf16[2,8,4,64,1024]{4,3,2,1,0:T(8,128)(2,1)}, bf16[4,2,256,2048]{3,2,1,0:T(8,128)(2,1)}) custom-call(bf16[2,8,4,64,1024]{4,3,2,1,0:T(8,128)(2,1)} %get-tuple-element.75.pair_in, bf16[256,2048]{1,0:T(8,128)(2,1)} %copy-done.16), custom_call_target="tpu_custom_call", output_to_operand_aliasing={{0}: (0, {})} | custom-call | flops 89999998976 | bytes 30000000 | tf_op jit(solution)/shard_map/pallas_call | solution.py:603
  402.3 62.4 %shard_map.208 = (bf16[2048,1024]{1,0:T(8,128)(2,1)}, bf16[2048,1024]{1,0:T(8,128)(2,1)}, bf16[2048,1024]{1,0:T(8,128)(2,1)}, bf16[2048,2048]{1,0:T(8,128)(2,1)}, bf16[2048,2048]{1,0:T(8,128)(2,1)}) custom-call(bf16[2048,2048]{1,0:T(8,128)(2,1)} %bitcast.138, bf16[2048,2048]{1,0:T(8,128)(2,1)} %bitcast.134, bf16[2,2048,1024]{2,1,0:T(8,128)(2,1)} %bitcast.136, ...), custom_call_target="tpu_custom_call" | custom-call | flops 68719476736 | bytes 30000000 | tf_op jit(solution)/shard_map/pallas_call | solution.py:1045
  464.8 74.0 %shard_map.210 = (bf16[8,2,64,1024]{3,2,1,0:T(8,128)(2,1)}, bf16[2048,2048]{1,0:T(8,128)(2,1)}) custom-call(bf16[2048,2048]{1,0:T(8,128)(2,1)} %bitcast.139, bf16[2048,1024]{1,0:T(8,128)(2,1)} %get-tuple-element.84.gate, bf16[2048,1024]{1,0:T(8,128)(2,1)} %get-tuple-element.85.up, ...), custom_call_target="tpu_custom_call", output_to_operand_aliasing={{1}: (3, {})} | custom-call | flops 60000002048 | bytes 30000000 | tf_op jit(solution)/shard_map/pallas_call | solution.py:909
  538.8 1.2 copy-done.3
  540.0 1.3 copy.100
  541.3 1.6 fusion.18.lefts
  542.9 14.6 %convolution_convert_fusion.refs_1_ = bf16[1024,2048]{1,0:T(8,128)(2,1)} fusion(bf16[2048,1024]{1,0:T(8,128)(2,1)} %get-tuple-element.92, bf16[2048,2048]{1,0:T(8,128)(2,1)} %bitcast.135), kind=kOutput, calls=%fused_computation.1 | convolution fusion | flops 8592031744 | bytes 16777216 | tf_op jit(solution)/shard_map/dot_general | solution.py:40
  557.5 1.5 pad_maximum_fusion.1.lefts
  559.3 1.2 copy-done.8
  560.6 1.2 copy-done.9
  561.8 7.5 shard_map.209
  569.3 1.3 copy-done.4
  570.6 30.0 %shard_map.211 = (bf16[256,2048]{1,0:T(8,128)(2,1)S(1)}, f32[1280,512]{1,0:T(8,128)}, f32[1280,512]{1,0:T(8,128)}) custom-call(bf16[256,2048]{1,0:T(8,128)(2,1)S(1)} %copy-done.18, bf16[1280,512]{1,0:T(8,128)(2,1)S(1)} %copy-done.7, bf16[1280,512]{1,0:T(8,128)(2,1)} %copy-done.5, bf16[256,2048]{1,0:T(8,128)(2,1)S(1)} %get-tuple-element.82.do_ref, ...), custom_call_target="tpu_custom_call" | custom-call | flops 80000000000 | bytes 20000000 | tf_op jit(solution)/shard_map/pallas_call | solution.py:217
  600.6 2.2 constant_dynamic-update-slice_fusion.1
  604.0 1.4 fusion.36
  605.4 1.5 collective-permute-start
  607.0 1.3 collective-permute-start.1
  608.3 1.3 collective-permute-start.2
  609.6 1.3 collective-permute-start.3
  610.9 1.5 pad_maximum_fusion.2.right
  612.4 3.8 fusion.40
  616.8 113.7 %shard_map.212 = (f32[64,4096]{1,0:T(8,128)}, bf16[8,2,64,1024]{3,2,1,0:T(8,128)(2,1)}, bf16[1024,2048]{1,0:T(8,128)(2,1)}) custom-call(bf16[2,2048,256]{2,1,0:T(8,128)(2,1)} %pad_maximum_fusion.1.lefts, bf16[256,4096]{1,0:T(8,128)(2,1)} %pad_maximum_fusion.2.right, ...), custom_call_target="tpu_custom_call", output_to_operand_aliasing={{1}: (3, {}), {2}: (4, {})} | custom-call | flops 80000000000 | bytes 30000000 | tf_op jit(solution)/shard_map/pallas_call | solution.py:807
  730.6 1.0 slice.129
  731.6 4.7 all-to-all-start
  736.4 2.9 copy.106
  739.3 2.4 fusion.38
  741.7 1.9 convert_add_fusion
  743.7 0.9 copy-done.22
  744.9 1.0 copy.102
  746.0 2.0 fusion.21
  748.1 0.8 copy-done.44
  749.0 5.8 fusion.6
  754.8 1.1 copy.105
  755.9 2.2 pad_bitcast_fusion.extra
  758.1 50.3 %shard_map.213 = f32[64,1280]{1,0:T(8,128)} custom-call(bf16[1,2048,256]{2,1,0:T(8,128)(2,1)} %copy-done.26, bf16[256,1024]{1,0:T(8,128)(2,1)} %copy-done.33, bf16[1,2048,256]{2,1,0:T(8,128)(2,1)} %pad_bitcast_fusion.extra), custom_call_target="tpu_custom_call" | custom-call | flops 80000000000 | bytes 30000000 | tf_op jit(solution)/shard_map/pallas_call | solution.py:807
  808.5 1.5 fusion.17
  810.0 2.3 copy.109
  812.3 0.7 slice_reduce_fusion
  813.0 0.7 fusion.39
  813.7 2.5 fusion.16
  816.2 2.0 convert_bitcast_fusion
  818.7 1.5 copy.118
  820.2 1.6 copy.119
  821.7 2.8 convert_element_type.124
  (149 shorter events, 8.8 us)
Async XLA Ops:
  7.2 552.1 %reduce-scatter.4.cloned.1.call-start = ((), (), s32[]{:S(2)}) async-start(), calls=%async_computation.4 | async-start | bytes 9437184 | tf_op jit(solution)/shard_map/reduce_scatter | solution.py:1138
  50.3 2.7 copy-start
  53.0 206.8 %copy-start.36 = (f32[2048,1]{0,1:T(1,128)}, f32[2048,1]{0,1:T(1,128)S(1)}, u32[]{:S(2)}) copy-start(f32[2048,1]{0,1:T(1,128)S(1)} %copy.120) | copy-start | bytes 24580
  53.5 6.0 copy-start.19
  53.9 206.0 %copy-start.39 = (f32[256]{0:T(256)}, f32[256]{0:T(256)S(1)}, u32[]{:S(2)}) copy-start(f32[256]{0:T(256)S(1)} %add_rsqrt_fusion) | copy-start | bytes 3076
  53.9 5.1 copy-start.43
  57.8 1.0 copy-start.30
  61.2 209.7 %copy-start.10 = (f32[256,128]{1,0:T(8,128)}, f32[256,128]{1,0:T(8,128)S(1)}, u32[]{:S(2)}) copy-start(f32[256,128]{1,0:T(8,128)S(1)} %get-tuple-element.163.sin_ref) | copy-start | bytes 393220
  61.3 209.7 %copy-start.12 = (f32[256,128]{1,0:T(8,128)}, f32[256,128]{1,0:T(8,128)S(1)}, u32[]{:S(2)}) copy-start(f32[256,128]{1,0:T(8,128)S(1)} %get-tuple-element.182.cos_ref) | copy-start | bytes 393220
  61.3 0.8 copy-start.23
  61.4 2.9 copy-start.31
  61.4 2.9 copy-start.32
  259.9 7.2 copy-start.28
  267.3 23.4 %copy-start.5 = (bf16[1280,512]{1,0:T(8,128)(2,1)}, bf16[1280,512]{1,0:T(8,128)(2,1)S(1)}, u32[]{:S(2)}) copy-start(bf16[1280,512]{1,0:T(8,128)(2,1)S(1)} %get-tuple-element.172.v_ref) | copy-start | bytes 3932164
  267.3 23.4 %copy-start.6 = (bf16[1280,512]{1,0:T(8,128)(2,1)}, bf16[1280,512]{1,0:T(8,128)(2,1)S(1)}, u32[]{:S(2)}) copy-start(bf16[1280,512]{1,0:T(8,128)(2,1)S(1)} %get-tuple-element.173.k_ref) | copy-start | bytes 3932164
  269.1 21.7 %copy-start.14 = (f32[1,2048]{1,0:T(1,128)}, f32[1,2048]{1,0:T(1,128)S(1)}, u32[]{:S(2)}) copy-start(f32[1,2048]{1,0:T(1,128)S(1)} %bitcast_convert_fusion.gain) | copy-start | bytes 24580
  271.0 19.8 %slice-start = ((s8[8388608]{0:T(1024)(128)(4,1)}), s8[4194304]{0:T(1024)(128)(4,1)S(1)}, s32[]{:S(2)}) async-start(s8[8388608]{0:T(1024)(128)(4,1)} %bitcast.97), calls=%async_computation.7 | async-start | bytes 8388608
  271.0 19.8 %slice-start.1 = ((s8[8388608]{0:T(1024)(128)(4,1)}), s8[4194304]{0:T(1024)(128)(4,1)S(1)}, s32[]{:S(2)}) async-start(s8[8388608]{0:T(1024)(128)(4,1)} %bitcast.97), calls=%async_computation.8 | async-start | bytes 8388608
  290.7 6.0 copy-start.2
  290.7 6.0 copy-start.17
  290.8 2.0 copy-start.1
  296.7 1.0 copy-start.16
  464.7 347.5 %reduce-scatter.6.cloned.1.call-start = ((), (), s32[]{:S(2)}) async-start(), calls=%async_computation.5 | async-start | bytes 9437184 | tf_op jit(solution)/shard_map/reduce_scatter | solution.py:1141
  538.8 1.3 copy-start.3
  540.0 1.3 copy-start.37
  540.0 1.3 copy-start.40
  542.9 14.6 %copy-start.26 = (bf16[1,2048,256]{2,1,0:T(8,128)(2,1)}, bf16[1,2048,256]{2,1,0:T(8,128)(2,1)S(1)}, u32[]{:S(2)}) copy-start(bf16[1,2048,256]{2,1,0:T(8,128)(2,1)S(1)} %fusion.18.lefts) | copy-start | bytes 3145732
  542.9 14.6 %copy-start.25 = (bf16[256,2048]{0,1:T(8,128)(2,1)S(1)}, bf16[256,2048]{0,1:T(8,128)(2,1)}, u32[]{:S(2)}) copy-start(bf16[256,2048]{0,1:T(8,128)(2,1)} %copy.100) | copy-start | bytes 3145732
  557.5 1.8 copy-start.15
  559.3 1.2 copy-start.8
  560.5 1.2 copy-start.9
  561.8 8.8 %copy-start.7 = (bf16[1280,512]{1,0:T(8,128)(2,1)S(1)}, bf16[1280,512]{1,0:T(8,128)(2,1)}, u32[]{:S(2)}) copy-start(bf16[1280,512]{1,0:T(8,128)(2,1)} %copy-done.6) | copy-start | bytes 3932164
  561.8 8.8 %copy-start.11 = (f32[256,128]{1,0:T(8,128)S(1)}, f32[256,128]{1,0:T(8,128)}, u32[]{:S(2)}) copy-start(f32[256,128]{1,0:T(8,128)} %copy-done.10) | copy-start | bytes 393220
  561.8 8.8 %copy-start.13 = (f32[256,128]{1,0:T(8,128)S(1)}, f32[256,128]{1,0:T(8,128)}, u32[]{:S(2)}) copy-start(f32[256,128]{1,0:T(8,128)} %copy-done.12) | copy-start | bytes 393220
  561.8 8.8 %copy-start.18 = (bf16[256,2048]{1,0:T(8,128)(2,1)S(1)}, bf16[256,2048]{1,0:T(8,128)(2,1)}, u32[]{:S(2)}) copy-start(bf16[256,2048]{1,0:T(8,128)(2,1)} %copy-done.17) | copy-start | bytes 3145732
  569.3 1.3 copy-start.4
  600.6 2.6 copy-start.27
  603.6 8.8 %slice-start.2 = ((s8[8388608]{0:T(1024)(128)(4,1)}), s8[4194304]{0:T(1024)(128)(4,1)S(1)}, s32[]{:S(2)}) async-start(s8[8388608]{0:T(1024)(128)(4,1)} %bitcast.131), calls=%async_computation.9 | async-start | bytes 8388608
  604.0 8.4 %slice-start.3 = ((s8[8388608]{0:T(1024)(128)(4,1)}), s8[4194304]{0:T(1024)(128)(4,1)S(1)}, s32[]{:S(2)}) async-start(s8[8388608]{0:T(1024)(128)(4,1)} %bitcast.131), calls=%async_computation.10 | async-start | bytes 8388608
  605.4 136.2 %collective-permute-start = (bf16[256,1024]{1,0:T(8,128)(2,1)}, bf16[256,1024]{1,0:T(8,128)(2,1)}, u32[]{:S(2)}, u32[]{:S(2)}) collective-permute-start(bf16[256,1024]{1,0:T(8,128)(2,1)} %get-tuple-element.168), channel_id=1, source_target_pairs={{4,0},{8,4},{12,8},{16,12},{20,16},{24,20},{28,24},{5,1},{9,5},{13... | collective-permute-start | bytes 1572872 | tf_op jit(solution)/shard_map/ppermute | solution.py:26
  607.0 134.7 %collective-permute-start.1 = (bf16[256,1024]{1,0:T(8,128)(2,1)}, bf16[256,1024]{1,0:T(8,128)(2,1)}, u32[]{:S(2)}, u32[]{:S(2)}) collective-permute-start(bf16[256,1024]{1,0:T(8,128)(2,1)} %get-tuple-element.171), channel_id=1, source_target_pairs={{8,0},{12,4},{16,8},{20,12},{24,16},{28,20},{9,1},{13,5},{17,9},{2... | collective-permute-start | bytes 1572872 | tf_op jit(solution)/shard_map/ppermute | solution.py:26
  608.3 133.4 %collective-permute-start.2 = (bf16[256,1024]{1,0:T(8,128)(2,1)}, bf16[256,1024]{1,0:T(8,128)(2,1)}, u32[]{:S(2)}, u32[]{:S(2)}) collective-permute-start(bf16[256,1024]{1,0:T(8,128)(2,1)} %get-tuple-element.170), channel_id=1, source_target_pairs={{12,0},{16,4},{20,8},{24,12},{28,16},{13,1},{17,5},{21,9},{25,13},... | collective-permute-start | bytes 1572872 | tf_op jit(solution)/shard_map/ppermute | solution.py:26
  609.6 132.1 %collective-permute-start.3 = (bf16[256,1024]{1,0:T(8,128)(2,1)}, bf16[256,1024]{1,0:T(8,128)(2,1)}, u32[]{:S(2)}, u32[]{:S(2)}) collective-permute-start(bf16[256,1024]{1,0:T(8,128)(2,1)} %get-tuple-element.169), channel_id=1, source_target_pairs={{16,0},{20,4},{24,8},{28,12},{17,1},{21,5},{25,9},{29,13},{18,2},{... | collective-permute-start | bytes 1572872 | tf_op jit(solution)/shard_map/ppermute | solution.py:26
  731.6 84.6 %all-to-all-start = ((bf16[8,2,64,1024]{3,2,1,0:T(8,128)(2,1)}), bf16[8,2,64,1024]{3,2,1,0:T(8,128)(2,1)}, u32[]{:S(2)}, u32[]{:S(2)}) async-start(bf16[8,2,64,1024]{3,2,1,0:T(8,128)(2,1)} %get-tuple-element.100), calls=%async_computation.2 | async-start | bytes 4194304 | tf_op jit(solution)/shard_map/all_to_all | solution.py:1155
  736.4 85.4 %reduce-scatter.8.cloned.1.call-start = ((), (), s32[]{:S(2)}) async-start(), calls=%async_computation.6 | async-start | bytes 5242880 | tf_op jit(solution)/shard_map/reduce_scatter | solution.py:1154
  739.3 2.4 copy-start.24
  743.6 1.0 copy-start.22
  744.6 1.3 copy-start.34
  745.9 2.2 copy-start.20
  745.9 2.2 copy-start.38
  745.9 2.3 copy-start.41
  745.9 3.1 copy-start.44
  749.0 5.8 copy-start.33
  758.1 50.3 %copy-start.21 = (f32[256,2048]{0,1:T(8,128)S(1)}, f32[256,2048]{0,1:T(8,128)}, u32[]{:S(2)}) copy-start(f32[256,2048]{0,1:T(8,128)} %copy.106) | copy-start | bytes 6291460
  758.1 50.3 %copy-start.29 = (f32[256,2048]{0,1:T(8,128)S(1)}, f32[256,2048]{0,1:T(8,128)}, u32[]{:S(2)}) copy-start(f32[256,2048]{0,1:T(8,128)} %get-tuple-element.181) | copy-start | bytes 6291460
  758.1 50.3 %copy-start.42 = (f32[256]{0:T(256)S(1)}, f32[256]{0:T(256)}, u32[]{:S(2)}) copy-start(f32[256]{0:T(256)} %copy-done.39) | copy-start | bytes 3076
  810.0 2.3 copy-start.35
Sparse Core Ops, SparseCore 0:
  464.9 94.4 reduce-scatter.3
  561.6 115.8 reduce-scatter.5
  740.2 65.3 reduce-scatter.7

commit v4 on v3

--- a/solution.py
+++ b/solution.py
@@ -79,12 +79,12 @@
 
 
 def attend_forward_kernel(
-    q_ref, k_ref, v_ref, bias_ref, cos_ref, sin_ref, o_ref, qr_ref, lse_ref
+    n_ref, w_ref, k_ref, v_ref, bias_ref, cos_ref, sin_ref, o_ref, qr_ref, lse_ref
 ):
-    rows = q_ref.shape[0]
+    rows = n_ref.shape[0]
     group = HEADS // KV_HEADS
     span = k_ref.shape[0] - rows + QTILE
-    rotated = turn(q_ref[...], cos_ref[...], sin_ref[...])
+    rotated = turn(product(n_ref[...], w_ref[...]), cos_ref[...], sin_ref[...])
     qr_ref[...] = rotated.astype(jnp.bfloat16)
     scaled = (qr_ref[...].astype(jnp.float32) * HEAD_DIM ** (-0.5)).astype(jnp.bfloat16)
     for tile in range(rows // QTILE):
@@ -115,8 +115,8 @@
             )
 
 
-def attend_forward(q, k, v, bias, cosine, sine):
-    rows, width = q.shape
+def attend_forward(normed, weight, k, v, bias, cosine, sine):
+    rows, width = normed.shape[0], weight.shape[1]
     steps = KV_HEADS * HEAD_DIM // LANES
     qw = width // steps
     heads = HEADS // steps
@@ -125,7 +125,8 @@
         attend_forward_kernel,
         grid=(steps,),
         in_specs=[
-            pl.BlockSpec((rows, qw), lambda i: (0, i)),
+            pl.BlockSpec(normed.shape, lambda i: (0, 0)),
+            pl.BlockSpec((weight.shape[0], qw), lambda i: (0, i)),
             pl.BlockSpec((window, LANES), lambda i: (0, i)),
             pl.BlockSpec((window, LANES), lambda i: (0, i)),
             pl.BlockSpec((window, rows), lambda i: (0, 0)),
@@ -144,12 +145,12 @@
         ],
         compiler_params=pltpu.CompilerParams(vmem_limit_bytes=48 * 1024 * 1024),
         cost_estimate=pl.CostEstimate(flops=40_000_000_000, bytes_accessed=10_000_000, transcendentals=0),
-    )(q, k, v, bias, cosine, sine)
+    )(normed, weight, k, v, bias, cosine, sine)
 
 
 def attend_backward_kernel(
-    qr_ref, k_ref, v_ref, do_ref, o_ref, lse_ref, bias_ref, cos_ref, sin_ref, earlier,
-    dq_ref, dk_ref, dv_ref
+    qr_ref, k_ref, v_ref, do_ref, o_ref, lse_ref, bias_ref, cos_ref, sin_ref,
+    carried_in, dq_ref, dk_low, dv_low, dk_own, dv_own, carried, dk_ref, dv_ref
 ):
     rows = qr_ref.shape[0]
     group = HEADS // KV_HEADS
@@ -203,9 +204,14 @@
         dq_ref[first : first + QTILE, :] = turn(
             dq, cos_ref[first : first + QTILE, :], -sin_ref[first : first + QTILE, :]
         ).astype(jnp.bfloat16)
-
-
-def attend_backward(qr, k, v, do, o, lse, bias, cosine, sine, earlier):
+    before = dk_low.shape[0]
+    dk_low[...] = dk_ref[:before, :].astype(jnp.bfloat16)
+    dv_low[...] = dv_ref[:before, :].astype(jnp.bfloat16)
+    dk_own[...] = dk_ref[before:, :]
+    dv_own[...] = dv_ref[before:, :]
+
+
+def attend_backward(qr, k, v, do, o, lse, bias, cosine, sine, carried):
     rows, width = qr.shape
     steps = KV_HEADS * HEAD_DIM // LANES
     qw = width // steps
@@ -224,15 +230,27 @@
             table, table,
             pl.BlockSpec(memory_space=pl.ANY),
         ],
-        out_specs=[wide, tall, tall],
+        out_specs=[
+            wide,
+            pl.BlockSpec((window - rows, LANES), lambda i: (0, i)),
+            pl.BlockSpec((window - rows, LANES), lambda i: (0, i)),
+            pl.BlockSpec((rows, LANES), lambda i: (0, i)),
+            pl.BlockSpec((rows, LANES), lambda i: (0, i)),
+            pl.BlockSpec(memory_space=pl.ANY),
+        ],
         out_shape=[
             jax.ShapeDtypeStruct((rows, width), jnp.bfloat16),
-            jax.ShapeDtypeStruct(k.shape, jnp.float32),
-            jax.ShapeDtypeStruct(k.shape, jnp.float32),
-        ],
+            jax.ShapeDtypeStruct((window - rows, k.shape[1]), jnp.bfloat16),
+            jax.ShapeDtypeStruct((window - rows, k.shape[1]), jnp.bfloat16),
+            jax.ShapeDtypeStruct((rows, k.shape[1]), jnp.float32),
+            jax.ShapeDtypeStruct((rows, k.shape[1]), jnp.float32),
+            jax.ShapeDtypeStruct(carried.shape, carried.dtype),
+        ],
+        input_output_aliases={9: 5},
+        scratch_shapes=[pltpu.VMEM((window, LANES), jnp.float32)] * 2,
         compiler_params=pltpu.CompilerParams(vmem_limit_bytes=48 * 1024 * 1024),
         cost_estimate=pl.CostEstimate(flops=80_000_000_000, bytes_accessed=20_000_000, transcendentals=0),
-    )(qr, k, v, do, o, lse, bias, cosine, sine, earlier)
+    )(qr, k, v, do, o, lse, bias, cosine, sine, carried)
 
 
 def turn_tables(position):
@@ -285,7 +303,12 @@
             arrived.add(name)
             started[name].wait_recv()
 
-    for at, (name, awaited, source, target, peer) in enumerate(copies):
+    for copy in copies:
+        if callable(copy):
+            copy()
+            continue
+        at = len(started)
+        name, awaited, source, target, peer = copy
         for other in awaited:
             arrive(other)
         started[name] = pltpu.make_async_remote_copy(
@@ -342,7 +365,7 @@
     return peers + [(0, 0, m) for m in range(1, fsdp_size)]
 
 
-def front_copies(parts, wholes, pair_ref, pair_all, down_ref, down_all, line, sizes):
+def front_copies(parts, wholes, pair_ref, pair_all, down_ref, down_all, sizes):
     ctx_size, fsdp_size = sizes
     chips = ctx_size // 2
     ctx, fsdp = lax.axis_index("ctx"), lax.axis_index("fsdp")
@@ -428,7 +451,7 @@
                 )
             queues.append(stages)
     sharing = []
-    lag, done = 2, 0
+    lag = 2
     for turn in range(len(queues) + lag * (len(orders[0]) + 1)):
         for stage in range(len(orders[0]) + 1):
             at = turn - lag * stage
@@ -436,25 +459,18 @@
                 sharing.extend(queues[at][stage])
         if turn == chips:
             sharing.extend(exchange)
-            for hop in line[:1]:
-                sharing.extend(hop)
-        if turn > chips and (turn - chips) % 4 == 0 and (turn - chips) // 4 < len(line) - 1:
-            sharing.extend(line[(turn - chips) // 4])
-            done = (turn - chips) // 4
-    for hop in line[done + 1 :]:
-        sharing.extend(hop)
-    return copies + sharing
+    return copies, sharing
 
 
 def front_kernel(sizes, count, paired, *refs):
     parts, refs = refs[:count], refs[count:]
     if paired:
-        pair_ref, down_ref, cot_ref, kv_ref, zero_ref, *refs = refs
+        pair_ref, down_ref, kv_ref, zero_ref, cot_in, *refs = refs
     else:
         pair_ref = down_ref = None
     wholes, refs = refs[:count], refs[count:]
     if paired:
-        pair_all, down_all, cot_all, window, *refs = refs
+        pair_all, down_all, window, cot_out, *refs = refs
     else:
         pair_all = down_all = None
     send_sems, recv_sems, own_sems, halo_send, halo_recv = refs
@@ -473,7 +489,6 @@
                 device_id_type=pl.DeviceIdType.MESH,
             )
             halos.append((step, copy))
-            pl.when(ctx + step < sizes[0])(copy.start)
     kept = []
     for n, (own, whole) in enumerate(zip(parts, wholes)):
         kept.append(
@@ -487,22 +502,25 @@
             (
                 (pair_ref.at[:, :, columns], pair_all.at[:, ctx, fsdp]),
                 (down_ref, down_all.at[fsdp]),
-                (cot_ref, cot_all.at[ctx // 2, ctx % 2]),
                 (kv_ref, window.at[reach]),
             )
         ):
             kept.append(pltpu.make_async_copy(source, target, own_sems.at[count + n]))
         for step in range(1, reach + 1):
             copy = pltpu.make_async_copy(
-                zero_ref, window.at[reach - step], own_sems.at[count + 3 + step]
+                zero_ref, window.at[reach - step], own_sems.at[count + 2 + step]
             )
             empty.append((step, copy))
     for copy in kept:
         copy.start()
     for step, copy in empty:
         pl.when(ctx - step < 0)(copy.start)
-    line = line_gather("cot", cot_ref, cot_all, sizes) if paired else []
-    copies = front_copies(parts, wholes, pair_ref, pair_all, down_ref, down_all, line, sizes)
+    copies, sharing = front_copies(
+        parts, wholes, pair_ref, pair_all, down_ref, down_all, sizes
+    )
+    for step, copy in halos:
+        copies.append(lambda step=step, copy=copy: pl.when(ctx + step < sizes[0])(copy.start))
+    copies += sharing
     run_copies(copies, send_sems, recv_sems)
     for copy in kept:
         copy.wait()
@@ -527,22 +545,22 @@
     ]
     arrays = list(parts)
     if paired:
-        count += ctx_size - 1 + 2 * (fsdp_size - 1) + 2 * chips - 1
+        count += ctx_size - 1 + 2 * (fsdp_size - 1)
         columns = pair.shape[2] // ctx_size
         shapes += [
             jax.ShapeDtypeStruct((2, ctx_size, fsdp_size, rows, columns), pair.dtype),
             jax.ShapeDtypeStruct((fsdp_size,) + down.shape, down.dtype),
-            jax.ShapeDtypeStruct((chips, 2) + cot.shape, cot.dtype),
             jax.ShapeDtypeStruct((reach + 1,) + key_value.shape, key_value.dtype),
         ]
-        arrays += [pair, down, cot, key_value, jnp.zeros_like(key_value)]
+        arrays += [pair, down, key_value, jnp.zeros_like(key_value)]
     hbm = pl.BlockSpec(memory_space=pl.ANY)
     vmem = pl.BlockSpec(memory_space=pltpu.VMEM)
     return pl.pallas_call(
         functools.partial(front_kernel, sizes, len(parts), paired),
-        in_specs=[vmem] * len(arrays),
-        out_specs=[hbm] * len(shapes),
-        out_shape=shapes,
+        in_specs=[vmem] * len(arrays) + [hbm] * paired,
+        out_specs=[hbm] * (len(shapes) + paired),
+        out_shape=shapes + ([jax.ShapeDtypeStruct(cot.shape, cot.dtype)] if paired else []),
+        input_output_aliases={len(arrays): len(shapes)} if paired else {},
         scratch_shapes=[
             pltpu.SemaphoreType.DMA((count,)),
             pltpu.SemaphoreType.DMA((count,)),
@@ -554,7 +572,7 @@
         cost_estimate=pl.CostEstimate(
             flops=90_000_000_000, bytes_accessed=1_000_000, transcendentals=0
         ),
-    )(*arrays)
+    )(*arrays, *([cot] if paired else []))
 
 
 def hidden_kernel(sizes, pieces, pair_in, normed_ref, pair_all, normed_all, send_sems, recv_sems, own_sem):
@@ -576,18 +594,25 @@
         lines.append(
             line_gather(("normed", n), normed_ref.at[strip], normed_all.at[:, :, strip], sizes)
         )
-    copies = [copy for line in lines for copy in line[0]]
+    ready = [[copy for hop in line for copy in hop if not copy[1]] for line in lines]
+    later = [[copy for copy in hop if copy[1]] for line in lines for hop in line]
+    later = [
+        [hop for hop in later[n * len(lines[0]) : (n + 1) * len(lines[0])] if hop]
+        for n in range(pieces)
+    ]
     pair_hops = [
         [copy for pieces in zip(*(hops[n] for hops in lists)) for copy in pieces]
         for n in range(len(masks))
     ]
-    copies += pair_hops[0]
-    depth = len(lines[0])
-    for turn in range(pieces + depth - 2):
-        for stage in range(1, depth):
-            if 0 <= turn - stage + 1 < pieces:
-                copies.extend(lines[turn - stage + 1][stage])
-        if turn == pieces // 2:
+    ahead, depth = 2, len(later[0])
+    copies = [copy for line in ready[:ahead] for copy in line] + pair_hops[0]
+    for turn in range(pieces + depth - 1):
+        for stage in range(depth):
+            if 0 <= turn - stage < pieces:
+                copies.extend(later[turn - stage][stage])
+            if stage == 0 and turn + ahead < pieces:
+                copies.extend(ready[turn + ahead])
+        if turn == 1:
             for hop in pair_hops[1:]:
                 copies.extend(hop)
     run_copies(copies, send_sems, recv_sems)
@@ -638,13 +663,22 @@
     )
 
 
-def reduce_kernel(
-    sizes, chunk, products, extras, carried, lefts, right, extra, *refs
-):
-    total, refs = refs[carried], refs[1 + 2 * carried :]
-    terms, core_got, line_sent, line_got = refs[:4]
-    core_send, core_recv, hop_send, hop_recv, line_send, line_recv = refs[4:10]
-    hop_buffers = refs[10:]
+def reduce_kernel(sizes, chunk, products, extras, halos, swaps, *refs):
+    refs = list(refs)
+
+    def take(amount):
+        taken = refs[:amount]
+        del refs[:amount]
+        return taken
+
+    lefts, right, extra = take(3)
+    sent, swap_in = take(halos), take(swaps)
+    (total,) = take(1)
+    halo_got, swap_out = take(halos), take(swaps)
+    terms, core_got, line_sent, line_got = take(4)
+    core_send, core_recv, hop_send, hop_recv, line_send, line_recv = take(6)
+    halo_send, halo_recv, swap_send, swap_recv, swap_own = take(5)
+    hop_buffers = refs
     ctx_size, fsdp_size = sizes
     chips = ctx_size // 2
     rows = total.shape[0]
@@ -660,11 +694,41 @@
     slots = [hop_slots(fsdp_size, order) for order in orders]
     ctx, fsdp = lax.axis_index("ctx"), lax.axis_index("fsdp")
     chip, side = ctx // 2, ctx % 2
-    greet(
-        [(0, 1, 0)]
-        + [(0, 0, m) for m in masks]
-        + [(1 << bit, 0, 0) for bit in range(chips.bit_length() - 1)]
-    )
+    if halos or swaps:
+        greet(front_masks(ctx_size, fsdp_size, True))
+    else:
+        greet(
+            [(0, 1, 0)]
+            + [(0, 0, m) for m in masks]
+            + [(1 << bit, 0, 0) for bit in range(chips.bit_length() - 1)]
+        )
+    back = []
+    for n in range(halos):
+        reach = halo_got[n].shape[0]
+        rows_of = halo_got[n].shape[1]
+        for step in range(1, reach + 1):
+            copy = pltpu.make_async_remote_copy(
+                src_ref=sent[n].at[pl.ds((reach - step) * rows_of, rows_of)],
+                dst_ref=halo_got[n].at[step - 1],
+                send_sem=halo_send.at[n, step - 1],
+                recv_sem=halo_recv.at[n, step - 1],
+                device_id=(lax.rem(ctx - step + ctx_size, ctx_size), fsdp),
+                device_id_type=pl.DeviceIdType.MESH,
+            )
+            back.append((step, copy))
+            pl.when(ctx - step >= 0)(copy.start)
+    swapped = []
+    for source, target in zip(swap_in, swap_out):
+        swapped.append(pltpu.make_async_copy(source.at[ctx], target.at[ctx], swap_own))
+        for mask in range(1, ctx_size):
+            swapped.append(
+                remote(
+                    source.at[ctx ^ mask], target.at[ctx],
+                    swap_send.at[mask], swap_recv.at[mask], (mask // 2, mask % 2, 0),
+                )
+            )
+    for copy in swapped:
+        copy.start()
 
     def core_copy(i):
         return remote(
@@ -782,9 +846,15 @@
         return carry
 
     lax.fori_loop(0, count, finish, 0)
-
-
-def reduce_rows(lefts, right, extra, carried, chunk, sizes, collective_id):
+    for copy in swapped:
+        copy.wait()
+    for step, copy in back:
+        pl.when(ctx + step < ctx_size)(copy.wait_recv)
+    for step, copy in back:
+        pl.when(ctx - step >= 0)(copy.wait_send)
+
+
+def reduce_rows(lefts, right, extra, halos, swaps, chunk, sizes, collective_id):
     ctx_size, fsdp_size = sizes
     chips = ctx_size // 2
     depth = lefts.shape[1]
@@ -796,6 +866,7 @@
     count = products + extras
     bits = fsdp_size.bit_length() - 1
     half = chunk // 2
+    reach = WINDOW // STRETCH
     buffers = []
     for _ in range(2):
         for j in range(bits):
@@ -805,12 +876,15 @@
     vmem = pl.BlockSpec(memory_space=pltpu.VMEM)
     hbm = pl.BlockSpec(memory_space=pl.ANY)
     return pl.pallas_call(
-        functools.partial(reduce_kernel, sizes, chunk, products, extras, len(carried)),
-        in_specs=[vmem] * 3 + [hbm] * len(carried),
-        out_specs=[vmem] + [hbm] * len(carried),
+        functools.partial(reduce_kernel, sizes, chunk, products, extras, len(halos), len(swaps)),
+        in_specs=[vmem] * 3 + [hbm] * (len(halos) + len(swaps)),
+        out_specs=[vmem] + [hbm] * (len(halos) + len(swaps)),
         out_shape=[jax.ShapeDtypeStruct((rows, count * chunk), jnp.float32)]
-        + [jax.ShapeDtypeStruct(array.shape, array.dtype) for array in carried],
-        input_output_aliases={3 + n: 1 + n for n in range(len(carried))},
+        + [
+            jax.ShapeDtypeStruct((reach, array.shape[0] // reach, array.shape[1]), array.dtype)
+            for array in halos
+        ]
+        + [jax.ShapeDtypeStruct(array.shape, array.dtype) for array in swaps],
         scratch_shapes=[
             pltpu.VMEM((count, chips, 2, fsdp_size, rows, chunk), jnp.bfloat16),
             pltpu.VMEM((count, chips, fsdp_size, rows, chunk), jnp.bfloat16),
@@ -822,13 +896,18 @@
             pltpu.SemaphoreType.DMA((2, bits, count)),
             pltpu.SemaphoreType.DMA((count, chips.bit_length() - 1)),
             pltpu.SemaphoreType.DMA((count, chips.bit_length() - 1)),
+            pltpu.SemaphoreType.DMA((max(len(halos), 1), reach)),
+            pltpu.SemaphoreType.DMA((max(len(halos), 1), reach)),
+            pltpu.SemaphoreType.DMA((ctx_size,)),
+            pltpu.SemaphoreType.DMA((ctx_size,)),
+            pltpu.SemaphoreType.DMA,
         ]
         + buffers,
         compiler_params=pltpu.CompilerParams(
             collective_id=collective_id, has_side_effects=True, vmem_limit_bytes=56 * 1024 * 1024
         ),
         cost_estimate=pl.CostEstimate(flops=80_000_000_000, bytes_accessed=30_000_000, transcendentals=0),
-    )(lefts, right, extra, *carried)
+    )(lefts, right, extra, *halos, *swaps)
 
 
 def hidden_grad_kernel(
@@ -926,6 +1005,33 @@
     )(normed, gate, up, carried)
 
 
+def norm_keys_kernel(stream, gain, weight, cosine, sine, normed_ref, pair_ref):
+    x = stream[...].astype(jnp.float32)
+    inverse = lax.rsqrt(jnp.mean(x * x, axis=1, keepdims=True) + EPS)
+    normed = (x * inverse * gain[...]).astype(jnp.bfloat16)
+    normed_ref[...] = normed
+    front = product(normed, weight[...])
+    kv_width = KV_HEADS * HEAD_DIM
+    keys = turn(front[:, :kv_width], cosine[...], sine[...])
+    pair_ref[:, :kv_width] = keys.astype(jnp.bfloat16)
+    pair_ref[:, kv_width:] = front[:, kv_width : 2 * kv_width].astype(jnp.bfloat16)
+
+
+def norm_keys(stream, gain, weight, cosine, sine):
+    rows = stream.shape[0]
+    return pl.pallas_call(
+        norm_keys_kernel,
+        out_shape=[
+            jax.ShapeDtypeStruct(stream.shape, jnp.bfloat16),
+            jax.ShapeDtypeStruct((rows, 2 * KV_HEADS * HEAD_DIM), jnp.bfloat16),
+        ],
+        compiler_params=pltpu.CompilerParams(vmem_limit_bytes=40 * 1024 * 1024),
+        cost_estimate=pl.CostEstimate(
+            flops=2 * rows * weight.size, bytes_accessed=8_000_000, transcendentals=0
+        ),
+    )(stream, gain, weight, cosine, sine)
+
+
 def out_norm_kernel(mix, weight, stream, gain, resid, normed, total):
     i, steps = pl.program_id(0), pl.num_programs(0)
     span = weight.shape[1]
@@ -966,7 +1072,10 @@
     )(mix, weight, stream, gain)
 
 
-def norm_back_kernel(columns, resid, gain, cot, weight, grad_ref, low_ref, mix_ref, gain_ref):
+def norm_back_kernel(
+    columns, resid, gain, cot, weight, earlier, carried_in,
+    grad_ref, low_ref, mix_ref, gain_ref, carried
+):
     @pl.when(pl.program_id(0) == 0)
     def _():
         h = resid[...]
@@ -981,7 +1090,7 @@
     mix_ref[...] = against(low_ref[...], weight[...]).astype(jnp.bfloat16)
 
 
-def norm_back_mix(columns, resid, gain, cot, weight):
+def norm_back_mix(columns, resid, gain, cot, weight, earlier, carried):
     rows, width = resid.shape
     steps = 4
     whole = pl.BlockSpec((rows, width), lambda i: (0, 0))
@@ -992,19 +1101,100 @@
         in_specs=[
             whole, whole, line, whole,
             pl.BlockSpec((width // steps, width), lambda i: (i, 0)),
-        ],
-        out_specs=[whole, whole, pl.BlockSpec((rows, width // steps), lambda i: (0, i)), line],
+            pl.BlockSpec(memory_space=pl.ANY),
+            pl.BlockSpec(memory_space=pl.ANY),
+        ],
+        out_specs=[
+            whole, whole,
+            pl.BlockSpec((rows, width // steps), lambda i: (0, i)),
+            line,
+            pl.BlockSpec(memory_space=pl.ANY),
+        ],
         out_shape=[
             jax.ShapeDtypeStruct((rows, width), jnp.float32),
             jax.ShapeDtypeStruct((rows, width), jnp.bfloat16),
             jax.ShapeDtypeStruct((rows, width), jnp.bfloat16),
             jax.ShapeDtypeStruct((1, width), jnp.float32),
-        ],
+            jax.ShapeDtypeStruct(carried.shape, carried.dtype),
+        ],
+        input_output_aliases={6: 4},
         compiler_params=pltpu.CompilerParams(vmem_limit_bytes=40 * 1024 * 1024),
         cost_estimate=pl.CostEstimate(
             flops=2 * rows * width * width, bytes_accessed=16_000_000, transcendentals=0
         ),
-    )(columns, resid, gain, cot, weight)
+    )(columns, resid, gain, cot, weight, earlier, carried)
+
+
+def input_grad_kernel(
+    dk_own, dv_own, dk_got, dv_got, cosine, sine, dq, query_weight, kv_weight, stream, gain, resid_grad,
+    kv_ref, gain_ref, grad_ref, total
+):
+    i, steps = pl.program_id(0), pl.num_programs(0)
+    span = query_weight.shape[0]
+    kv_width = dk_own.shape[1]
+
+    @pl.when(i == 0)
+    def _():
+        ctx, size = lax.axis_index("ctx"), lax.axis_size("ctx")
+        dk, dv = dk_own[...], dv_own[...]
+        for step in range(1, dk_got.shape[0] + 1):
+            there = ctx + step < size
+            dk += jnp.where(there, dk_got[step - 1].astype(jnp.float32), 0.0)
+            dv += jnp.where(there, dv_got[step - 1].astype(jnp.float32), 0.0)
+        kv_ref[:, :kv_width] = turn(dk, cosine[...], -sine[...]).astype(jnp.bfloat16)
+        kv_ref[:, kv_width:] = dv.astype(jnp.bfloat16)
+
+    cols = pl.ds(pl.multiple_of(i * span, span), span)
+    total[:, cols] = against(dq[...], query_weight[...]) + against(
+        kv_ref[...], kv_weight[:, : 2 * kv_width]
+    )
+
+    @pl.when(i == steps - 1)
+    def _():
+        x = stream[...].astype(jnp.float32)
+        inverse = lax.rsqrt(jnp.mean(x * x, axis=1, keepdims=True) + EPS)
+        normal = x * inverse
+        slope = total[...]
+        gain_ref[...] = jnp.sum(slope * normal, axis=0, keepdims=True)
+        grad = resid_grad[...] + norm_back(slope * gain[...], normal, inverse)
+        grad_ref[...] = grad.astype(jnp.bfloat16)
+
+
+def input_grad(dk_own, dv_own, dk_got, dv_got, cosine, sine, dq, query_weight, kv_weight, stream, gain, resid_grad):
+    rows, width = stream.shape
+    steps = 4
+    span = width // steps
+
+    def whole(array):
+        return pl.BlockSpec(array.shape, lambda i: (0,) * array.ndim)
+
+    def strip(array):
+        return pl.BlockSpec((span, array.shape[1]), lambda i: (i, 0))
+
+    kept = (dk_own, dv_own, dk_got, dv_got, cosine, sine, dq)
+    kv_shape = (rows, 2 * dk_own.shape[1])
+    return pl.pallas_call(
+        input_grad_kernel,
+        grid=(steps,),
+        in_specs=[whole(array) for array in kept]
+        + [strip(query_weight), strip(kv_weight)]
+        + [whole(array) for array in (stream, gain, resid_grad)],
+        out_specs=[
+            pl.BlockSpec(kv_shape, lambda i: (0, 0)),
+            pl.BlockSpec((1, width), lambda i: (0, 0)),
+            pl.BlockSpec((rows, width), lambda i: (0, 0)),
+        ],
+        out_shape=[
+            jax.ShapeDtypeStruct(kv_shape, jnp.bfloat16),
+            jax.ShapeDtypeStruct((1, width), jnp.float32),
+            jax.ShapeDtypeStruct((rows, width), jnp.bfloat16),
+        ],
+        scratch_shapes=[pltpu.VMEM((rows, width), jnp.float32)],
+        compiler_params=pltpu.CompilerParams(vmem_limit_bytes=48 * 1024 * 1024),
+        cost_estimate=pl.CostEstimate(
+            flops=3 * rows * width * width, bytes_accessed=24_000_000, transcendentals=0
+        ),
+    )(*kept, query_weight, kv_weight, stream, gain, resid_grad)
 
 
 def hidden_layer_kernel(
@@ -1109,24 +1299,19 @@
 
     inv_one = lax.rsqrt(jnp.mean(stream * stream, axis=1, keepdims=True) + EPS)
     normal_one = stream * inv_one
-    normed_one = (normal_one * gain_one).astype(jnp.bfloat16)
-    kv_front = product(normed_one, kv_all)
-    key_low = rope(kv_front[:, :kv_width], cosine, sine).astype(jnp.bfloat16)
-    value_low = kv_front[:, kv_width : 2 * kv_width].astype(jnp.bfloat16)
-    own_pair = jnp.concatenate([key_low, value_low], axis=1)
-    query_all, out_all, pair_all, down_own, cot_all, window = gather_front(
+    normed_one, own_pair = norm_keys(tokens[0], gain_one[None], kv_all, cosine, sine)
+    query_all, out_all, pair_all, down_own, window, cot_own = gather_front(
         (query_weight, out_weight), jnp.stack([gate_weight, up_weight]), down_weight,
         cotangent[0], own_pair, sizes, 6,
     )
-    cot_all = cot_all.reshape(ctx_size * tok_rows, D)
+    cot_all = lax.all_gather(cot_own, "ctx", axis=0, tiled=True)
     query_all = query_all.reshape(D, D)
     out_all = out_all.reshape(D, D)
     down_own = down_own.reshape(ff_own, D)
     window = window.reshape(-1, 2 * kv_width)
     key_window, value_window = window[:, :kv_width], window[:, kv_width:]
-    query_front = product(normed_one, query_all)
     attn_mix, query_low, log_total = attend_forward(
-        query_front, key_window, value_window, bias, cosine, sine
+        normed_one, query_all, key_window, value_window, bias, cosine, sine
     )
     resid, normed_two = out_norm(attn_mix, out_all, tokens[0], gain_two[None])
     pair, normed_all = gather_hidden(pair_all, normed_two, sizes)
@@ -1138,49 +1323,35 @@
     columns = lax.psum_scatter(columns, "ctx", scatter_dimension=0, tiled=True)
     pair_sum, down_part = reduce_hidden(normed_all, grad_gate_low, grad_up_low, down_part, sizes)
     down_terms = across(hidden, cot_all).astype(jnp.bfloat16)
+    grad_resid, grad_resid_low, grad_mix_low, mlp_gain_local, down_terms = norm_back_mix(
+        columns, resid, gain_two[None], cotangent[0], out_all, pair_sum, down_terms
+    )
     down_sum = lax.psum_scatter(down_part, "ctx", scatter_dimension=0, tiled=True)
-    grad_resid, grad_resid_low, grad_mix_low, mlp_gain_local = norm_back_mix(
-        columns, resid, gain_two[None], cotangent[0], out_all
-    )
-    grad_query_low, grad_key_window, grad_value_window = attend_backward(
+    grad_query_low, dk_low, dv_low, dk_own, dv_own, down_terms = attend_backward(
         query_low, key_window, value_window, grad_mix_low, attn_mix, log_total, bias, cosine, sine,
-        pair_sum,
-    )
-    wide_grad, pair_sum, down_terms = reduce_rows(
+        down_terms,
+    )
+    grad_down = lax.psum_scatter(down_terms, "fsdp", scatter_dimension=0, tiled=True)
+    wide_grad, dk_got, dv_got = reduce_rows(
         jnp.stack([normed_one.T, attn_mix.T]),
         jnp.concatenate([grad_query_low, grad_resid_low], axis=1),
-        None, (pair_sum, down_terms), 512, sizes, 4,
-    )
-    grad_down = lax.psum_scatter(down_terms, "fsdp", scatter_dimension=0, tiled=True)
-    pair_sum = lax.all_to_all(pair_sum, "ctx", split_axis=0, concat_axis=0, tiled=True)
-    own_start = reach_blocks * tok_rows
-    grad_pair = jnp.concatenate([grad_key_window, grad_value_window], axis=1)
-    grad_pair_total = after(grad_pair[own_start:], wide_grad)
-    grad_pair_low = grad_pair[:own_start].astype(jnp.bfloat16)
-    for step in range(1, reach_blocks + 1):
-        first_row = (reach_blocks - step) * tok_rows
-        later = passed_along(grad_pair_low[first_row : first_row + tok_rows], "ctx", -step)
-        grad_pair_total = grad_pair_total + later.astype(jnp.float32)
-    grad_key_low = rope(grad_pair_total[:, :kv_width], cosine, -sine).astype(jnp.bfloat16)
-    grad_value_low = grad_pair_total[:, kv_width:].astype(jnp.bfloat16)
-    kv_low = jnp.concatenate([grad_key_low, grad_value_low], axis=1)
-    grad_normed_one = against(grad_query_low, query_all) + against(
-        jnp.pad(kv_low, ((0, 0), (0, LANES))), kv_all
-    )
-    attn_gain_local = jnp.sum(grad_normed_one * normal_one, axis=0)
-    gain_terms = jnp.stack([attn_gain_local, mlp_gain_local[0]], axis=1).astype(jnp.bfloat16)
+        None, (dk_low, dv_low), (), 512, sizes, 4,
+    )
+    kv_low, attn_gain_local, grad_input = input_grad(
+        dk_own, dv_own, dk_got, dv_got, cosine, sine, grad_query_low, query_all, kv_all,
+        tokens[0], gain_one[None], grad_resid,
+    )
+    gain_terms = jnp.stack([attn_gain_local[0], mlp_gain_local[0]], axis=1).astype(jnp.bfloat16)
     gain_terms = jnp.pad(gain_terms, ((0, 0), (0, 2 * LANES - 2)))[None]
-    (kv_grad,) = reduce_rows(
-        normed_one.T[None], kv_low, gain_terms, (), 2 * LANES, sizes, 5
-    )
-    pair_sum = after(pair_sum, kv_grad)
+    kv_grad, pair_sum = reduce_rows(
+        normed_one.T[None], kv_low, gain_terms, (), (pair_sum,), 2 * LANES, sizes, 5
+    )
     mixed = after(resid, kv_grad) + after(down_sum, kv_grad).astype(jnp.float32)
     mixed = mixed.astype(jnp.bfloat16)
     pair_sum = pair_sum.transpose(1, 2, 0, 3).reshape(2, own_rows, FF).astype(jnp.float32)
-    grad_input = grad_resid + norm_back(grad_normed_one * gain_one, normal_one, inv_one)
     return (
         mixed[None],
-        grad_input.astype(jnp.bfloat16)[None],
+        grad_input[None],
         kv_grad[:, 2 * kv_width],
         wide_grad[:, :D],
         kv_grad[:, :kv_width],

time: 839 us -> 777 us (0.926)
  matrix products: 35.3 us -> 14.4 us
  Pallas kernels: 697 us -> 685 us
  other arithmetic: 33.5 us -> 22.8 us
  starting transfers between devices: 10.3 us -> 0.34 us
  local copies, waits for them, and re-layouts: 40.5 us -> 30.8 us
    pallas_call x2, Pallas kernels: 230 us -> 174 us  [gather_front(): pl.pallas_call(functools.partial(front_kernel, sizes, len(parts), paired)...]
    dot_general x4 -> x0, matrix products: 20.8 us -> none  [the longest x2 11.2 us: product(): return jnp.dot(left, right, preferred_element_type=jnp.float32)]
    pallas_call x1, Pallas kernels: 105 us -> 121 us  [gather_hidden(): pl.pallas_call(functools.partial(hidden_kernel, sizes, pieces), in_specs=...]
    pallas_call x0 -> x2, Pallas kernels: none -> 12.9 us  [the longest x1 11.4 us: input_grad(): pl.pallas_call(input_grad_kernel, grid=(steps,), in_specs=[whole(array) f...]
    unnamed x105 -> x89, local copies, waits for them, and re-layouts: 21.9 us -> 19.9 us
  transfers between devices with their start and end apart: 8 -> 4, of which waited for: 1 -> 1; matrix products, arithmetic and copies ran while one was open for 8% -> 5% of each run, Pallas kernels for 33% -> 58%
where the time goes in v4:
time: 777 us; the launch traced here: 771 us
  Pallas kernels  685 us (88%)
  local copies, waits for them, and re-layouts  30.8 us (4%)
  other arithmetic  22.8 us (3%)
  between operations  14.5 us (2%)
  matrix products  14.4 us (2%)
    pallas_call x2, Pallas kernels, gather_front(): pl.pallas_call(functools.partial(front_kernel, sizes, len(parts), paired)...  174 us
    pallas_call x2, Pallas kernels, reduce_rows(): pl.pallas_call(functools.partial(reduce_kernel, sizes, chunk, products, e...  170 us
    pallas_call x1, Pallas kernels, gather_hidden(): pl.pallas_call(functools.partial(hidden_kernel, sizes, pieces), in_specs=...  121 us
    pallas_call x1, Pallas kernels, reduce_hidden(): pl.pallas_call(functools.partial(hidden_grad_kernel, sizes), in_specs=[vm...  79.9 us
    pallas_call x1, Pallas kernels, hidden_layer(): pl.pallas_call(hidden_layer_kernel, grid=(tokens // tile,), in_specs=[wid...  62.6 us
    pallas_call x1, Pallas kernels, attend_backward(): pl.pallas_call(attend_backward_kernel, grid=(steps,), in_specs=[wide, tal...  29.6 us
    pallas_call x1, Pallas kernels, attend_forward(): pl.pallas_call(attend_forward_kernel, grid=(steps,), in_specs=[pl.BlockSp...  23.3 us
    unnamed x89, local copies, waits for them, and re-layouts  19.9 us
  transfers between devices with their start and end apart: 4, of which 1 were waited for; matrix products, arithmetic and copies ran while one was open for 5% of the time, Pallas kernels for 58%

profile of v4, /device:TPU:0, one launch (start us, length us, event | category | flops | bytes accessed | tf_op | source)
XLA Modules:
  0.0 771.4 jit_solution(9614850467417647400)
XLA Ops:
  7.2 0.6 compare_reduce_fusion.1
  7.9 0.6 compare_reduce_fusion
  8.5 1.3 fusion.5
  9.8 0.1 copy.54
  9.9 1.3 fusion.6
  11.3 0.1 copy.55
  11.4 0.1 scatter.9
  11.5 1.5 pad_maximum_fusion.3.refs_0_
  13.1 37.3 %shard_map.203 = bf16[4,2,4,64,1152]{4,3,2,1,0:T(8,128)(2,1)} custom-call(bf16[64,1152]{1,0:T(8,128)(2,1)} %pad_maximum_fusion.3.refs_0_), custom_call_target="tpu_custom_call" | custom-call | flops 89999998976 | bytes 1000000 | tf_op jit(solution)/shard_map/pallas_call | solution.py:558
  50.4 1.9 convert_reduce_fusion
  52.4 0.2 reduce-window.4
  52.8 1.0 copy.67.refs_6_
  53.8 0.5 fusion.4
  54.3 1.5 pad_maximum_fusion.refs_2_
  55.8 0.3 pad_maximum_fusion.4
  56.2 1.4 copy-done
  57.5 1.5 shard_map.204
  59.1 0.8 copy-done.29
  59.8 0.9 broadcast_in_dim.37.refs_5_
  60.8 137.2 %shard_map.205 = (bf16[4,2,4,64,2048]{4,3,2,1,0:T(8,128)(2,1)}, bf16[4,2,4,64,2048]{4,3,2,1,0:T(8,128)(2,1)}, bf16[2,8,4,64,1024]{4,3,2,1,0:T(8,128)(2,1)}, bf16...) custom-call(bf16[64,2048]{1,0:T(8,128)(2,1)} %refs_0_.1, ...), custom_call_target="tpu_custom_call", output_to_operand_aliasing={{5}: (6, {})} | custom-call | flops 89999998976 | bytes 1000000 | tf_op jit(solution)/shard_map/pallas_call | solution.py:558
  198.0 0.2 reduce-scatter.4.cloned.1.call-start
  198.2 0.1 convert_reduce_fusion.2
  198.3 1.9 fusion.2.bias_ref
  200.2 1.9 fusion.9
  202.2 23.3 %shard_map.206 = (bf16[256,2048]{1,0:T(8,128)(2,1)S(1)}, bf16[256,2048]{1,0:T(8,128)(2,1)S(1)}, f32[32,256]{1,0:T(8,128)S(1)}) custom-call(bf16[256,2048]{1,0:T(8,128)(2,1)S(1)} %get-tuple-element.78.n_ref, bf16[2048,2048]{1,0:T(8,128)(2,1)} %bitcast.68, bf16[1280,512]{1,0:T(8,128)(2,1)S(1)} %get-tuple-element.128.k_ref, ...), custom_call_target="tpu_custom_call" | custom-call | flops 40000000000 | bytes 10000000 | tf_op jit(solution)/shard_map/pallas_call | solution.py:124
  225.6 4.0 shard_map.207
  229.6 1.3 copy-done.2
  231.0 1.0 copy-done.27
  231.9 121.3 %shard_map.208 = (bf16[2,8,4,64,1024]{4,3,2,1,0:T(8,128)(2,1)}, bf16[4,2,256,2048]{3,2,1,0:T(8,128)(2,1)}) custom-call(bf16[2,8,4,64,1024]{4,3,2,1,0:T(8,128)(2,1)} %get-tuple-element.86.pair_in, bf16[256,2048]{1,0:T(8,128)(2,1)} %copy-done.27), custom_call_target="tpu_custom_call", output_to_operand_aliasing={{0}: (0, {})} | custom-call | flops 89999998976 | bytes 30000000 | tf_op jit(solution)/shard_map/pallas_call | solution.py:628
  353.3 62.6 %shard_map.209 = (bf16[2048,1024]{1,0:T(8,128)(2,1)}, bf16[2048,1024]{1,0:T(8,128)(2,1)}, bf16[2048,1024]{1,0:T(8,128)(2,1)}, bf16[2048,2048]{1,0:T(8,128)(2,1)}, bf16[2048,2048]{1,0:T(8,128)(2,1)}) custom-call(bf16[2048,2048]{1,0:T(8,128)(2,1)} %bitcast.86, bf16[2048,2048]{1,0:T(8,128)(2,1)} %all-gather.2.cloned.1.call-done.cot, ...), custom_call_target="tpu_custom_call" | custom-call | flops 68719476736 | bytes 30000000 | tf_op jit(solution)/shard_map/pallas_call | solution.py:1235
  416.0 1.1 copy-done.21
  417.1 1.3 copy.57
  418.5 1.3 copy.58
  419.8 2.9 pad_maximum_fusion.1.refs_0_
  422.7 79.9 %shard_map.210 = (bf16[8,2,64,1024]{3,2,1,0:T(8,128)(2,1)}, bf16[2048,2048]{1,0:T(8,128)(2,1)}) custom-call(bf16[2048,2048]{1,0:T(8,128)(2,1)} %bitcast.87, bf16[2048,1024]{1,0:T(8,128)(2,1)} %get-tuple-element.93.gate, bf16[2048,1024]{1,0:T(8,128)(2,1)} %get-tuple-element.94.up, ...), custom_call_target="tpu_custom_call", output_to_operand_aliasing={{1}: (3, {})} | custom-call | flops 60000002048 | bytes 30000000 | tf_op jit(solution)/shard_map/pallas_call | solution.py:988
  502.7 14.4 %convolution_convert_fusion.carried_in = bf16[1024,2048]{1,0:T(8,128)(2,1)} fusion(bf16[2048,1024]{1,0:T(8,128)(2,1)} %get-tuple-element.97, bf16[2048,2048]{1,0:T(8,128)(2,1)} %all-gather.2.cloned.1.call-done.cot), kind=kOutput, calls=%fused_computation.1 | convolution fusion | flops 8592031744 | bytes 16777216 | tf_op jit(solution)/shard_map/dot_general | solution.py:40
  517.2 1.6 copy-done.3
  518.8 1.6 copy-done.9
  520.4 1.3 copy-done.17
  521.6 7.4 shard_map.211
  529.0 1.3 copy-done.10
  530.4 1.0 copy-done.26
  531.3 29.6 %shard_map.212 = (bf16[256,2048]{1,0:T(8,128)(2,1)S(1)}, bf16[1024,512]{1,0:T(8,128)(2,1)S(1)}, bf16[1024,512]{1,0:T(8,128)(2,1)S(1)}, f32[256,512]{1,0:T(8,128)...) custom-call(bf16[256,2048]{1,0:T(8,128)(2,1)S(1)} %copy-done.31, ...), custom_call_target="tpu_custom_call", output_to_operand_aliasing={{5}: (9, {})} | custom-call | flops 80000000000 | bytes 20000000 | tf_op jit(solution)/shard_map/pallas_call | solution.py:223
  561.0 1.7 pad_maximum_fusion.2.refs_1_
  562.8 0.3 copy-done.33
  563.0 0.6 broadcast_in_dim.68.refs_2_
  563.6 110.0 %shard_map.213 = (f32[64,4096]{1,0:T(8,128)}, bf16[4,256,512]{2,1,0:T(8,128)(2,1)}, bf16[4,256,512]{2,1,0:T(8,128)(2,1)}) custom-call(bf16[2,2048,256]{2,1,0:T(8,128)(2,1)} %pad_maximum_fusion.1.refs_0_, bf16[256,4096]{1,0:T(8,128)(2,1)} %pad_maximum_fusion.2.refs_1_, bf16[1,16,128]{2,1,0:T(8,128)(2,1)} %broadcast_in_dim.68.refs_2_, ...), custom_call_target="tpu_custom_call" | custom-call | flops 80000000000 | bytes 30000000 | tf_op jit(solution)/shard_map/pallas_call | solution.py:878
  673.7 1.2 copy-done.18
  674.9 1.2 copy-done.19
  676.1 11.4 %shard_map.214 = (bf16[256,1024]{1,0:T(8,128)(2,1)S(1)}, f32[1,2048]{1,0:T(1,128)S(1)}, bf16[256,2048]{1,0:T(8,128)(2,1)}) custom-call(f32[256,512]{1,0:T(8,128)S(1)} %get-tuple-element.101.dk_own, f32[256,512]{1,0:T(8,128)S(1)} %get-tuple-element.102.dv_own, bf16[4,256,512]{2,1,0:T(8,128)(2,1)S(1)} %copy-done.18, bf16[4,256,512]{2,1,0:T(8,128)(2,1)S(1)} %copy-done.19, ...), custom_call_target="tpu_custom_call" | custom-call | flops 3221225472 | bytes 24000000 | tf_op jit(solution)/shard_map/pallas_call | solution.py:1176
  687.5 0.8 copy-done.28
  688.3 0.3 copy.59
  688.6 1.1 pad_bitcast_fusion.refs_2_
  689.8 59.6 %shard_map.215 = (f32[64,1280]{1,0:T(8,128)}, bf16[8,2,64,1024]{3,2,1,0:T(8,128)(2,1)}) custom-call(bf16[1,2048,256]{2,1,0:T(8,128)(2,1)} %bitcast.72, bf16[256,1024]{1,0:T(8,128)(2,1)} %copy-done.28, bf16[1,2048,256]{2,1,0:T(8,128)(2,1)} %pad_bitcast_fusion.refs_2_, bf16[8,2,64,1024]{3,2,1,0:T(8,128)(2,1)} %get-tuple-element.96.earlier.refs_3_), custom_call_target="tpu_custom_call" | custom-call | flops 80000000000 | bytes 30000000 | tf_op jit(solution)/shard_map/pallas_call | solution.py:878
  749.5 2.0 convert_bitcast_fusion
  751.5 0.6 fusion.8
  752.1 1.5 copy.62
  753.6 1.5 copy.63
  755.0 0.7 slice_reduce_fusion
  755.7 0.7 fusion.11
  756.5 1.0 fusion.10
  757.5 1.3 fusion.3
  758.8 3.1 reduce-scatter.8.cloned.1.call-done
  761.9 2.8 convert_element_type.73
  (95 shorter events, 0.7 us)
Async XLA Ops:
  7.2 346.1 %all-gather.2.cloned.1.call-start = ((), (), s32[]{:S(2)}) async-start(), calls=%async_computation.3 | async-start | bytes 9437184 | tf_op jit(solution)/shard_map/all_gather | solution.py:1307
  13.1 39.3 %copy-start.40 = (s32[1,4]{1,0:T(1,128)S(1)}, s32[1,4]{1,0:T(1,128)}, u32[]{:S(2)}) copy-start(s32[1,4]{1,0:T(1,128)} %param.18) | copy-start | bytes 52
  13.1 39.7 %copy-start.5 = (bf16[1,256,2048]{2,1,0:T(8,128)(2,1)S(1)}, bf16[1,256,2048]{2,1,0:T(8,128)(2,1)}, u32[]{:S(2)}) copy-start(bf16[1,256,2048]{2,1,0:T(8,128)(2,1)} %param.17) | copy-start | bytes 3145732
  50.4 3.9 copy-start.36
  50.4 5.7 copy-start.1
  52.3 3.8 copy-start.22
  52.4 173.2 %copy-start.24 = (f32[2048]{0:T(1024)}, f32[2048]{0:T(1024)S(1)}, u32[]{:S(2)}) copy-start(f32[2048]{0:T(1024)S(1)} %get-tuple-element.121) | copy-start | bytes 24580
  52.6 1.8 copy-start.37
  54.3 3.2 copy-start
  56.1 146.0 %copy-start.13 = (f32[256,128]{1,0:T(8,128)}, f32[256,128]{1,0:T(8,128)S(1)}, u32[]{:S(2)}) copy-start(f32[256,128]{1,0:T(8,128)S(1)} %get-tuple-element.136.cosine.cos_ref) | copy-start | bytes 393220
  56.1 146.0 %copy-start.15 = (f32[256,128]{1,0:T(8,128)}, f32[256,128]{1,0:T(8,128)S(1)}, u32[]{:S(2)}) copy-start(f32[256,128]{1,0:T(8,128)S(1)} %get-tuple-element.137.sine.sin_ref) | copy-start | bytes 393220
  59.0 0.8 copy-start.29
  59.8 142.3 %copy-start.20 = (bf16[256,2048]{1,0:T(8,128)(2,1)}, bf16[256,2048]{1,0:T(8,128)(2,1)S(1)}, u32[]{:S(2)}) copy-start(bf16[256,2048]{1,0:T(8,128)(2,1)S(1)} %get-tuple-element.78.n_ref) | copy-start | bytes 3145732
  198.0 319.2 %reduce-scatter.4.cloned.1.call-start = ((), (), s32[]{:S(2)}) async-start(), calls=%async_computation.4 | async-start | bytes 9437184 | tf_op jit(solution)/shard_map/reduce_scatter | solution.py:1323
  202.1 23.4 %copy-start.11 = (bf16[1280,512]{1,0:T(8,128)(2,1)}, bf16[1280,512]{1,0:T(8,128)(2,1)S(1)}, u32[]{:S(2)}) copy-start(bf16[1280,512]{1,0:T(8,128)(2,1)S(1)} %get-tuple-element.127.v_ref) | copy-start | bytes 3932164
  202.1 23.4 %copy-start.12 = (bf16[1280,512]{1,0:T(8,128)(2,1)}, bf16[1280,512]{1,0:T(8,128)(2,1)S(1)}, u32[]{:S(2)}) copy-start(bf16[1280,512]{1,0:T(8,128)(2,1)S(1)} %get-tuple-element.128.k_ref) | copy-start | bytes 3932164
  202.1 23.4 %slice-start = ((s8[8388608]{0:T(1024)(128)(4,1)}), s8[4194304]{0:T(1024)(128)(4,1)S(1)}, s32[]{:S(2)}) async-start(s8[8388608]{0:T(1024)(128)(4,1)} %bitcast.53), calls=%async_computation.7 | async-start | bytes 8388608
  202.2 23.4 %slice-start.1 = ((s8[8388608]{0:T(1024)(128)(4,1)}), s8[4194304]{0:T(1024)(128)(4,1)S(1)}, s32[]{:S(2)}) async-start(s8[8388608]{0:T(1024)(128)(4,1)} %bitcast.53), calls=%async_computation.8 | async-start | bytes 8388608
  225.5 4.1 copy-start.7
  225.5 4.1 copy-start.30
  229.6 1.3 copy-start.2
  231.0 1.0 copy-start.27
  415.9 1.2 copy-start.21
  415.9 2.5 copy-start.8
  416.0 333.5 %reduce-scatter.6.cloned.1.call-start = ((), (), s32[]{:S(2)}) async-start(), calls=%async_computation.5 | async-start | bytes 9437184 | tf_op jit(solution)/shard_map/reduce_scatter | solution.py:1329
  418.5 1.3 copy-start.34
  502.7 259.2 %reduce-scatter.8.cloned.1.call-start = ((), (), s32[]{:S(2)}) async-start(), calls=%async_computation.6 | async-start | bytes 5242880 | tf_op jit(solution)/shard_map/reduce_scatter | solution.py:1334
  502.7 14.4 %copy-start.6 = (bf16[1,256,2048]{2,1,0:T(8,128)(2,1)S(1)}, bf16[1,256,2048]{2,1,0:T(8,128)(2,1)}, u32[]{:S(2)}) copy-start(bf16[1,256,2048]{2,1,0:T(8,128)(2,1)} %param.17) | copy-start | bytes 3145732
  502.7 14.4 %copy-start.25 = (f32[2048]{0:T(1024)S(1)}, f32[2048]{0:T(1024)}, u32[]{:S(2)}) copy-start(f32[2048]{0:T(1024)} %copy-done.24) | copy-start | bytes 24580
  517.2 1.6 copy-start.3
  518.8 1.6 copy-start.9
  520.4 1.3 copy-start.17
  521.6 9.7 %copy-start.14 = (f32[256,128]{1,0:T(8,128)S(1)}, f32[256,128]{1,0:T(8,128)}, u32[]{:S(2)}) copy-start(f32[256,128]{1,0:T(8,128)} %copy-done.13) | copy-start | bytes 393220
  521.6 9.7 %copy-start.16 = (f32[256,128]{1,0:T(8,128)S(1)}, f32[256,128]{1,0:T(8,128)}, u32[]{:S(2)}) copy-start(f32[256,128]{1,0:T(8,128)} %copy-done.15) | copy-start | bytes 393220
  521.6 9.7 %copy-start.31 = (bf16[256,2048]{1,0:T(8,128)(2,1)S(1)}, bf16[256,2048]{1,0:T(8,128)(2,1)}, u32[]{:S(2)}) copy-start(bf16[256,2048]{1,0:T(8,128)(2,1)} %copy-done.30) | copy-start | bytes 3145732
  529.0 1.3 copy-start.10
  530.4 1.0 copy-start.26
  561.0 1.7 copy-start.32
  561.0 2.0 copy-start.33
  563.6 110.1 %copy-start.23 = (f32[2048]{0:T(1024)S(1)}, f32[2048]{0:T(1024)}, u32[]{:S(2)}) copy-start(f32[2048]{0:T(1024)} %copy-done.22) | copy-start | bytes 24580
  673.7 1.2 copy-start.18
  674.9 1.2 copy-start.19
  687.5 0.8 copy-start.28
  753.6 1.5 copy-start.39
  753.6 2.9 copy-start.35
  753.6 3.9 copy-start.38
  755.0 2.5 copy-start.4
Sparse Core Ops, SparseCore 0:
  198.1 118.7 all-gather.1
  416.1 87.7 reduce-scatter.3
  506.2 109.5 reduce-scatter.5
  689.9 71.9 reduce-scatter.7

commit v5 on v4

--- a/solution.py
+++ b/solution.py
@@ -911,11 +911,12 @@
 
 
 def hidden_grad_kernel(
-    sizes, normed, gate, up, carried_in, pair_sum, carried,
+    sizes, normed, gate, up, hidden, cot, carried_in, pair_sum, down_terms, carried,
     terms, pair_sent, pair_got, pair_send, pair_recv
 ):
     ctx_size, fsdp_size = sizes
     count, span = terms.shape[1], normed.shape[1] // terms.shape[1]
+    piece = max(LANES, hidden.shape[1] // count)
     masks = [1 << bit for bit in range(fsdp_size.bit_length() - 1)]
     orders = [masks, masks[::-1]]
     bits = len(masks)
@@ -944,6 +945,11 @@
             for h, grad in enumerate((gate, up)):
                 term = across(normed[:, rows], grad[...])
                 terms[h, t] = term.astype(jnp.bfloat16).reshape(terms.shape[2:])
+
+        @pl.when(t < hidden.shape[1] // piece)
+        def _():
+            rows = pl.ds(pl.multiple_of(t * piece, piece), piece)
+            down_terms[rows, :] = across(hidden[:, rows], cot[...]).astype(jnp.bfloat16)
 
         for j in range(bits):
             @pl.when((t >= j) & (t < count + j))
@@ -978,7 +984,7 @@
     lax.fori_loop(0, count, finish, 0)
 
 
-def reduce_hidden(normed, gate, up, carried, sizes):
+def reduce_hidden(normed, gate, up, hidden, cot, carried, sizes):
     ctx_size, fsdp_size = sizes
     bits = fsdp_size.bit_length() - 1
     rows, columns = normed.shape[1] // (ctx_size * fsdp_size), gate.shape[1]
@@ -987,13 +993,14 @@
     hbm = pl.BlockSpec(memory_space=pl.ANY)
     return pl.pallas_call(
         functools.partial(hidden_grad_kernel, sizes),
-        in_specs=[vmem] * 3 + [hbm],
-        out_specs=[vmem, hbm],
+        in_specs=[vmem] * 5 + [hbm],
+        out_specs=[vmem, vmem, hbm],
         out_shape=[
             jax.ShapeDtypeStruct((ctx_size, 2, rows, columns), jnp.bfloat16),
+            jax.ShapeDtypeStruct((hidden.shape[1], cot.shape[1]), jnp.bfloat16),
             jax.ShapeDtypeStruct(carried.shape, carried.dtype),
         ],
-        input_output_aliases={3: 1},
+        input_output_aliases={5: 2},
         scratch_shapes=[
             pltpu.VMEM((2, ctx_size, fsdp_size, rows, columns), jnp.bfloat16), pair, pair,
         ]
@@ -1002,7 +1009,7 @@
             collective_id=3, has_side_effects=True, vmem_limit_bytes=60 * 1024 * 1024
         ),
         cost_estimate=pl.CostEstimate(flops=60_000_000_000, bytes_accessed=30_000_000, transcendentals=0),
-    )(normed, gate, up, carried)
+    )(normed, gate, up, hidden, cot, carried)
 
 
 def norm_keys_kernel(stream, gain, weight, cosine, sine, normed_ref, pair_ref):
@@ -1321,8 +1328,9 @@
         normed_all, cot_all, pair, down_own
     )
     columns = lax.psum_scatter(columns, "ctx", scatter_dimension=0, tiled=True)
-    pair_sum, down_part = reduce_hidden(normed_all, grad_gate_low, grad_up_low, down_part, sizes)
-    down_terms = across(hidden, cot_all).astype(jnp.bfloat16)
+    pair_sum, down_terms, down_part = reduce_hidden(
+        normed_all, grad_gate_low, grad_up_low, hidden, cot_all, down_part, sizes
+    )
     grad_resid, grad_resid_low, grad_mix_low, mlp_gain_local, down_terms = norm_back_mix(
         columns, resid, gain_two[None], cotangent[0], out_all, pair_sum, down_terms
     )
@@ -1335,7 +1343,7 @@
     wide_grad, dk_got, dv_got = reduce_rows(
         jnp.stack([normed_one.T, attn_mix.T]),
         jnp.concatenate([grad_query_low, grad_resid_low], axis=1),
-        None, (dk_low, dv_low), (), 512, sizes, 4,
+        None, (dk_low, dv_low), (), 4 * LANES, sizes, 4,
     )
     kv_low, attn_gain_local, grad_input = input_grad(
         dk_own, dv_own, dk_got, dv_got, cosine, sine, grad_query_low, query_all, kv_all,

time: 777 us -> 780 us (level)
  Pallas kernels: 685 us -> 701 us
  matrix products: 14.4 us -> 0 us
    dot_general x1 -> x0, matrix products: 14.4 us -> none  [across(): lax.dot_general(left, right, (((0,), (0,)), ((), ())), preferred_element_...]
    pallas_call x2, Pallas kernels: 170 us -> 179 us  [reduce_rows(): pl.pallas_call(functools.partial(reduce_kernel, sizes, chunk, products, e...]
  transfers between devices with their start and end apart: 4 -> 4, of which waited for: 1 -> 1; matrix products, arithmetic and copies ran while one was open for 5% -> 3% of each run, Pallas kernels for 58% -> 60%
where the time goes in v5:
time: 780 us; the launch traced here: 775 us
  Pallas kernels  701 us (90%)
  local copies, waits for them, and re-layouts  32.6 us (4%)
  other arithmetic  22.7 us (3%)
  between operations  14.6 us (2%)
    pallas_call x2, Pallas kernels, reduce_rows(): pl.pallas_call(functools.partial(reduce_kernel, sizes, chunk, products, e...  179 us
    pallas_call x2, Pallas kernels, gather_front(): pl.pallas_call(functools.partial(front_kernel, sizes, len(parts), paired)...  174 us
    pallas_call x1, Pallas kernels, gather_hidden(): pl.pallas_call(functools.partial(hidden_kernel, sizes, pieces), in_specs=...  122 us
    pallas_call x1, Pallas kernels, reduce_hidden(): pl.pallas_call(functools.partial(hidden_grad_kernel, sizes), in_specs=[vm...  86.1 us
    pallas_call x1, Pallas kernels, hidden_layer(): pl.pallas_call(hidden_layer_kernel, grid=(tokens // tile,), in_specs=[wid...  62.6 us
    pallas_call x1, Pallas kernels, attend_backward(): pl.pallas_call(attend_backward_kernel, grid=(steps,), in_specs=[wide, tal...  29.2 us
    pallas_call x1, Pallas kernels, attend_forward(): pl.pallas_call(attend_forward_kernel, grid=(steps,), in_specs=[pl.BlockSp...  23.4 us
    unnamed x89, local copies, waits for them, and re-layouts  21.7 us
  transfers between devices with their start and end apart: 4, of which 1 were waited for; matrix products, arithmetic and copies ran while one was open for 3% of the time, Pallas kernels for 60%

profile of v5, /device:TPU:0, one launch (start us, length us, event | category | flops | bytes accessed | tf_op | source)
XLA Modules:
  0.0 774.8 jit_solution(18380733610092437263)
XLA Ops:
  7.2 0.6 compare_reduce_fusion.1
  7.9 0.6 compare_reduce_fusion
  8.5 1.3 fusion.5
  9.8 0.1 copy.54
  9.9 1.3 fusion.6
  11.3 0.1 copy.55
  11.4 0.1 scatter.9
  11.5 1.5 pad_maximum_fusion.3.refs_0_
  13.1 37.3 %shard_map.203 = bf16[4,2,4,64,1152]{4,3,2,1,0:T(8,128)(2,1)} custom-call(bf16[64,1152]{1,0:T(8,128)(2,1)} %pad_maximum_fusion.3.refs_0_), custom_call_target="tpu_custom_call" | custom-call | flops 89999998976 | bytes 1000000 | tf_op jit(solution)/shard_map/pallas_call | solution.py:558
  50.4 1.9 convert_reduce_fusion
  52.4 0.2 reduce-window.4
  52.8 1.0 copy.67.refs_6_
  53.8 0.5 fusion.4
  54.3 1.5 pad_maximum_fusion.refs_2_
  55.8 0.3 pad_maximum_fusion.4
  56.1 1.4 copy-done
  57.5 1.5 shard_map.204
  59.0 0.8 copy-done.29
  59.8 0.9 broadcast_in_dim.37.refs_5_
  60.8 137.2 %shard_map.205 = (bf16[4,2,4,64,2048]{4,3,2,1,0:T(8,128)(2,1)}, bf16[4,2,4,64,2048]{4,3,2,1,0:T(8,128)(2,1)}, bf16[2,8,4,64,1024]{4,3,2,1,0:T(8,128)(2,1)}, bf16...) custom-call(bf16[64,2048]{1,0:T(8,128)(2,1)} %refs_0_.1, ...), custom_call_target="tpu_custom_call", output_to_operand_aliasing={{5}: (6, {})} | custom-call | flops 89999998976 | bytes 1000000 | tf_op jit(solution)/shard_map/pallas_call | solution.py:558
  197.9 0.6 reduce-scatter.4.cloned.1.call-start
  198.6 1.9 fusion.2.bias_ref
  200.6 1.9 fusion.9
  202.5 23.4 %shard_map.206 = (bf16[256,2048]{1,0:T(8,128)(2,1)S(1)}, bf16[256,2048]{1,0:T(8,128)(2,1)S(1)}, f32[32,256]{1,0:T(8,128)S(1)}) custom-call(bf16[256,2048]{1,0:T(8,128)(2,1)S(1)} %get-tuple-element.79.n_ref, bf16[2048,2048]{1,0:T(8,128)(2,1)} %bitcast.66, bf16[1280,512]{1,0:T(8,128)(2,1)S(1)} %get-tuple-element.130.k_ref, ...), custom_call_target="tpu_custom_call" | custom-call | flops 40000000000 | bytes 10000000 | tf_op jit(solution)/shard_map/pallas_call | solution.py:124
  226.0 4.0 shard_map.207
  230.0 1.3 copy-done.2
  231.3 1.0 copy-done.27
  232.3 121.6 %shard_map.208 = (bf16[2,8,4,64,1024]{4,3,2,1,0:T(8,128)(2,1)}, bf16[4,2,256,2048]{3,2,1,0:T(8,128)(2,1)}) custom-call(bf16[2,8,4,64,1024]{4,3,2,1,0:T(8,128)(2,1)} %get-tuple-element.87.pair_in, bf16[256,2048]{1,0:T(8,128)(2,1)} %copy-done.27), custom_call_target="tpu_custom_call", output_to_operand_aliasing={{0}: (0, {})} | custom-call | flops 89999998976 | bytes 30000000 | tf_op jit(solution)/shard_map/pallas_call | solution.py:628
  353.9 62.6 %shard_map.209 = (bf16[2048,1024]{1,0:T(8,128)(2,1)}, bf16[2048,1024]{1,0:T(8,128)(2,1)}, bf16[2048,1024]{1,0:T(8,128)(2,1)}, bf16[2048,2048]{1,0:T(8,128)(2,1)}, bf16[2048,2048]{1,0:T(8,128)(2,1)}) custom-call(bf16[2048,2048]{1,0:T(8,128)(2,1)} %bitcast.84, bf16[2048,2048]{1,0:T(8,128)(2,1)} %all-gather.2.cloned.1.call-done.cot, ...), custom_call_target="tpu_custom_call" | custom-call | flops 68719476736 | bytes 30000000 | tf_op jit(solution)/shard_map/pallas_call | solution.py:1242
  416.6 1.1 copy-done.21
  417.8 1.3 copy.57
  419.1 1.3 copy.58
  420.4 0.3 copy-done.34
  420.7 2.8 pad_maximum_fusion.1.refs_0_
  423.5 86.1 %shard_map.210 = (bf16[8,2,64,1024]{3,2,1,0:T(8,128)(2,1)}, bf16[1024,2048]{1,0:T(8,128)(2,1)}, bf16[2048,2048]{1,0:T(8,128)(2,1)}) custom-call(bf16[2048,2048]{1,0:T(8,128)(2,1)} %bitcast.85, bf16[2048,1024]{1,0:T(8,128)(2,1)} %get-tuple-element.94.gate, bf16[2048,1024]{1,0:T(8,128)(2,1)} %get-tuple-element.95.up, ...), custom_call_target="tpu_custom_call", output_to_operand_aliasing={{2}: (5, {})} | custom-call | flops 60000002048 | bytes 30000000 | tf_op jit(solution)/shard_map/pallas_call | solution.py:994
  509.8 1.1 copy-done.6
  510.9 1.6 copy-done.3
  512.5 1.9 copy-done.9
  514.4 1.2 copy-done.17
  515.7 7.7 shard_map.211
  523.3 1.4 copy-done.10
  524.7 1.0 copy-done.26
  525.7 29.2 %shard_map.212 = (bf16[256,2048]{1,0:T(8,128)(2,1)S(1)}, bf16[1024,512]{1,0:T(8,128)(2,1)S(1)}, bf16[1024,512]{1,0:T(8,128)(2,1)S(1)}, f32[256,512]{1,0:T(8,128)...) custom-call(bf16[256,2048]{1,0:T(8,128)(2,1)S(1)} %copy-done.31, ...), custom_call_target="tpu_custom_call", output_to_operand_aliasing={{5}: (9, {})} | custom-call | flops 80000000000 | bytes 20000000 | tf_op jit(solution)/shard_map/pallas_call | solution.py:223
  554.9 1.7 pad_maximum_fusion.2.refs_1_
  556.6 0.3 copy-done.33
  556.9 0.6 broadcast_in_dim.68.refs_2_
  557.5 119.5 %shard_map.213 = (f32[64,4096]{1,0:T(8,128)}, bf16[4,256,512]{2,1,0:T(8,128)(2,1)}, bf16[4,256,512]{2,1,0:T(8,128)(2,1)}) custom-call(bf16[2,2048,256]{2,1,0:T(8,128)(2,1)} %pad_maximum_fusion.1.refs_0_, bf16[256,4096]{1,0:T(8,128)(2,1)} %pad_maximum_fusion.2.refs_1_, bf16[1,16,128]{2,1,0:T(8,128)(2,1)} %broadcast_in_dim.68.refs_2_, ...), custom_call_target="tpu_custom_call" | custom-call | flops 80000000000 | bytes 30000000 | tf_op jit(solution)/shard_map/pallas_call | solution.py:878
  676.9 1.2 copy-done.18
  678.2 1.2 copy-done.19
  679.4 11.5 %shard_map.214 = (bf16[256,1024]{1,0:T(8,128)(2,1)S(1)}, f32[1,2048]{1,0:T(1,128)S(1)}, bf16[256,2048]{1,0:T(8,128)(2,1)}) custom-call(f32[256,512]{1,0:T(8,128)S(1)} %get-tuple-element.103.dk_own, f32[256,512]{1,0:T(8,128)S(1)} %get-tuple-element.104.dv_own, bf16[4,256,512]{2,1,0:T(8,128)(2,1)S(1)} %copy-done.18, bf16[4,256,512]{2,1,0:T(8,128)(2,1)S(1)} %copy-done.19, ...), custom_call_target="tpu_custom_call" | custom-call | flops 3221225472 | bytes 24000000 | tf_op jit(solution)/shard_map/pallas_call | solution.py:1183
  690.8 0.8 copy-done.28
  691.7 0.3 copy.59
  692.0 1.1 pad_bitcast_fusion.refs_2_
  693.1 59.7 %shard_map.215 = (f32[64,1280]{1,0:T(8,128)}, bf16[8,2,64,1024]{3,2,1,0:T(8,128)(2,1)}) custom-call(bf16[1,2048,256]{2,1,0:T(8,128)(2,1)} %bitcast.70, bf16[256,1024]{1,0:T(8,128)(2,1)} %copy-done.28, bf16[1,2048,256]{2,1,0:T(8,128)(2,1)} %pad_bitcast_fusion.refs_2_, bf16[8,2,64,1024]{3,2,1,0:T(8,128)(2,1)} %get-tuple-element.98.earlier.refs_3_), custom_call_target="tpu_custom_call" | custom-call | flops 80000000000 | bytes 30000000 | tf_op jit(solution)/shard_map/pallas_call | solution.py:878
  752.9 2.0 convert_bitcast_fusion
  754.9 0.6 fusion.8
  755.5 1.5 copy.62
  757.0 1.5 copy.63
  758.4 0.7 slice_reduce_fusion
  759.1 0.7 fusion.11
  759.8 1.0 fusion.10
  760.9 1.3 fusion.3
  762.2 3.1 reduce-scatter.8.cloned.1.call-done
  765.2 2.8 convert_element_type.69
  (94 shorter events, 0.8 us)
Async XLA Ops:
  7.2 346.8 %all-gather.2.cloned.1.call-start = ((), (), s32[]{:S(2)}) async-start(), calls=%async_computation.3 | async-start | bytes 9437184 | tf_op jit(solution)/shard_map/all_gather | solution.py:1314
  13.1 39.3 %copy-start.40 = (s32[1,4]{1,0:T(1,128)S(1)}, s32[1,4]{1,0:T(1,128)}, u32[]{:S(2)}) copy-start(s32[1,4]{1,0:T(1,128)} %param.18) | copy-start | bytes 52
  13.1 39.7 %copy-start.5 = (bf16[1,256,2048]{2,1,0:T(8,128)(2,1)S(1)}, bf16[1,256,2048]{2,1,0:T(8,128)(2,1)}, u32[]{:S(2)}) copy-start(bf16[1,256,2048]{2,1,0:T(8,128)(2,1)} %param.17) | copy-start | bytes 3145732
  50.4 3.9 copy-start.36
  50.4 5.7 copy-start.1
  52.3 3.8 copy-start.22
  52.4 173.6 %copy-start.24 = (f32[2048]{0:T(1024)}, f32[2048]{0:T(1024)S(1)}, u32[]{:S(2)}) copy-start(f32[2048]{0:T(1024)S(1)} %get-tuple-element.123) | copy-start | bytes 24580
  52.6 1.7 copy-start.37
  54.3 3.2 copy-start
  56.1 146.4 %copy-start.13 = (f32[256,128]{1,0:T(8,128)}, f32[256,128]{1,0:T(8,128)S(1)}, u32[]{:S(2)}) copy-start(f32[256,128]{1,0:T(8,128)S(1)} %get-tuple-element.138.cosine.cos_ref) | copy-start | bytes 393220
  56.1 146.4 %copy-start.15 = (f32[256,128]{1,0:T(8,128)}, f32[256,128]{1,0:T(8,128)S(1)}, u32[]{:S(2)}) copy-start(f32[256,128]{1,0:T(8,128)S(1)} %get-tuple-element.139.sine.sin_ref) | copy-start | bytes 393220
  59.0 0.8 copy-start.29
  59.8 142.7 %copy-start.20 = (bf16[256,2048]{1,0:T(8,128)(2,1)}, bf16[256,2048]{1,0:T(8,128)(2,1)S(1)}, u32[]{:S(2)}) copy-start(bf16[256,2048]{1,0:T(8,128)(2,1)S(1)} %get-tuple-element.79.n_ref) | copy-start | bytes 3145732
  197.9 311.8 %reduce-scatter.4.cloned.1.call-start = ((), (), s32[]{:S(2)}) async-start(), calls=%async_computation.4 | async-start | bytes 9437184 | tf_op jit(solution)/shard_map/reduce_scatter | solution.py:1330
  202.4 23.5 %copy-start.11 = (bf16[1280,512]{1,0:T(8,128)(2,1)}, bf16[1280,512]{1,0:T(8,128)(2,1)S(1)}, u32[]{:S(2)}) copy-start(bf16[1280,512]{1,0:T(8,128)(2,1)S(1)} %get-tuple-element.129.v_ref) | copy-start | bytes 3932164
  202.4 23.5 %copy-start.12 = (bf16[1280,512]{1,0:T(8,128)(2,1)}, bf16[1280,512]{1,0:T(8,128)(2,1)S(1)}, u32[]{:S(2)}) copy-start(bf16[1280,512]{1,0:T(8,128)(2,1)S(1)} %get-tuple-element.130.k_ref) | copy-start | bytes 3932164
  202.5 23.5 %slice-start = ((s8[8388608]{0:T(1024)(128)(4,1)}), s8[4194304]{0:T(1024)(128)(4,1)S(1)}, s32[]{:S(2)}) async-start(s8[8388608]{0:T(1024)(128)(4,1)} %bitcast.51), calls=%async_computation.7 | async-start | bytes 8388608
  202.5 23.5 %slice-start.1 = ((s8[8388608]{0:T(1024)(128)(4,1)}), s8[4194304]{0:T(1024)(128)(4,1)S(1)}, s32[]{:S(2)}) async-start(s8[8388608]{0:T(1024)(128)(4,1)} %bitcast.51), calls=%async_computation.8 | async-start | bytes 8388608
  225.9 4.1 copy-start.7
  225.9 4.1 copy-start.30
  230.0 1.3 copy-start.2
  231.3 1.0 copy-start.27
  416.5 1.2 copy-start.21
  416.6 2.5 copy-start.8
  416.6 336.3 %reduce-scatter.6.cloned.1.call-start = ((), (), s32[]{:S(2)}) async-start(), calls=%async_computation.5 | async-start | bytes 9437184 | tf_op jit(solution)/shard_map/reduce_scatter | solution.py:1337
  419.1 1.6 copy-start.34
  509.6 1.2 copy-start.6
  509.6 1.2 copy-start.25
  509.7 255.6 %reduce-scatter.8.cloned.1.call-start = ((), (), s32[]{:S(2)}) async-start(), calls=%async_computation.6 | async-start | bytes 5242880 | tf_op jit(solution)/shard_map/reduce_scatter | solution.py:1342
  510.9 1.6 copy-start.3
  512.5 1.9 copy-start.9
  514.4 1.3 copy-start.17
  515.7 10.0 %copy-start.14 = (f32[256,128]{1,0:T(8,128)S(1)}, f32[256,128]{1,0:T(8,128)}, u32[]{:S(2)}) copy-start(f32[256,128]{1,0:T(8,128)} %copy-done.13) | copy-start | bytes 393220
  515.7 10.0 %copy-start.16 = (f32[256,128]{1,0:T(8,128)S(1)}, f32[256,128]{1,0:T(8,128)}, u32[]{:S(2)}) copy-start(f32[256,128]{1,0:T(8,128)} %copy-done.15) | copy-start | bytes 393220
  515.7 10.0 %copy-start.31 = (bf16[256,2048]{1,0:T(8,128)(2,1)S(1)}, bf16[256,2048]{1,0:T(8,128)(2,1)}, u32[]{:S(2)}) copy-start(bf16[256,2048]{1,0:T(8,128)(2,1)} %copy-done.30) | copy-start | bytes 3145732
  523.3 1.4 copy-start.10
  524.7 1.0 copy-start.26
  554.9 1.7 copy-start.32
  554.9 2.0 copy-start.33
  557.5 119.5 %copy-start.23 = (f32[2048]{0:T(1024)S(1)}, f32[2048]{0:T(1024)}, u32[]{:S(2)}) copy-start(f32[2048]{0:T(1024)} %copy-done.22) | copy-start | bytes 24580
  676.9 1.2 copy-start.18
  678.2 1.2 copy-start.19
  690.8 0.8 copy-start.28
  757.0 1.5 copy-start.39
  757.0 2.9 copy-start.35
  757.0 3.9 copy-start.38
  758.4 2.5 copy-start.4
Sparse Core Ops, SparseCore 0:
  198.1 118.3 all-gather.1
  416.7 87.1 reduce-scatter.3
  509.8 118.4 reduce-scatter.5
  693.3 71.9 reduce-scatter.7

commit v6 on v4

--- a/solution.py
+++ b/solution.py
@@ -769,7 +769,7 @@
             value += hops[h][j][1][i, slots[h][j].index(r), z].astype(jnp.float32)
         return value
 
-    slack = 3
+    slack = 6
     last = bits + 1 + slack * len(near_first)
 
     def step(t, carry):

time: 777 us -> 777 us (level)
  no operation moved by 1% of the time
where the time goes in v6:
time: 777 us; the launch traced here: 771 us
  Pallas kernels  687 us (88%)
  local copies, waits for them, and re-layouts  30.8 us (4%)
  other arithmetic  22.8 us (3%)
  between operations  14.5 us (2%)
  matrix products  14.4 us (2%)
    pallas_call x2, Pallas kernels, gather_front(): pl.pallas_call(functools.partial(front_kernel, sizes, len(parts), paired)...  174 us
    pallas_call x2, Pallas kernels, reduce_rows(): pl.pallas_call(functools.partial(reduce_kernel, sizes, chunk, products, e...  171 us
    pallas_call x1, Pallas kernels, gather_hidden(): pl.pallas_call(functools.partial(hidden_kernel, sizes, pieces), in_specs=...  121 us
    pallas_call x1, Pallas kernels, reduce_hidden(): pl.pallas_call(functools.partial(hidden_grad_kernel, sizes), in_specs=[vm...  79.9 us
    pallas_call x1, Pallas kernels, hidden_layer(): pl.pallas_call(hidden_layer_kernel, grid=(tokens // tile,), in_specs=[wid...  62.6 us
    pallas_call x1, Pallas kernels, attend_backward(): pl.pallas_call(attend_backward_kernel, grid=(steps,), in_specs=[wide, tal...  29.6 us
    pallas_call x1, Pallas kernels, attend_forward(): pl.pallas_call(attend_forward_kernel, grid=(steps,), in_specs=[pl.BlockSp...  23.3 us
    unnamed x89, local copies, waits for them, and re-layouts  19.9 us
  transfers between devices with their start and end apart: 4, of which 1 were waited for; matrix products, arithmetic and copies ran while one was open for 5% of the time, Pallas kernels for 58%

profile of v6, /device:TPU:0, one launch (start us, length us, event | category | flops | bytes accessed | tf_op | source)
XLA Modules:
  0.0 771.3 jit_solution(644290681157402449)
XLA Ops:
  7.2 0.6 compare_reduce_fusion.1
  7.9 0.6 compare_reduce_fusion
  8.5 1.3 fusion.5
  9.8 0.1 copy.54
  9.9 1.3 fusion.6
  11.3 0.1 copy.55
  11.4 0.1 scatter.9
  11.5 1.5 pad_maximum_fusion.3.refs_0_
  13.1 37.3 %shard_map.203 = bf16[4,2,4,64,1152]{4,3,2,1,0:T(8,128)(2,1)} custom-call(bf16[64,1152]{1,0:T(8,128)(2,1)} %pad_maximum_fusion.3.refs_0_), custom_call_target="tpu_custom_call" | custom-call | flops 89999998976 | bytes 1000000 | tf_op jit(solution)/shard_map/pallas_call | solution.py:558
  50.4 1.9 convert_reduce_fusion
  52.4 0.2 reduce-window.4
  52.8 1.0 copy.67.refs_6_
  53.8 0.5 fusion.4
  54.3 1.5 pad_maximum_fusion.refs_2_
  55.8 0.3 pad_maximum_fusion.4
  56.2 1.4 copy-done
  57.5 1.5 shard_map.204
  59.1 0.8 copy-done.29
  59.8 0.9 broadcast_in_dim.37.refs_5_
  60.8 137.2 %shard_map.205 = (bf16[4,2,4,64,2048]{4,3,2,1,0:T(8,128)(2,1)}, bf16[4,2,4,64,2048]{4,3,2,1,0:T(8,128)(2,1)}, bf16[2,8,4,64,1024]{4,3,2,1,0:T(8,128)(2,1)}, bf16...) custom-call(bf16[64,2048]{1,0:T(8,128)(2,1)} %refs_0_.1, ...), custom_call_target="tpu_custom_call", output_to_operand_aliasing={{5}: (6, {})} | custom-call | flops 89999998976 | bytes 1000000 | tf_op jit(solution)/shard_map/pallas_call | solution.py:558
  198.0 0.2 reduce-scatter.4.cloned.1.call-start
  198.2 0.1 convert_reduce_fusion.2
  198.3 1.9 fusion.2.bias_ref
  200.2 1.9 fusion.9
  202.2 23.3 %shard_map.206 = (bf16[256,2048]{1,0:T(8,128)(2,1)S(1)}, bf16[256,2048]{1,0:T(8,128)(2,1)S(1)}, f32[32,256]{1,0:T(8,128)S(1)}) custom-call(bf16[256,2048]{1,0:T(8,128)(2,1)S(1)} %get-tuple-element.78.n_ref, bf16[2048,2048]{1,0:T(8,128)(2,1)} %bitcast.68, bf16[1280,512]{1,0:T(8,128)(2,1)S(1)} %get-tuple-element.128.k_ref, ...), custom_call_target="tpu_custom_call" | custom-call | flops 40000000000 | bytes 10000000 | tf_op jit(solution)/shard_map/pallas_call | solution.py:124
  225.6 4.0 shard_map.207
  229.6 1.3 copy-done.2
  231.0 1.0 copy-done.27
  231.9 121.3 %shard_map.208 = (bf16[2,8,4,64,1024]{4,3,2,1,0:T(8,128)(2,1)}, bf16[4,2,256,2048]{3,2,1,0:T(8,128)(2,1)}) custom-call(bf16[2,8,4,64,1024]{4,3,2,1,0:T(8,128)(2,1)} %get-tuple-element.86.pair_in, bf16[256,2048]{1,0:T(8,128)(2,1)} %copy-done.27), custom_call_target="tpu_custom_call", output_to_operand_aliasing={{0}: (0, {})} | custom-call | flops 89999998976 | bytes 30000000 | tf_op jit(solution)/shard_map/pallas_call | solution.py:628
  353.3 62.6 %shard_map.209 = (bf16[2048,1024]{1,0:T(8,128)(2,1)}, bf16[2048,1024]{1,0:T(8,128)(2,1)}, bf16[2048,1024]{1,0:T(8,128)(2,1)}, bf16[2048,2048]{1,0:T(8,128)(2,1)}, bf16[2048,2048]{1,0:T(8,128)(2,1)}) custom-call(bf16[2048,2048]{1,0:T(8,128)(2,1)} %bitcast.86, bf16[2048,2048]{1,0:T(8,128)(2,1)} %all-gather.2.cloned.1.call-done.cot, ...), custom_call_target="tpu_custom_call" | custom-call | flops 68719476736 | bytes 30000000 | tf_op jit(solution)/shard_map/pallas_call | solution.py:1235
  416.0 1.1 copy-done.21
  417.1 1.3 copy.57
  418.5 1.3 copy.58
  419.8 2.9 pad_maximum_fusion.1.refs_0_
  422.7 79.9 %shard_map.210 = (bf16[8,2,64,1024]{3,2,1,0:T(8,128)(2,1)}, bf16[2048,2048]{1,0:T(8,128)(2,1)}) custom-call(bf16[2048,2048]{1,0:T(8,128)(2,1)} %bitcast.87, bf16[2048,1024]{1,0:T(8,128)(2,1)} %get-tuple-element.93.gate, bf16[2048,1024]{1,0:T(8,128)(2,1)} %get-tuple-element.94.up, ...), custom_call_target="tpu_custom_call", output_to_operand_aliasing={{1}: (3, {})} | custom-call | flops 60000002048 | bytes 30000000 | tf_op jit(solution)/shard_map/pallas_call | solution.py:988
  502.7 14.4 %convolution_convert_fusion.carried_in = bf16[1024,2048]{1,0:T(8,128)(2,1)} fusion(bf16[2048,1024]{1,0:T(8,128)(2,1)} %get-tuple-element.97, bf16[2048,2048]{1,0:T(8,128)(2,1)} %all-gather.2.cloned.1.call-done.cot), kind=kOutput, calls=%fused_computation.1 | convolution fusion | flops 8592031744 | bytes 16777216 | tf_op jit(solution)/shard_map/dot_general | solution.py:40
  517.2 1.6 copy-done.3
  518.8 1.6 copy-done.9
  520.4 1.3 copy-done.17
  521.6 7.4 shard_map.211
  529.0 1.3 copy-done.10
  530.4 1.0 copy-done.26
  531.3 29.6 %shard_map.212 = (bf16[256,2048]{1,0:T(8,128)(2,1)S(1)}, bf16[1024,512]{1,0:T(8,128)(2,1)S(1)}, bf16[1024,512]{1,0:T(8,128)(2,1)S(1)}, f32[256,512]{1,0:T(8,128)...) custom-call(bf16[256,2048]{1,0:T(8,128)(2,1)S(1)} %copy-done.31, ...), custom_call_target="tpu_custom_call", output_to_operand_aliasing={{5}: (9, {})} | custom-call | flops 80000000000 | bytes 20000000 | tf_op jit(solution)/shard_map/pallas_call | solution.py:223
  561.0 1.7 pad_maximum_fusion.2.refs_1_
  562.8 0.3 copy-done.33
  563.0 0.6 broadcast_in_dim.68.refs_2_
  563.6 110.0 %shard_map.213 = (f32[64,4096]{1,0:T(8,128)}, bf16[4,256,512]{2,1,0:T(8,128)(2,1)}, bf16[4,256,512]{2,1,0:T(8,128)(2,1)}) custom-call(bf16[2,2048,256]{2,1,0:T(8,128)(2,1)} %pad_maximum_fusion.1.refs_0_, bf16[256,4096]{1,0:T(8,128)(2,1)} %pad_maximum_fusion.2.refs_1_, bf16[1,16,128]{2,1,0:T(8,128)(2,1)} %broadcast_in_dim.68.refs_2_, ...), custom_call_target="tpu_custom_call" | custom-call | flops 80000000000 | bytes 30000000 | tf_op jit(solution)/shard_map/pallas_call | solution.py:878
  673.7 1.2 copy-done.18
  674.9 1.2 copy-done.19
  676.1 11.4 %shard_map.214 = (bf16[256,1024]{1,0:T(8,128)(2,1)S(1)}, f32[1,2048]{1,0:T(1,128)S(1)}, bf16[256,2048]{1,0:T(8,128)(2,1)}) custom-call(f32[256,512]{1,0:T(8,128)S(1)} %get-tuple-element.101.dk_own, f32[256,512]{1,0:T(8,128)S(1)} %get-tuple-element.102.dv_own, bf16[4,256,512]{2,1,0:T(8,128)(2,1)S(1)} %copy-done.18, bf16[4,256,512]{2,1,0:T(8,128)(2,1)S(1)} %copy-done.19, ...), custom_call_target="tpu_custom_call" | custom-call | flops 3221225472 | bytes 24000000 | tf_op jit(solution)/shard_map/pallas_call | solution.py:1176
  687.5 0.8 copy-done.28
  688.3 0.3 copy.59
  688.6 1.1 pad_bitcast_fusion.refs_2_
  689.8 61.3 %shard_map.215 = (f32[64,1280]{1,0:T(8,128)}, bf16[8,2,64,1024]{3,2,1,0:T(8,128)(2,1)}) custom-call(bf16[1,2048,256]{2,1,0:T(8,128)(2,1)} %bitcast.72, bf16[256,1024]{1,0:T(8,128)(2,1)} %copy-done.28, bf16[1,2048,256]{2,1,0:T(8,128)(2,1)} %pad_bitcast_fusion.refs_2_, bf16[8,2,64,1024]{3,2,1,0:T(8,128)(2,1)} %get-tuple-element.96.earlier.refs_3_), custom_call_target="tpu_custom_call" | custom-call | flops 80000000000 | bytes 30000000 | tf_op jit(solution)/shard_map/pallas_call | solution.py:878
  751.1 2.0 convert_bitcast_fusion
  753.2 0.6 fusion.8
  753.8 1.5 copy.62
  755.2 1.5 copy.63
  756.7 0.7 slice_reduce_fusion
  757.4 0.7 fusion.11
  758.1 1.0 fusion.10
  759.2 1.3 fusion.3
  760.4 1.4 reduce-scatter.8.cloned.1.call-done
  761.8 2.8 convert_element_type.73
  (95 shorter events, 0.7 us)
Async XLA Ops:
  7.2 346.1 %all-gather.2.cloned.1.call-start = ((), (), s32[]{:S(2)}) async-start(), calls=%async_computation.3 | async-start | bytes 9437184 | tf_op jit(solution)/shard_map/all_gather | solution.py:1307
  13.1 39.3 %copy-start.40 = (s32[1,4]{1,0:T(1,128)S(1)}, s32[1,4]{1,0:T(1,128)}, u32[]{:S(2)}) copy-start(s32[1,4]{1,0:T(1,128)} %param.18) | copy-start | bytes 52
  13.1 39.7 %copy-start.5 = (bf16[1,256,2048]{2,1,0:T(8,128)(2,1)S(1)}, bf16[1,256,2048]{2,1,0:T(8,128)(2,1)}, u32[]{:S(2)}) copy-start(bf16[1,256,2048]{2,1,0:T(8,128)(2,1)} %param.17) | copy-start | bytes 3145732
  50.4 3.9 copy-start.36
  50.4 5.7 copy-start.1
  52.3 3.8 copy-start.22
  52.4 173.2 %copy-start.24 = (f32[2048]{0:T(1024)}, f32[2048]{0:T(1024)S(1)}, u32[]{:S(2)}) copy-start(f32[2048]{0:T(1024)S(1)} %get-tuple-element.121) | copy-start | bytes 24580
  52.6 1.8 copy-start.37
  54.3 3.2 copy-start
  56.1 146.0 %copy-start.13 = (f32[256,128]{1,0:T(8,128)}, f32[256,128]{1,0:T(8,128)S(1)}, u32[]{:S(2)}) copy-start(f32[256,128]{1,0:T(8,128)S(1)} %get-tuple-element.136.cosine.cos_ref) | copy-start | bytes 393220
  56.1 146.0 %copy-start.15 = (f32[256,128]{1,0:T(8,128)}, f32[256,128]{1,0:T(8,128)S(1)}, u32[]{:S(2)}) copy-start(f32[256,128]{1,0:T(8,128)S(1)} %get-tuple-element.137.sine.sin_ref) | copy-start | bytes 393220
  59.0 0.8 copy-start.29
  59.8 142.3 %copy-start.20 = (bf16[256,2048]{1,0:T(8,128)(2,1)}, bf16[256,2048]{1,0:T(8,128)(2,1)S(1)}, u32[]{:S(2)}) copy-start(bf16[256,2048]{1,0:T(8,128)(2,1)S(1)} %get-tuple-element.78.n_ref) | copy-start | bytes 3145732
  198.0 319.2 %reduce-scatter.4.cloned.1.call-start = ((), (), s32[]{:S(2)}) async-start(), calls=%async_computation.4 | async-start | bytes 9437184 | tf_op jit(solution)/shard_map/reduce_scatter | solution.py:1323
  202.1 23.4 %copy-start.11 = (bf16[1280,512]{1,0:T(8,128)(2,1)}, bf16[1280,512]{1,0:T(8,128)(2,1)S(1)}, u32[]{:S(2)}) copy-start(bf16[1280,512]{1,0:T(8,128)(2,1)S(1)} %get-tuple-element.127.v_ref) | copy-start | bytes 3932164
  202.1 23.4 %copy-start.12 = (bf16[1280,512]{1,0:T(8,128)(2,1)}, bf16[1280,512]{1,0:T(8,128)(2,1)S(1)}, u32[]{:S(2)}) copy-start(bf16[1280,512]{1,0:T(8,128)(2,1)S(1)} %get-tuple-element.128.k_ref) | copy-start | bytes 3932164
  202.1 23.4 %slice-start = ((s8[8388608]{0:T(1024)(128)(4,1)}), s8[4194304]{0:T(1024)(128)(4,1)S(1)}, s32[]{:S(2)}) async-start(s8[8388608]{0:T(1024)(128)(4,1)} %bitcast.53), calls=%async_computation.7 | async-start | bytes 8388608
  202.2 23.4 %slice-start.1 = ((s8[8388608]{0:T(1024)(128)(4,1)}), s8[4194304]{0:T(1024)(128)(4,1)S(1)}, s32[]{:S(2)}) async-start(s8[8388608]{0:T(1024)(128)(4,1)} %bitcast.53), calls=%async_computation.8 | async-start | bytes 8388608
  225.5 4.1 copy-start.7
  225.5 4.1 copy-start.30
  229.6 1.3 copy-start.2
  231.0 1.0 copy-start.27
  415.9 1.2 copy-start.21
  415.9 2.5 copy-start.8
  416.0 335.2 %reduce-scatter.6.cloned.1.call-start = ((), (), s32[]{:S(2)}) async-start(), calls=%async_computation.5 | async-start | bytes 9437184 | tf_op jit(solution)/shard_map/reduce_scatter | solution.py:1329
  418.5 1.3 copy-start.34
  502.7 259.1 %reduce-scatter.8.cloned.1.call-start = ((), (), s32[]{:S(2)}) async-start(), calls=%async_computation.6 | async-start | bytes 5242880 | tf_op jit(solution)/shard_map/reduce_scatter | solution.py:1334
  502.7 14.4 %copy-start.6 = (bf16[1,256,2048]{2,1,0:T(8,128)(2,1)S(1)}, bf16[1,256,2048]{2,1,0:T(8,128)(2,1)}, u32[]{:S(2)}) copy-start(bf16[1,256,2048]{2,1,0:T(8,128)(2,1)} %param.17) | copy-start | bytes 3145732
  502.7 14.4 %copy-start.25 = (f32[2048]{0:T(1024)S(1)}, f32[2048]{0:T(1024)}, u32[]{:S(2)}) copy-start(f32[2048]{0:T(1024)} %copy-done.24) | copy-start | bytes 24580
  517.2 1.6 copy-start.3
  518.8 1.6 copy-start.9
  520.4 1.3 copy-start.17
  521.6 9.7 %copy-start.14 = (f32[256,128]{1,0:T(8,128)S(1)}, f32[256,128]{1,0:T(8,128)}, u32[]{:S(2)}) copy-start(f32[256,128]{1,0:T(8,128)} %copy-done.13) | copy-start | bytes 393220
  521.6 9.7 %copy-start.16 = (f32[256,128]{1,0:T(8,128)S(1)}, f32[256,128]{1,0:T(8,128)}, u32[]{:S(2)}) copy-start(f32[256,128]{1,0:T(8,128)} %copy-done.15) | copy-start | bytes 393220
  521.6 9.7 %copy-start.31 = (bf16[256,2048]{1,0:T(8,128)(2,1)S(1)}, bf16[256,2048]{1,0:T(8,128)(2,1)}, u32[]{:S(2)}) copy-start(bf16[256,2048]{1,0:T(8,128)(2,1)} %copy-done.30) | copy-start | bytes 3145732
  529.0 1.3 copy-start.10
  530.4 1.0 copy-start.26
  561.0 1.7 copy-start.32
  561.0 2.0 copy-start.33
  563.6 110.1 %copy-start.23 = (f32[2048]{0:T(1024)S(1)}, f32[2048]{0:T(1024)}, u32[]{:S(2)}) copy-start(f32[2048]{0:T(1024)} %copy-done.22) | copy-start | bytes 24580
  673.7 1.2 copy-start.18
  674.9 1.2 copy-start.19
  687.5 0.8 copy-start.28
  755.2 1.5 copy-start.39
  755.2 2.9 copy-start.35
  755.2 3.9 copy-start.38
  756.7 2.5 copy-start.4
Sparse Core Ops, SparseCore 0:
  198.1 118.7 all-gather.1
  416.1 87.7 reduce-scatter.3
  506.2 109.5 reduce-scatter.5
  689.9 71.8 reduce-scatter.7
